TPU v7x, 32 devices: a whole 2x2x4 slice. The times are simulated.
32 devices in a mesh: batch: 8 (over z, x), mp: 4 (over y, core).
Axes of the slice: x: 2, y: 2, z: 4, core: 2. Of those that a mesh axis runs over, the one named last changes fastest.
Arguments:
- tokens: bfloat16 [8, 256, 2048], P('batch'), may hold values from -6 to 6
- patches: bfloat16 [8, 256, 1664], P('batch'), may hold values from -6 to 6
- lengths: int32 [8], P('batch'), may hold values from 1 to 256, as said below
- patch_keep: int32 [8, 256], P('batch'), may hold values from 0 to 1, as said below
- norm_gains: bfloat16 [3, 2048], P(None, 'batch'), may hold values from 0.5 to 1.5
- self_qkv: bfloat16 [3, 2048, 2048], P(None, 'batch', 'mp'), may hold values from -0.125 to 0.125
- self_out: bfloat16 [2048, 2048], P('mp', 'batch'), may hold values from -0.5 to 0.5
- cross_q: bfloat16 [2048, 2048], P('batch', 'mp'), may hold values from -0.125 to 0.125
- cross_kv: bfloat16 [2, 2048, 2048], P(None, 'batch', 'mp'), may hold values from -0.125 to 0.125
- cross_out: bfloat16 [2048, 2048], P('mp', 'batch'), may hold values from -1 to 1
- patch_proj: bfloat16 [1664, 2048], P('batch', 'mp'), may hold values from -0.15625 to 0.15625
- ffn_in: bfloat16 [2, 2048, 5120], P(None, 'batch', 'mp'), may hold values from -0.125 to 0.125
- ffn_out: bfloat16 [5120, 2048], P('mp', 'batch'), may hold values from -0.125 to 0.125
- cotangent: bfloat16 [8, 256, 2048], P('batch'), may hold values from -6 to 6
Outputs:
- output: bfloat16 [8, 256, 2048], P('batch')
- input_grad: float32 [8, 256, 2048], P('batch')
- gains_grad: float32 [3, 2048], P(None, 'batch')
- self_qkv_grad: float32 [3, 2048, 2048], P(None, 'batch', 'mp')
- self_out_grad: float32 [2048, 2048], P('mp', 'batch')
- cross_q_grad: float32 [2048, 2048], P('batch', 'mp')
- cross_kv_grad: float32 [2, 2048, 2048], P(None, 'batch', 'mp')
- cross_out_grad: float32 [2048, 2048], P('mp', 'batch')
- patch_proj_grad: float32 [1664, 2048], P('batch', 'mp')
- ffn_in_grad: float32 [2, 2048, 5120], P(None, 'batch', 'mp')
- ffn_out_grad: float32 [5120, 2048], P('mp', 'batch')
Inputs may be any that keep to these rules, and one draw needn't show every extreme that they name: `lengths`: slots at or beyond an item's length are padding; some item has length 256. `patch_keep`: 1 marks a patch token that may be attended to; the first patch token of every item is 1.
All inputs are finite; a program needn't handle non-finite values.
Results may differ from a plain program's by a relative error of at most 0.03.
Values may be sent and summed in bfloat16 or wider, within the bound.
A program may use at most 320 MiB of HBM per device.

v0:
```python
import jax
import jax.numpy as jnp
from jax import lax
from jax.sharding import PartitionSpec as P

HD = 64


epsilon = 1e-06


def rms_scale(values, gain):
    return values * lax.rsqrt(jnp.mean(values * values, axis=-1, keepdims=True) + epsilon) * gain


def gated_gelu(gate_up):
    return jax.nn.gelu(gate_up[0], approximate=True) * gate_up[1]


def rounded(values):
    return values.astype(jnp.bfloat16)


def split_heads(values):
    return values.reshape(values.shape[0], values.shape[1], -1, HD)


def merge_heads(values):
    return values.reshape(values.shape[0], values.shape[1], -1)


def masked_scores(queries, key_rows, allowed):
    scores = jnp.einsum(
        "bshe,bkhe->bhsk", queries, key_rows, preferred_element_type=jnp.float32
    ) * HD ** (-0.5)
    return jnp.where(allowed[:, None], scores, -1000000000.0)


def attend(queries, key_rows, value_rows, allowed):
    scores = masked_scores(queries, key_rows, allowed)
    log_total = jax.nn.logsumexp(scores, axis=-1, keepdims=True)
    attn_probs = jnp.exp(scores - log_total)
    mixed = jnp.einsum(
        "bhsk,bkhe->bshe", rounded(attn_probs), value_rows, preferred_element_type=jnp.float32
    )
    return (rounded(merge_heads(mixed)), log_total)


def attend_back(queries, key_rows, value_rows, allowed, log_total, grad_mixed):
    attn_probs = jnp.exp(masked_scores(queries, key_rows, allowed) - log_total)
    grad_probs = jnp.einsum(
        "bshe,bkhe->bhsk", grad_mixed, value_rows, preferred_element_type=jnp.float32
    )
    grad_scores = rounded(
        attn_probs * (grad_probs - jnp.sum(attn_probs * grad_probs, axis=-1, keepdims=True))
    )
    grad_queries = jnp.einsum(
        "bhsk,bkhe->bshe", grad_scores, key_rows, preferred_element_type=jnp.float32
    ) * HD ** (-0.5)
    grad_keys = jnp.einsum(
        "bhsk,bshe->bkhe", grad_scores, queries, preferred_element_type=jnp.float32
    ) * HD ** (-0.5)
    grad_values = jnp.einsum(
        "bhsk,bshe->bkhe", rounded(attn_probs), grad_mixed, preferred_element_type=jnp.float32
    )
    return (merge_heads(grad_queries), merge_heads(grad_keys), merge_heads(grad_values))


def branch_total(partial_value):
    share = lax.psum_scatter(
        partial_value.astype(jnp.bfloat16), "mp", scatter_dimension=1, tiled=True
    ).astype(jnp.float32)
    return lax.all_gather(share.astype(jnp.bfloat16), "mp", axis=1, tiled=True).astype(share.dtype)


def input_total(partial_value):
    share = lax.psum_scatter(
        partial_value.astype(jnp.bfloat16), "mp", scatter_dimension=1, tiled=True
    ).astype(jnp.float32)
    return lax.all_gather(share.astype(jnp.bfloat16), "mp", axis=1, tiled=True).astype(share.dtype)


def norm_back(values, gain, grad_normed):
    pullback = jax.vjp(rms_scale, values, gain)[1]
    return pullback(grad_normed)


def on_device(
    tokens,
    patches,
    lengths,
    patch_keep,
    norm_gains,
    self_qkv,
    self_out,
    cross_q,
    cross_kv,
    cross_out,
    patch_proj,
    ffn_in,
    ffn_out,
    cotangent,
):
    gathered = (
        lax.all_gather(norm_gains, "batch", axis=1, tiled=True),
        lax.all_gather(self_qkv, "batch", axis=1, tiled=True),
        lax.all_gather(self_out, "batch", axis=1, tiled=True),
        lax.all_gather(cross_q, "batch", axis=0, tiled=True),
        lax.all_gather(cross_kv, "batch", axis=1, tiled=True),
        lax.all_gather(cross_out, "batch", axis=1, tiled=True),
        lax.all_gather(patch_proj, "batch", axis=0, tiled=True),
        lax.all_gather(ffn_in, "batch", axis=1, tiled=True),
        lax.all_gather(ffn_out, "batch", axis=1, tiled=True),
    )
    (
        gains_full,
        qkv_full,
        self_out_full,
        cross_q_full,
        cross_kv_full,
        cross_out_full,
        patch_full,
        ffn_in_full,
        ffn_out_full,
    ) = gathered
    gains_full = gains_full.astype(jnp.float32)
    slot_count = tokens.shape[1]
    row_index = lax.broadcasted_iota(jnp.int32, (slot_count, slot_count), 0)
    col_index = lax.broadcasted_iota(jnp.int32, (slot_count, slot_count), 1)
    self_allowed = (col_index <= row_index)[None] & (col_index[None] < lengths[:, None, None])
    cross_allowed = (patch_keep > 0)[:, None, :]
    inputs = tokens.astype(jnp.float32)
    normed_self = rounded(rms_scale(inputs, gains_full[0]))
    projected = rounded(
        jnp.einsum("bsd,cdf->cbsf", normed_self, qkv_full, preferred_element_type=jnp.float32)
    )
    self_queries = split_heads(projected[0])
    self_keys = split_heads(projected[1])
    self_values = split_heads(projected[2])
    mixed_self, total_self = attend(self_queries, self_keys, self_values, self_allowed)
    after_self = inputs + branch_total(
        jnp.einsum("bsk,kd->bsd", mixed_self, self_out_full, preferred_element_type=jnp.float32)
    )
    normed_cross = rounded(rms_scale(after_self, gains_full[1]))
    cross_queries = rounded(
        jnp.einsum("bsd,df->bsf", normed_cross, cross_q_full, preferred_element_type=jnp.float32)
    )
    memory_part = rounded(
        jnp.einsum("bpk,kd->bpd", patches, patch_full, preferred_element_type=jnp.float32)
    )
    memory = lax.all_gather(memory_part, "mp", axis=2, tiled=True)
    key_value = rounded(
        jnp.einsum("bpd,cdf->cbpf", memory, cross_kv_full, preferred_element_type=jnp.float32)
    )
    query_heads = split_heads(cross_queries)
    cross_keys = split_heads(key_value[0])
    cross_values = split_heads(key_value[1])
    mixed_cross, total_cross = attend(query_heads, cross_keys, cross_values, cross_allowed)
    after_cross = after_self + branch_total(
        jnp.einsum("bsk,kd->bsd", mixed_cross, cross_out_full, preferred_element_type=jnp.float32)
    )
    normed_ffn = rounded(rms_scale(after_cross, gains_full[2]))
    gate_up = jnp.einsum(
        "bsd,cdf->cbsf", normed_ffn, ffn_in_full, preferred_element_type=jnp.float32
    )
    hidden = rounded(gated_gelu(gate_up))
    output = after_cross + branch_total(
        jnp.einsum("bsf,fd->bsd", hidden, ffn_out_full, preferred_element_type=jnp.float32)
    )
    regathered = (
        lax.all_gather(norm_gains, "batch", axis=1, tiled=True),
        lax.all_gather(self_qkv, "batch", axis=1, tiled=True),
        lax.all_gather(self_out, "batch", axis=1, tiled=True),
        lax.all_gather(cross_q, "batch", axis=0, tiled=True),
        lax.all_gather(cross_kv, "batch", axis=1, tiled=True),
        lax.all_gather(cross_out, "batch", axis=1, tiled=True),
        lax.all_gather(patch_proj, "batch", axis=0, tiled=True),
        lax.all_gather(ffn_in, "batch", axis=1, tiled=True),
        lax.all_gather(ffn_out, "batch", axis=1, tiled=True),
    )
    (
        gains_full,
        qkv_full,
        self_out_full,
        cross_q_full,
        cross_kv_full,
        cross_out_full,
        patch_full,
        ffn_in_full,
        ffn_out_full,
    ) = regathered
    gains_full = gains_full.astype(jnp.float32)
    grad_output = cotangent.astype(jnp.float32)
    grad_rounded = rounded(grad_output)
    grad_ffn_out = jnp.einsum(
        "bsf,bsd->fd", hidden, grad_rounded, preferred_element_type=jnp.float32
    )
    grad_hidden = jnp.einsum(
        "bsd,fd->bsf", grad_rounded, ffn_out_full, preferred_element_type=jnp.float32
    )
    grad_gate_up = rounded(jax.vjp(gated_gelu, gate_up)[1](grad_hidden)[0])
    grad_ffn_in = jnp.einsum(
        "bsd,cbsf->cdf", normed_ffn, grad_gate_up, preferred_element_type=jnp.float32
    )
    grad_normed = input_total(
        jnp.einsum("cbsf,cdf->bsd", grad_gate_up, ffn_in_full, preferred_element_type=jnp.float32)
    )
    grad_cross_side, grad_gain_ffn = norm_back(after_cross, gains_full[2], grad_normed)
    grad_after_cross = grad_output + grad_cross_side
    grad_rounded = rounded(grad_after_cross)
    grad_cross_out = jnp.einsum(
        "bsk,bsd->kd", mixed_cross, grad_rounded, preferred_element_type=jnp.float32
    )
    grad_mixed = split_heads(
        rounded(
            jnp.einsum(
                "bsd,kd->bsk", grad_rounded, cross_out_full, preferred_element_type=jnp.float32
            )
        )
    )
    grad_queries, grad_keys, grad_values = attend_back(
        query_heads, cross_keys, cross_values, cross_allowed, total_cross, grad_mixed
    )
    grad_queries = rounded(grad_queries)
    grad_key_value = rounded(jnp.stack([grad_keys, grad_values]))
    grad_cross_q = jnp.einsum(
        "bsd,bsf->df", normed_cross, grad_queries, preferred_element_type=jnp.float32
    )
    grad_cross_kv = jnp.einsum(
        "bpd,cbpf->cdf", memory, grad_key_value, preferred_element_type=jnp.float32
    )
    grad_memory = lax.psum_scatter(
        jnp.einsum(
            "cbpf,cdf->bpd", grad_key_value, cross_kv_full, preferred_element_type=jnp.float32
        ).astype(jnp.bfloat16),
        "mp",
        scatter_dimension=2,
        tiled=True,
    ).astype(jnp.float32)
    grad_patch = jnp.einsum(
        "bpk,bpd->kd", patches, rounded(grad_memory), preferred_element_type=jnp.float32
    )
    grad_normed = input_total(
        jnp.einsum("bsf,df->bsd", grad_queries, cross_q_full, preferred_element_type=jnp.float32)
    )
    grad_self_side, grad_gain_cross = norm_back(after_self, gains_full[1], grad_normed)
    grad_after_self = grad_after_cross + grad_self_side
    grad_rounded = rounded(grad_after_self)
    grad_self_out = jnp.einsum(
        "bsk,bsd->kd", mixed_self, grad_rounded, preferred_element_type=jnp.float32
    )
    grad_mixed = split_heads(
        rounded(
            jnp.einsum(
                "bsd,kd->bsk", grad_rounded, self_out_full, preferred_element_type=jnp.float32
            )
        )
    )
    grad_queries, grad_keys, grad_values = attend_back(
        self_queries, self_keys, self_values, self_allowed, total_self, grad_mixed
    )
    grad_projected = rounded(jnp.stack([grad_queries, grad_keys, grad_values]))
    grad_self_qkv = jnp.einsum(
        "bsd,cbsf->cdf", normed_self, grad_projected, preferred_element_type=jnp.float32
    )
    grad_normed = input_total(
        jnp.einsum("cbsf,cdf->bsd", grad_projected, qkv_full, preferred_element_type=jnp.float32)
    )
    grad_input_side, grad_gain_self = norm_back(inputs, gains_full[0], grad_normed)
    grad_input = grad_after_self + grad_input_side
    grad_gains = jnp.stack([grad_gain_self, grad_gain_cross, grad_gain_ffn])
    summed = (
        lax.psum_scatter(grad_gains, "batch", scatter_dimension=1, tiled=True),
        lax.psum_scatter(grad_self_qkv, "batch", scatter_dimension=1, tiled=True),
        lax.psum_scatter(grad_self_out, "batch", scatter_dimension=1, tiled=True),
        lax.psum_scatter(grad_cross_q, "batch", scatter_dimension=0, tiled=True),
        lax.psum_scatter(grad_cross_kv, "batch", scatter_dimension=1, tiled=True),
        lax.psum_scatter(grad_cross_out, "batch", scatter_dimension=1, tiled=True),
        lax.psum_scatter(grad_patch, "batch", scatter_dimension=0, tiled=True),
        lax.psum_scatter(grad_ffn_in, "batch", scatter_dimension=1, tiled=True),
        lax.psum_scatter(grad_ffn_out, "batch", scatter_dimension=1, tiled=True),
    )
    return (
        rounded(output),
        grad_input,
        summed[0],
        summed[1],
        summed[2],
        summed[3],
        summed[4],
        summed[5],
        summed[6],
        summed[7],
        summed[8],
    )


def solution(mesh):
    placed = (
        P("batch", None, None),
        P("batch", None, None),
        P("batch"),
        P("batch", None),
        P(None, "batch"),
        P(None, "batch", "mp"),
        P("mp", "batch"),
        P("batch", "mp"),
        P(None, "batch", "mp"),
        P("mp", "batch"),
        P("batch", "mp"),
        P(None, "batch", "mp"),
        P("mp", "batch"),
        P("batch", None, None),
    )
    return jax.shard_map(
        on_device,
        mesh=mesh,
        in_specs=placed,
        out_specs=(
            P("batch", None, None),
            P("batch", None, None),
            P(None, "batch"),
            P(None, "batch", "mp"),
            P("mp", "batch"),
            P("batch", "mp"),
            P(None, "batch", "mp"),
            P("mp", "batch"),
            P("batch", "mp"),
            P(None, "batch", "mp"),
            P("mp", "batch"),
        ),
        check_vma=False,
    )
```

profile of v0, /device:TPU:0, one launch (start us, length us, event | category | flops | bytes accessed | tf_op | source)
XLA Modules:
  0.0 2315.5 jit_solution(13292706991255117648)
XLA Ops:
  9.5 28.4 %all_gather.56 = bf16[3,2048]{1,0:T(4,128)(2,1)S(1)} all-gather(bf16[3,256]{1,0:T(4,128)(2,1)} %param.18), channel_id=1, replica_groups=mesh['batch'=8,'mp'=4] {'batch'}, dimensions={1}, use_global_device_ids=true | all-gather | bytes 13824 | tf_op jit(solution)/shard_map/all_gather | solution.py:105
  40.1 72.0 %all-gather.17.cloned.1.call-done = bf16[3,2048,512]{2,1,0:T(8,128)(2,1)} async-done(((bf16[3,256,512]{2,1,0:T(8,128)(2,1)}), bf16[3,2048,512]{2,1,0:T(8,128)(2,1)}) %all-gather.17.cloned.1.call-update) | async-done | bytes 6291472 | tf_op jit(solution)/shard_map/all_gather | solution.py:106
  119.6 43.9 %all-gather.19.cloned.1.call-done = bf16[512,2048]{1,0:T(8,128)(2,1)} async-done(((bf16[512,256]{1,0:T(8,128)(2,1)}), bf16[512,2048]{1,0:T(8,128)(2,1)}) %all-gather.19.cloned.1.call-update) | async-done | bytes 2097168 | tf_op jit(solution)/shard_map/all_gather | solution.py:107
  166.9 42.3 %all-gather.23.cloned.1.call-done = bf16[1664,512]{1,0:T(8,128)(2,1)} async-done(((bf16[208,512]{1,0:T(8,128)(2,1)}), bf16[1664,512]{1,0:T(8,128)(2,1)}) %all-gather.23.cloned.1.call-update) | async-done | bytes 1703952 | tf_op jit(solution)/shard_map/all_gather | solution.py:111
  212.6 23.4 %reduce-scatter.21.cloned.1.call-done = bf16[1,64,2048]{2,1,0:T(8,128)(2,1)} async-done(((bf16[1,256,2048]{2,1,0:T(8,128)(2,1)}), bf16[1,64,2048]{2,1,0:T(8,128)(2,1)}) %reduce-scatter.21.cloned.1.call-update) | async-done | bytes 262160 | tf_op jit(solution)/shard_map/reduce_scatter | solution.py:70
  254.8 75.7 %all-gather.25.cloned.1.call-done = bf16[2,2048,512]{2,1,0:T(8,128)(2,1)} async-done(((bf16[2,256,512]{2,1,0:T(8,128)(2,1)}), bf16[2,2048,512]{2,1,0:T(8,128)(2,1)}) %all-gather.25.cloned.1.call-update) | async-done | bytes 4194320 | tf_op jit(solution)/shard_map/all_gather | solution.py:109
  348.9 49.9 %all-gather.27.cloned.1.call-done = bf16[2048,512]{1,0:T(8,128)(2,1)} async-done(((bf16[256,512]{1,0:T(8,128)(2,1)}), bf16[2048,512]{1,0:T(8,128)(2,1)}) %all-gather.27.cloned.1.call-update) | async-done | bytes 2097168 | tf_op jit(solution)/shard_map/all_gather | solution.py:108
  407.8 42.9 %all-gather.29.cloned.1.call-done = bf16[512,2048]{1,0:T(8,128)(2,1)} async-done(((bf16[512,256]{1,0:T(8,128)(2,1)}), bf16[512,2048]{1,0:T(8,128)(2,1)}) %all-gather.29.cloned.1.call-update) | async-done | bytes 2097168 | tf_op jit(solution)/shard_map/all_gather | solution.py:110
  454.1 23.2 %reduce-scatter.23.cloned.1.call-done = bf16[1,64,2048]{2,1,0:T(8,128)(2,1)} async-done(((bf16[1,256,2048]{2,1,0:T(8,128)(2,1)}), bf16[1,64,2048]{2,1,0:T(8,128)(2,1)}) %reduce-scatter.23.cloned.1.call-update) | async-done | bytes 262160 | tf_op jit(solution)/shard_map/reduce_scatter | solution.py:70
  498.7 149.9 %all-gather.33.cloned.1.call-done = bf16[2,2048,1280]{2,1,0:T(8,128)(2,1)} async-done(((bf16[2,256,1280]{2,1,0:T(8,128)(2,1)}), bf16[2,2048,1280]{2,1,0:T(8,128)(2,1)}) %all-gather.33.cloned.1.call-update) | async-done | bytes 10485776 | tf_op jit(solution)/shard_map/all_gather | solution.py:112
  657.6 78.4 %all-gather.35.cloned.1.call-done = bf16[1280,2048]{1,0:T(8,128)(2,1)} async-done(((bf16[1280,256]{1,0:T(8,128)(2,1)}), bf16[1280,2048]{1,0:T(8,128)(2,1)}) %all-gather.35.cloned.1.call-update) | async-done | bytes 5242896 | tf_op jit(solution)/shard_map/all_gather | solution.py:113
  770.8 27.9 %reduce-scatter.25.cloned.1.call-done = bf16[1,64,2048]{2,1,0:T(8,128)(2,1)} async-done(((bf16[1,256,2048]{2,1,0:T(8,128)(2,1)}), bf16[1,64,2048]{2,1,0:T(8,128)(2,1)}) %reduce-scatter.25.cloned.1.call-update) | async-done | bytes 262160 | tf_op jit(solution)/shard_map/reduce_scatter | solution.py:70
  850.9 25.0 %reduce-scatter.29.cloned.1.call-done = bf16[1,64,2048]{2,1,0:T(8,128)(2,1)} async-done(((bf16[1,256,2048]{2,1,0:T(8,128)(2,1)}), bf16[1,64,2048]{2,1,0:T(8,128)(2,1)}) %reduce-scatter.29.cloned.1.call-update) | async-done | bytes 262160 | tf_op jit(solution)/shard_map/reduce_scatter | solution.py:77
  876.0 18.3 all-gather.41.cloned.1.call-done
  918.3 25.0 %reduce-scatter.31.cloned.1.call-done = bf16[1,64,2048]{2,1,0:T(8,128)(2,1)} async-done(((bf16[1,256,2048]{2,1,0:T(8,128)(2,1)}), bf16[1,64,2048]{2,1,0:T(8,128)(2,1)}) %reduce-scatter.31.cloned.1.call-update) | async-done | bytes 262160 | tf_op jit(solution)/shard_map/reduce_scatter | solution.py:77
  1029.5 27.4 %reduce-scatter.49.cloned.1.call-done = f32[256,3]{1,0:T(8,128)} async-done(((f32[2048,3]{1,0:T(8,128)}), f32[256,3]{1,0:T(8,128)}) %reduce-scatter.49.cloned.1.call-update) | async-done | bytes 3088
  1058.4 150.4 %reduce-scatter.39.cloned.1.call-done = f32[2,256,512]{1,2,0:T(8,128)} async-done(((f32[2,2048,512]{1,2,0:T(8,128)}), f32[2,256,512]{1,2,0:T(8,128)}) %reduce-scatter.39.cloned.1.call-update) | async-done | bytes 1048592 | tf_op jit(solution)/shard_map/reduce_scatter | solution.py:277
  1211.3 208.3 %reduce-scatter.33.cloned.1.call-done = f32[3,256,512]{1,2,0:T(8,128)} async-done(((f32[3,2048,512]{1,2,0:T(8,128)}), f32[3,256,512]{1,2,0:T(8,128)}) %reduce-scatter.33.cloned.1.call-update) | async-done | bytes 1572880 | tf_op jit(solution)/shard_map/reduce_scatter | solution.py:274
  1422.7 345.2 %reduce-scatter.45.cloned.1.call-done = f32[2,256,1280]{1,2,0:T(8,128)} async-done(((f32[2,2048,1280]{1,2,0:T(8,128)}), f32[2,256,1280]{1,2,0:T(8,128)}) %reduce-scatter.45.cloned.1.call-update) | async-done | bytes 2621456 | tf_op jit(solution)/shard_map/reduce_scatter | solution.py:280
  1771.1 88.4 %reduce-scatter.37.cloned.1.call-done = f32[256,512]{1,0:T(8,128)} async-done(((f32[2048,512]{1,0:T(8,128)}), f32[256,512]{1,0:T(8,128)}) %reduce-scatter.37.cloned.1.call-update) | async-done | bytes 524304 | tf_op jit(solution)/shard_map/reduce_scatter | solution.py:276
  1859.5 92.5 %reduce-scatter.41.cloned.1.call-done = f32[512,256]{1,0:T(8,128)} async-done(((f32[512,2048]{1,0:T(8,128)}), f32[512,256]{1,0:T(8,128)}) %reduce-scatter.41.cloned.1.call-update) | async-done | bytes 524304 | tf_op jit(solution)/shard_map/reduce_scatter | solution.py:278
  1951.9 81.9 %reduce-scatter.51.cloned.1.call-done = f32[208,512]{1,0:T(8,128)} async-done(((f32[1664,512]{1,0:T(8,128)}), f32[208,512]{1,0:T(8,128)}) %reduce-scatter.51.cloned.1.call-update) | async-done | bytes 426000
  2033.8 91.9 %reduce-scatter.35.cloned.1.call-done = f32[512,256]{1,0:T(8,128)} async-done(((f32[512,2048]{1,0:T(8,128)}), f32[512,256]{1,0:T(8,128)}) %reduce-scatter.35.cloned.1.call-update) | async-done | bytes 524304 | tf_op jit(solution)/shard_map/reduce_scatter | solution.py:275
  2125.7 182.7 %reduce-scatter.47.cloned.1.call-done = f32[1280,256]{1,0:T(8,128)} async-done(((f32[1280,2048]{1,0:T(8,128)}), f32[1280,256]{1,0:T(8,128)}) %reduce-scatter.47.cloned.1.call-update) | async-done | bytes 1310736 | tf_op jit(solution)/shard_map/reduce_scatter | solution.py:281
  (251 shorter events, 304.7 us)
Async XLA Ops:
  7.2 104.9 %all-gather.17.cloned.1.call-start = ((), (), s32[]{:S(2)}) async-start(), calls=%async_computation.16 | async-start | bytes 7077888 | tf_op jit(solution)/shard_map/all_gather | solution.py:106
  7.9 155.5 %all-gather.19.cloned.1.call-start = ((), (), s32[]{:S(2)}) async-start(), calls=%async_computation.17 | async-start | bytes 2359296 | tf_op jit(solution)/shard_map/all_gather | solution.py:107
  8.7 200.5 %all-gather.23.cloned.1.call-start = ((), (), s32[]{:S(2)}) async-start(), calls=%async_computation.20 | async-start | bytes 1916928 | tf_op jit(solution)/shard_map/all_gather | solution.py:111
  9.4 226.6 %reduce-scatter.21.cloned.1.call-start = ((), (), s32[]{:S(2)}) async-start(), calls=%async_computation.18 | async-start | bytes 1310720 | tf_op jit(solution)/shard_map/reduce_scatter | solution.py:70
  166.8 88.0 %all-gather.45.cloned.1.call-start = ((), (), s32[]{:S(2)}) async-start(), calls=%async_computation.44 | async-start | bytes 1310720 | tf_op jit(solution)/shard_map/all_gather | solution.py:151
  212.0 118.5 %all-gather.25.cloned.1.call-start = ((), (), s32[]{:S(2)}) async-start(), calls=%async_computation.21 | async-start | bytes 4718592 | tf_op jit(solution)/shard_map/all_gather | solution.py:109
  212.5 134.6 %all-gather.21.cloned.1.call-start = ((), (), s32[]{:S(2)}) async-start(), calls=%async_computation.19 | async-start | bytes 1310720 | tf_op jit(solution)/shard_map/all_gather | solution.py:73
  236.0 162.8 %all-gather.27.cloned.1.call-start = ((), (), s32[]{:S(2)}) async-start(), calls=%async_computation.22 | async-start | bytes 2359296 | tf_op jit(solution)/shard_map/all_gather | solution.py:108
  236.8 213.9 %all-gather.29.cloned.1.call-start = ((), (), s32[]{:S(2)}) async-start(), calls=%async_computation.23 | async-start | bytes 2359296 | tf_op jit(solution)/shard_map/all_gather | solution.py:110
  237.5 239.8 %reduce-scatter.23.cloned.1.call-start = ((), (), s32[]{:S(2)}) async-start(), calls=%async_computation.24 | async-start | bytes 1310720 | tf_op jit(solution)/shard_map/reduce_scatter | solution.py:70
  477.4 171.2 %all-gather.33.cloned.1.call-start = ((), (), s32[]{:S(2)}) async-start(), calls=%async_computation.26 | async-start | bytes 11796480 | tf_op jit(solution)/shard_map/all_gather | solution.py:112
  477.9 258.1 %all-gather.35.cloned.1.call-start = ((), (), s32[]{:S(2)}) async-start(), calls=%async_computation.27 | async-start | bytes 5898240 | tf_op jit(solution)/shard_map/all_gather | solution.py:113
  478.7 292.0 %reduce-scatter.27.cloned.1.call-start = ((), (), s32[]{:S(2)}) async-start(), calls=%async_computation.30 | async-start | bytes 1310720 | tf_op jit(solution)/shard_map/reduce_scatter | solution.py:77
  798.7 77.2 %reduce-scatter.29.cloned.1.call-start = ((), (), s32[]{:S(2)}) async-start(), calls=%async_computation.32 | async-start | bytes 1310720 | tf_op jit(solution)/shard_map/reduce_scatter | solution.py:77
  875.9 67.4 %reduce-scatter.31.cloned.1.call-start = ((), (), s32[]{:S(2)}) async-start(), calls=%async_computation.34 | async-start | bytes 1310720 | tf_op jit(solution)/shard_map/reduce_scatter | solution.py:77
  949.9 106.9 %reduce-scatter.49.cloned.1.call-start = ((), (), s32[]{:S(2)}) async-start(), calls=%async_computation.45 | async-start | bytes 1179648
  965.8 243.0 %reduce-scatter.39.cloned.1.call-start = ((), (), s32[]{:S(2)}) async-start(), calls=%async_computation.39 | async-start | bytes 9437184 | tf_op jit(solution)/shard_map/reduce_scatter | solution.py:277
  971.8 447.9 %reduce-scatter.33.cloned.1.call-start = ((), (), s32[]{:S(2)}) async-start(), calls=%async_computation.36 | async-start | bytes 14155776 | tf_op jit(solution)/shard_map/reduce_scatter | solution.py:274
  980.3 787.6 %reduce-scatter.45.cloned.1.call-start = ((), (), s32[]{:S(2)}) async-start(), calls=%async_computation.42 | async-start | bytes 23592960 | tf_op jit(solution)/shard_map/reduce_scatter | solution.py:280
  993.3 866.1 %reduce-scatter.37.cloned.1.call-start = ((), (), s32[]{:S(2)}) async-start(), calls=%async_computation.38 | async-start | bytes 4718592 | tf_op jit(solution)/shard_map/reduce_scatter | solution.py:276
  997.1 954.8 %reduce-scatter.41.cloned.1.call-start = ((), (), s32[]{:S(2)}) async-start(), calls=%async_computation.40 | async-start | bytes 4718592 | tf_op jit(solution)/shard_map/reduce_scatter | solution.py:278
  1002.4 1031.4 %reduce-scatter.51.cloned.1.call-start = ((), (), s32[]{:S(2)}) async-start(), calls=%async_computation.46 | async-start | bytes 3833856
  1010.7 1115.0 %reduce-scatter.35.cloned.1.call-start = ((), (), s32[]{:S(2)}) async-start(), calls=%async_computation.37 | async-start | bytes 4718592 | tf_op jit(solution)/shard_map/reduce_scatter | solution.py:275
  1016.0 1292.4 %reduce-scatter.47.cloned.1.call-start = ((), (), s32[]{:S(2)}) async-start(), calls=%async_computation.43 | async-start | bytes 11796480 | tf_op jit(solution)/shard_map/reduce_scatter | solution.py:281
  (57 other events, 2884.1 us)
Sparse Core Ops, SparseCore 0:
  10.2 101.8 all-gather.16
  114.2 49.2 all-gather.18
  165.7 43.4 all-gather.22
  212.1 23.8 reduce-scatter.20
  257.1 73.3 all-gather.24
  349.5 49.2 all-gather.26
  401.1 49.5 all-gather.28
  454.2 23.0 reduce-scatter.22
  497.7 150.8 all-gather.32
  650.6 85.3 all-gather.34
  747.6 23.0 reduce-scatter.26
  773.8 24.8 reduce-scatter.24
  851.0 24.8 reduce-scatter.28
  918.3 24.8 reduce-scatter.30
  964.1 24.9 reduce-scatter.42
  993.5 63.3 reduce-scatter.48
  1060.3 148.4 reduce-scatter.38
  1212.8 206.7 reduce-scatter.32
  1423.9 343.8 reduce-scatter.44
  1772.3 87.0 reduce-scatter.36
  1863.7 88.2 reduce-scatter.40
  1956.5 77.1 reduce-scatter.50
  2037.8 87.8 reduce-scatter.34
  2130.3 178.0 reduce-scatter.46
  (7 shorter events, 114.9 us)
where the time goes:
time: 2320 us
  waiting for transfers between devices  2080 us (90%)
  matrix products  123 us (5%)
  local copies, waits for them, and re-layouts  41.3 us (2%)
  blocking collectives  28.4 us (1%)
  other arithmetic  25 us (1%)
    reduce_scatter x1, waiting for transfers between devices, on_device(): lax.psum_scatter(grad_ffn_in, 'batch', scatter_dimension=1, tiled=True)  345 us
    reduce_scatter x1, waiting for transfers between devices, on_device(): lax.psum_scatter(grad_self_qkv, 'batch', scatter_dimension=1, tiled=True)  208 us
    reduce_scatter x1, waiting for transfers between devices, on_device(): lax.psum_scatter(grad_ffn_out, 'batch', scatter_dimension=1, tiled=True)  183 us
    reduce_scatter x1, waiting for transfers between devices, on_device(): lax.psum_scatter(grad_cross_kv, 'batch', scatter_dimension=1, tiled=True)  150 us
    all_gather x1, waiting for transfers between devices, on_device(): lax.all_gather(ffn_in, 'batch', axis=1, tiled=True)  150 us
    unnamed x33, waiting for transfers between devices  115 us
    reduce_scatter x1, waiting for transfers between devices, on_device(): lax.psum_scatter(grad_cross_out, 'batch', scatter_dimension=1, tiled=True)  92.5 us
    reduce_scatter x1, waiting for transfers between devices, on_device(): lax.psum_scatter(grad_self_out, 'batch', scatter_dimension=1, tiled=True)  91.9 us
  transfers between devices with their start and end apart: 31, of which 30 were waited for; matrix products, arithmetic and copies ran while one was open for 5% of the time, Pallas kernels for 0%

commit v1 on v0

v1 whole, which is shorter than its diff:
```python
import functools

import jax
import jax.numpy as jnp
from jax import lax
from jax.experimental import pallas as pl
from jax.experimental.pallas import tpu as pltpu
from jax.sharding import Mesh
from jax.sharding import PartitionSpec as P

HD = 64
EPS = 1e-06
RELATIVE = ((1, 1), (1, 0), (0, 1), (0, 0))
VMEM_LIMIT = 48 * 2**20


def rounded(values):
    return values.astype(jnp.bfloat16)


def flip(value, by):
    return value + by * (1 - 2 * value)


class Plane:
    def __init__(self):
        self.x = lax.axis_index("x")
        part = lax.axis_index("mp")
        self.y = part // 2
        self.c = part % 2

    def device(self, dx, dy, dc):
        return {"x": flip(self.x, dx), "mp": flip(self.y, dy) * 2 + flip(self.c, dc)}

    def block(self, dx, dy, dc):
        return (flip(self.x, dx) * 2 + flip(self.y, dy)) * 2 + flip(self.c, dc)

    def greet(self, relations):
        barrier = pltpu.get_barrier_semaphore()
        for relation in relations:
            pl.semaphore_signal(
                barrier, inc=1, device_id=self.device(*relation), device_id_type=pl.DeviceIdType.MESH
            )
        pl.semaphore_wait(barrier, len(relations))

    def send(self, src, dst, sems, slot, relation):
        copy = pltpu.make_async_remote_copy(
            src_ref=src,
            dst_ref=dst,
            send_sem=sems.at[0, slot],
            recv_sem=sems.at[1, slot],
            device_id=self.device(*relation),
            device_id_type=pl.DeviceIdType.MESH,
        )
        copy.start()
        return copy


ALL_RELATIONS = ((0, 0, 1), (1, 1, 0), (1, 0, 0), (0, 1, 0))
ROW_RELATIONS = ((0, 0, 1), (0, 1, 0))


def reduce_blocks(plane, part, from_core, to_chip, from_chip, sems):
    pair = [
        plane.send(part.at[plane.block(dx, dy, 1)], from_core.at[i], sems, i, (0, 0, 1))
        for i, (dx, dy) in enumerate(RELATIVE)
    ]
    across = []
    for i, (dx, dy) in enumerate(RELATIVE):
        pair[i].wait_recv()
        both = part[plane.block(dx, dy, 0)].astype(jnp.float32) + from_core[i].astype(jnp.float32)
        if i < 3:
            to_chip[i] = rounded(both)
            across.append(plane.send(to_chip.at[i], from_chip.at[i], sems, 4 + i, (dx, dy, 0)))
    for i in (2, 1, 0):
        across[i].wait_recv()
        both = both + from_chip[i].astype(jnp.float32)
    for copy in pair + across:
        copy.wait_send()
    return both


def gather_blocks(plane, out, sems, first):
    mine = plane.block(0, 0, 0)
    sends = [
        plane.send(out.at[mine], out.at[mine], sems, first + i, (dx, dy, 0))
        for i, (dx, dy) in enumerate(RELATIVE[:3])
    ]
    sends.append(plane.send(out.at[mine], out.at[mine], sems, first + 3, (0, 0, 1)))
    for i in (2, 1, 0):
        dx, dy = RELATIVE[i]
        theirs = plane.block(dx, dy, 0)
        sends[i].wait_recv()
        sends.append(plane.send(out.at[theirs], out.at[theirs], sems, first + 4 + i, (0, 0, 1)))
    for copy in sends[3:]:
        copy.wait_recv()
    for copy in sends:
        copy.wait_send()


def gather_rows(plane, out, sems, first):
    mine = plane.y * 2 + plane.c
    theirs = flip(plane.y, 1) * 2 + plane.c
    over = plane.send(out.at[mine], out.at[mine], sems, first, (0, 1, 0))
    beside = plane.send(out.at[mine], out.at[mine], sems, first + 1, (0, 0, 1))
    over.wait_recv()
    onward = plane.send(out.at[theirs], out.at[theirs], sems, first + 2, (0, 0, 1))
    beside.wait_recv()
    onward.wait_recv()
    for copy in (over, beside, onward):
        copy.wait_send()


def forward_kernel(part, residual, gain, after, normed, from_core, to_chip, from_chip, sems):
    plane = Plane()
    plane.greet(ALL_RELATIONS)
    values = residual[...] + reduce_blocks(plane, part, from_core, to_chip, from_chip, sems)
    after[...] = values
    scale = lax.rsqrt(jnp.mean(values * values, axis=-1, keepdims=True) + EPS)
    normed[plane.block(0, 0, 0)] = rounded(values * scale * gain[...])
    gather_blocks(plane, normed, sems, 7)


def back_values(values, gain, grad):
    scale = lax.rsqrt(jnp.mean(values * values, axis=-1, keepdims=True) + EPS)
    gain_part = jnp.sum(grad * values * scale, axis=0, keepdims=True)
    scaled = grad * gain
    side = scale * scaled - values * (scale * scale * scale) * jnp.mean(
        scaled * values, axis=-1, keepdims=True
    )
    return side, gain_part


def backward_kernel(
    part, values, grad, gain, grad_out, gain_part, grad_all, from_core, to_chip, from_chip, sems
):
    plane = Plane()
    plane.greet(ALL_RELATIONS)
    total = reduce_blocks(plane, part, from_core, to_chip, from_chip, sems)
    side, gain_sum = back_values(values[...], gain[...], total)
    gain_part[...] = gain_sum
    result = grad[...] + side
    grad_out[...] = result
    grad_all[plane.block(0, 0, 0)] = rounded(result)
    gather_blocks(plane, grad_all, sems, 7)


def output_kernel(part, residual, out, from_core, to_chip, from_chip, sems):
    plane = Plane()
    plane.greet(ALL_RELATIONS)
    values = residual[...] + reduce_blocks(plane, part, from_core, to_chip, from_chip, sems)
    out[plane.y * 2 + plane.c] = rounded(values)
    gather_rows(plane, out, sems, 7)


def input_kernel(part, values, grad, gain, out, gain_part, from_core, to_chip, from_chip, sems):
    plane = Plane()
    plane.greet(ALL_RELATIONS)
    total = reduce_blocks(plane, part, from_core, to_chip, from_chip, sems)
    side, gain_sum = back_values(values[...], gain[...], total)
    gain_part[...] = gain_sum
    out[plane.y * 2 + plane.c] = grad[...] + side
    gather_rows(plane, out, sems, 7)


def gather_kernel(own, out, sems):
    plane = Plane()
    plane.greet(ALL_RELATIONS)
    out[plane.block(0, 0, 0)] = own[...]
    gather_blocks(plane, out, sems, 0)


def scatter_kernel(part, out, from_core, to_chip, from_chip, sems):
    plane = Plane()
    plane.greet(ALL_RELATIONS)
    out[...] = rounded(reduce_blocks(plane, part, from_core, to_chip, from_chip, sems))


def plane_call(kernel, name, number, outs, rows, columns, copies, reduces, operands):
    whole = pl.BlockSpec(memory_space=pltpu.VMEM)
    scratch = []
    if reduces:
        scratch = [
            pltpu.VMEM((4, rows, columns), jnp.bfloat16),
            pltpu.VMEM((3, rows, columns), jnp.bfloat16),
            pltpu.VMEM((3, rows, columns), jnp.bfloat16),
        ]
    scratch.append(pltpu.SemaphoreType.DMA((2, copies)))
    return pl.pallas_call(
        kernel,
        name=name,
        out_shape=outs,
        in_specs=[whole] * len(operands),
        out_specs=jax.tree.map(lambda _: whole, outs),
        scratch_shapes=scratch,
        compiler_params=pltpu.CompilerParams(
            collective_id=number, has_side_effects=True, vmem_limit_bytes=VMEM_LIMIT
        ),
    )(*operands)


def full(shape, dtype=jnp.float32):
    return jax.ShapeDtypeStruct(shape, dtype)


def forward_step(part, residual, gain):
    rows, columns = residual.shape
    return plane_call(
        forward_kernel, "forward_step", 0,
        (full((rows, columns)), full((8, rows, columns), jnp.bfloat16)),
        rows, columns, 14, True, (part, residual, gain),
    )


def backward_step(part, values, grad, gain):
    rows, columns = values.shape
    return plane_call(
        backward_kernel, "backward_step", 1,
        (full((rows, columns)), full((1, columns)), full((8, rows, columns), jnp.bfloat16)),
        rows, columns, 14, True, (part, values, grad, gain),
    )


def output_step(part, residual):
    rows, columns = residual.shape
    return plane_call(
        output_kernel, "output_step", 2, full((4, rows, columns), jnp.bfloat16),
        rows, columns, 10, True, (part, residual),
    )


def input_step(part, values, grad, gain):
    rows, columns = values.shape
    return plane_call(
        input_kernel, "input_step", 3, (full((4, rows, columns)), full((1, columns))),
        rows, columns, 10, True, (part, values, grad, gain),
    )


def gather_step(own):
    rows, columns = own.shape
    return plane_call(
        gather_kernel, "gather_step", 4, full((8, rows, columns), own.dtype),
        rows, columns, 7, False, (own,),
    )


def scatter_step(part):
    _, rows, columns = part.shape
    return plane_call(
        scatter_kernel, "scatter_step", 5, full((rows, columns), part.dtype),
        rows, columns, 7, True, (part,),
    )


def split_heads(values):
    return values.reshape(2, values.shape[0] // 2, -1, HD)


def merge_heads(values):
    return values.reshape(2 * values.shape[1], -1)


def masked_scores(queries, key_rows, allowed):
    scores = jnp.einsum(
        "bshe,bkhe->bhsk", queries, key_rows, preferred_element_type=jnp.float32
    ) * HD ** (-0.5)
    return jnp.where(allowed[:, None], scores, -1000000000.0)


def attend(queries, key_rows, value_rows, allowed):
    scores = masked_scores(queries, key_rows, allowed)
    log_total = jax.nn.logsumexp(scores, axis=-1, keepdims=True)
    attn_probs = jnp.exp(scores - log_total)
    mixed = jnp.einsum(
        "bhsk,bkhe->bshe", rounded(attn_probs), value_rows, preferred_element_type=jnp.float32
    )
    return (rounded(merge_heads(mixed)), log_total)


def attend_back(queries, key_rows, value_rows, allowed, log_total, grad_mixed):
    attn_probs = jnp.exp(masked_scores(queries, key_rows, allowed) - log_total)
    grad_probs = jnp.einsum(
        "bshe,bkhe->bhsk", grad_mixed, value_rows, preferred_element_type=jnp.float32
    )
    grad_scores = rounded(
        attn_probs * (grad_probs - jnp.sum(attn_probs * grad_probs, axis=-1, keepdims=True))
    )
    grad_queries = jnp.einsum(
        "bhsk,bkhe->bshe", grad_scores, key_rows, preferred_element_type=jnp.float32
    ) * HD ** (-0.5)
    grad_keys = jnp.einsum(
        "bhsk,bshe->bkhe", grad_scores, queries, preferred_element_type=jnp.float32
    ) * HD ** (-0.5)
    grad_values = jnp.einsum(
        "bhsk,bshe->bkhe", rounded(attn_probs), grad_mixed, preferred_element_type=jnp.float32
    )
    return tuple(rounded(merge_heads(g)) for g in (grad_queries, grad_keys, grad_values))


def gated_gelu(gate_up):
    return jax.nn.gelu(gate_up[0], approximate=True) * gate_up[1]


def dot(pattern, left, right):
    return jnp.einsum(pattern, left, right, preferred_element_type=jnp.float32)


SWAP = ((0, 1), (1, 0))


def halves(values, axis, x):
    size = values.shape[axis] // 2
    keep = lax.dynamic_slice_in_dim(values, x * size, size, axis)
    give = lax.dynamic_slice_in_dim(values, (1 - x) * size, size, axis)
    return keep, give


def in_order(own, other, axis, x):
    return jnp.where(
        x == 0,
        jnp.concatenate([own, other], axis),
        jnp.concatenate([other, own], axis),
    )


def exchange(values, cut, join, x):
    keep, give = halves(values, cut, x)
    return in_order(keep, lax.ppermute(give, "x", SWAP), join, x)


def both_items(values, x):
    return in_order(values, lax.ppermute(values, "x", SWAP), 0, x)


def gather_in(weight, x):
    swapped = exchange(weight, weight.ndim - 1, weight.ndim - 2, x)
    return lax.all_gather(swapped, "z", axis=weight.ndim - 2, tiled=True)


def gather_out(weight, x):
    return lax.all_gather(exchange(weight, 0, 1, x), "z", axis=0, tiled=False)


def scatter_in(grad, x):
    share = lax.psum_scatter(rounded(grad), "z", scatter_dimension=grad.ndim - 2, tiled=True)
    return exchange(share, grad.ndim - 2, grad.ndim - 1, x).astype(jnp.float32)


def scatter_out(grad, x):
    share = lax.psum_scatter(rounded(grad), "z", scatter_dimension=0, tiled=False)
    return exchange(share, 1, 0, x).astype(jnp.float32)


def on_device(
    tokens,
    patches,
    lengths,
    patch_keep,
    norm_gains,
    self_qkv,
    self_out,
    cross_q,
    cross_kv,
    cross_out,
    patch_proj,
    ffn_in,
    ffn_out,
    cotangent,
):
    x = lax.axis_index("x")
    m = lax.axis_index("mp")
    slots, width = tokens.shape[1], tokens.shape[2]
    rows = slots // 4
    gains = lax.all_gather(norm_gains, ("z", "x"), axis=1, tiled=True).astype(jnp.float32)
    gain_of = [gains[i : i + 1] for i in range(3)]
    facts = jnp.concatenate([patch_keep, lengths[:, None]], axis=1)
    facts = lax.all_gather(facts, "x", axis=0, tiled=True)
    patch_keep, lengths = facts[:, :-1], facts[:, -1]

    patch_w = gather_in(patch_proj, x)
    qkv_w = gather_in(self_qkv, x)
    self_out_w = gather_out(self_out, x)
    cross_kv_w = gather_in(cross_kv, x)
    cross_q_w = gather_in(cross_q, x)
    cross_out_w = gather_out(cross_out, x)
    ffn_in_w = gather_in(ffn_in, x)
    ffn_out_w = gather_out(ffn_out, x)

    row_index = lax.broadcasted_iota(jnp.int32, (slots, slots), 0)
    col_index = lax.broadcasted_iota(jnp.int32, (slots, slots), 1)
    self_allowed = (col_index <= row_index)[None] & (col_index[None] < lengths[:, None, None])
    cross_allowed = (patch_keep > 0)[:, None, :]

    token_all = both_items(tokens[0], x)
    patch_all = both_items(patches[0], x)
    grad_all = both_items(cotangent[0], x)
    own_tokens = lax.dynamic_slice_in_dim(tokens[0], m * rows, rows, 0).astype(jnp.float32)
    own_grad = lax.dynamic_slice_in_dim(cotangent[0], m * rows, rows, 0).astype(jnp.float32)

    values = token_all.astype(jnp.float32)
    normed_self = rounded(
        values
        * lax.rsqrt(jnp.mean(values * values, axis=-1, keepdims=True) + EPS)
        * gain_of[0]
    )

    def to_blocks(partial_value):
        return rounded(partial_value).reshape(8, rows, width)

    def from_blocks(blocks):
        return blocks.reshape(8 * rows, width)

    memory_part = rounded(dot("pk,kd->pd", patch_all, patch_w))
    memory_blocks = gather_step(memory_part)
    memory = (
        memory_blocks.reshape(2, 4, memory_part.shape[0], -1)
        .transpose(2, 1, 0, 3)
        .reshape(memory_part.shape[0], -1)
    )

    projected = rounded(dot("sd,cdf->csf", normed_self, qkv_w))
    self_parts = [split_heads(projected[i]) for i in range(3)]
    mixed_self, total_self = attend(*self_parts, self_allowed)
    part = dot("sk,zkd->szd", mixed_self, self_out_w)
    after_self, normed_cross = forward_step(to_blocks(part), own_tokens, gain_of[1])
    normed_cross = from_blocks(normed_cross)

    key_value = rounded(dot("pd,cdf->cpf", memory, cross_kv_w))
    query_heads = split_heads(rounded(dot("sd,df->sf", normed_cross, cross_q_w)))
    cross_keys = split_heads(key_value[0])
    cross_values = split_heads(key_value[1])
    mixed_cross, total_cross = attend(query_heads, cross_keys, cross_values, cross_allowed)
    part = dot("sk,zkd->szd", mixed_cross, cross_out_w)
    after_cross, normed_ffn = forward_step(to_blocks(part), after_self, gain_of[2])
    normed_ffn = from_blocks(normed_ffn)

    gate_up = dot("sd,cdf->csf", normed_ffn, ffn_in_w)
    hidden = rounded(gated_gelu(gate_up))
    part = dot("sf,zfd->szd", hidden, ffn_out_w)
    output = output_step(to_blocks(part), after_cross).reshape(1, slots, width)

    cuts = ffn_out_w.shape[0]

    def cut(grad):
        return grad.reshape(grad.shape[0], cuts, -1)

    grad_ffn_out = scatter_out(dot("sf,szd->zfd", hidden, cut(grad_all)), x)
    grad_hidden = dot("szd,zfd->sf", cut(grad_all), ffn_out_w)
    grad_gate_up = rounded(jax.vjp(gated_gelu, gate_up)[1](grad_hidden)[0])
    grad_ffn_in = scatter_in(dot("sd,csf->cdf", normed_ffn, grad_gate_up), x)
    part = dot("csf,cdf->sd", grad_gate_up, ffn_in_w)
    grad_after_cross, gain_ffn, grad_all = backward_step(
        to_blocks(part), after_cross, own_grad, gain_of[2]
    )
    grad_all = from_blocks(grad_all)

    grad_cross_out = scatter_out(dot("sk,szd->zkd", mixed_cross, cut(grad_all)), x)
    grad_mixed = split_heads(rounded(dot("szd,zkd->sk", cut(grad_all), cross_out_w)))
    grad_queries, grad_keys, grad_values = attend_back(
        query_heads, cross_keys, cross_values, cross_allowed, total_cross, grad_mixed
    )
    part = dot("sf,df->sd", grad_queries, cross_q_w)
    grad_after_self, gain_cross, grad_all = backward_step(
        to_blocks(part), after_self, grad_after_cross, gain_of[1]
    )
    grad_all = from_blocks(grad_all)
    grad_key_value = jnp.stack([grad_keys, grad_values])
    grad_cross_q = scatter_in(dot("sd,sf->df", normed_cross, grad_queries), x)
    grad_cross_kv = scatter_in(dot("pd,cpf->cdf", memory, grad_key_value), x)
    part = rounded(dot("cpf,cdf->pd", grad_key_value, cross_kv_w))
    part = part.reshape(part.shape[0], 4, 2, -1).transpose(2, 1, 0, 3)
    grad_memory = scatter_step(part.reshape(8, *memory_part.shape))
    grad_patch = scatter_in(dot("pk,pd->kd", patch_all, grad_memory), x)

    grad_self_out = scatter_out(dot("sk,szd->zkd", mixed_self, cut(grad_all)), x)
    grad_mixed = split_heads(rounded(dot("szd,zkd->sk", cut(grad_all), self_out_w)))
    grad_projected = jnp.stack(attend_back(*self_parts, self_allowed, total_self, grad_mixed))
    grad_self_qkv = scatter_in(dot("sd,csf->cdf", normed_self, grad_projected), x)
    part = dot("csf,cdf->sd", grad_projected, qkv_w)
    grad_input, gain_self = input_step(to_blocks(part), own_tokens, grad_after_self, gain_of[0])
    grad_input = grad_input.reshape(1, slots, width)
    grad_gains = jnp.concatenate([gain_self, gain_cross, gain_ffn], axis=0)
    grad_gains = lax.psum_scatter(
        lax.psum(grad_gains, "mp"), ("z", "x"), scatter_dimension=1, tiled=True
    )
    return (
        output,
        grad_input,
        grad_gains,
        grad_self_qkv,
        grad_self_out,
        grad_cross_q,
        grad_cross_kv,
        grad_cross_out,
        grad_patch,
        grad_ffn_in,
        grad_ffn_out,
    )


def solution(mesh):
    batch, parts = mesh.shape["batch"], mesh.shape["mp"]
    planes = Mesh(mesh.devices.reshape(batch // 2, 2, parts), ("z", "x", "mp"))
    b = ("z", "x")
    weights = (
        P(None, b, "mp"),
        P("mp", b),
        P(b, "mp"),
        P(None, b, "mp"),
        P("mp", b),
        P(b, "mp"),
        P(None, b, "mp"),
        P("mp", b),
    )
    row = P(b, None, None)
    return jax.shard_map(
        on_device,
        mesh=planes,
        in_specs=(row, row, P(b), P(b, None), P(None, b)) + weights + (row,),
        out_specs=(row, row, P(None, b)) + weights,
        check_vma=False,
    )
```

time: 2320 us -> 1000 us (0.43)
  waiting for transfers between devices: 2080 us -> 384 us
  Pallas kernels: 0 us -> 222 us
  blocking collectives: 28.4 us -> 124 us
  local copies, waits for them, and re-layouts: 41.3 us -> 104 us
  matrix products: 123 us -> 92.7 us
  starting transfers between devices: 2.24 us -> 29.2 us
    reduce_scatter x14 -> x8, waiting for transfers between devices: 1300 us -> 297 us  [the longest x5 212 us: scatter_in(): lax.psum_scatter(rounded(grad), 'z', scatter_dimension=grad.ndim - 2, til...]
    all_gather x15 -> x7, waiting for transfers between devices: 664 us -> 43.3 us  [the longest x3 43.3 us: gather_out(): return lax.all_gather(exchange(weight, 0, 1, x), 'z', axis=0, tiled=False)]
    pallas_call x0 -> x8, Pallas kernels: none -> 222 us  [plane_call(): pl.pallas_call(kernel, name=name, out_shape=outs, in_specs=[whole] * len(...]
    unnamed x33 -> x17, waiting for transfers between devices: 115 us -> 0.28 us
    all_gather x1 -> x3, blocking collectives: 28.4 us -> 116 us  [the longest x1 64.2 us: on_device(): facts = lax.all_gather(facts, 'x', axis=0, tiled=True)]
    ppermute x0 -> x19, waiting for transfers between devices: none -> 43 us  [the longest x16 43 us: exchange(): return in_order(keep, lax.ppermute(give, 'x', SWAP), join, x)]
    ppermute x0 -> x19, starting transfers between devices: none -> 27.8 us  [the longest x16 22.8 us: exchange(): return in_order(keep, lax.ppermute(give, 'x', SWAP), join, x)]
    dot_general x23, matrix products: 107 us -> 83.1 us  [dot(): return jnp.einsum(pattern, left, right, preferred_element_type=jnp.float32)]
  transfers between devices with their start and end apart: 31 -> 35, of which waited for: 30 -> 17; matrix products, arithmetic and copies ran while one was open for 5% -> 14% of each run, Pallas kernels for 0% -> 12%
where the time goes in v1:
time: 1000 us; the launch traced here: 999 us
  waiting for transfers between devices  384 us (38%)
  Pallas kernels  222 us (22%)
  blocking collectives  124 us (12%)
  local copies, waits for them, and re-layouts  104 us (10%)
  matrix products  92.7 us (9%)
  starting transfers between devices  29.2 us (3%)
  other arithmetic  26.8 us (3%)
  between operations  16.1 us (2%)
    pallas_call x8, Pallas kernels, plane_call(): pl.pallas_call(kernel, name=name, out_shape=outs, in_specs=[whole] * len(...  222 us
    reduce_scatter x5, waiting for transfers between devices, scatter_in(): lax.psum_scatter(rounded(grad), 'z', scatter_dimension=grad.ndim - 2, til...  212 us
    reduce_scatter x3, waiting for transfers between devices, scatter_out(): lax.psum_scatter(rounded(grad), 'z', scatter_dimension=0, tiled=False)  85.4 us
    dot_general x23, matrix products, dot(): return jnp.einsum(pattern, left, right, preferred_element_type=jnp.float32)  83.1 us
    all_gather x1, blocking collectives, on_device(): facts = lax.all_gather(facts, 'x', axis=0, tiled=True)  64.2 us
    all_gather x3, waiting for transfers between devices, gather_out(): return lax.all_gather(exchange(weight, 0, 1, x), 'z', axis=0, tiled=False)  43.3 us
    ppermute x16, waiting for transfers between devices, exchange(): return in_order(keep, lax.ppermute(give, 'x', SWAP), join, x)  43 us
    unnamed x152, local copies, waits for them, and re-layouts  31.1 us
  transfers between devices with their start and end apart: 35, of which 17 were waited for; matrix products, arithmetic and copies ran while one was open for 14% of the time, Pallas kernels for 12%

profile of v1, /device:TPU:0, one launch (start us, length us, event | category | flops | bytes accessed | tf_op | source)
XLA Modules:
  0.0 999.0 jit_solution(17972378549637845203)
XLA Ops:
  11.7 6.2 collective-permute-done.1
  21.1 8.4 collective-permute-done.4
  50.9 11.2 %collective-permute-done = bf16[2,256,640]{1,2,0:T(8,128)(2,1)S(1)} collective-permute-done((bf16[2,256,640]{1,2,0:T(8,128)(2,1)S(1)}, bf16[2,256,640]{1,2,0:T(8,128)(2,1)S(1)}, u32[]{:S(2)}, u32[]{:S(2)}) %collective-permute-start) | collective-permute-done | bytes 655392 | tf_op jit(solution)/shard_map/ppermute | solution.py:329
  70.1 64.2 %all-gather = s32[2,1,257]{2,1,0:T(1,128)S(1)} all-gather(s32[1,1,257]{2,1,0:T(1,128)S(1)} %add_bitcast_fusion), channel_id=1, replica_groups=mesh['z'=4,'x'=2,'mp'=4] {'x'}, dimensions={0}, use_global_device_ids=true | all-gather | bytes 3084 | tf_op jit(solution)/shard_map/all_gather | solution.py:378
  134.4 26.6 %all_gather.38 = bf16[3,2048]{1,0:T(4,128)(2,1)S(1)} all-gather(bf16[3,256]{1,0:T(4,128)(2,1)S(1)} %copy-done.57), channel_id=1, replica_groups=mesh['z'=4,'x'=2,'mp'=4] {'z','x'}, dimensions={1}, use_global_device_ids=true | all-gather | bytes 13824 | tf_op jit(solution)/shard_map/all_gather | solution.py:375
  167.2 25.6 %all_gather.35 = bf16[1664,256]{1,0:T(8,128)(2,1)S(1)} all-gather(bf16[416,256]{1,0:T(8,128)(2,1)S(1)} %maximum_select_fusion.21), channel_id=1, replica_groups=mesh['z'=4,'x'=2,'mp'=4] {'z'}, dimensions={0}, use_global_device_ids=true | all-gather | bytes 1064960 | tf_op jit(solution)/shard_map/all_gather | solution.py:338
  197.1 15.4 %gather_step.1 = bf16[8,512,256]{2,1,0:T(8,128)(2,1)S(1)} custom-call(bf16[512,256]{1,0:T(8,128)(2,1)S(1)} %convolution_convert_fusion.17.own), custom_call_target="tpu_custom_call" | custom-call | tf_op jit(solution)/shard_map/gather_step/pallas_call | solution.py:189
  245.2 32.9 %forward_step.2 = (f32[64,2048]{1,0:T(8,128)S(1)}, bf16[8,64,2048]{2,1,0:T(8,128)(2,1)S(1)}) custom-call(bf16[8,64,2048]{2,1,0:T(8,128)(2,1)S(1)} %reshape.384.part, f32[64,2048]{1,0:T(8,128)S(1)} %bitcast_convert_fusion.4.residual.values, f32[1,2048]{1,0:T(1,128)S(1)} %get-tuple-element.120.gain), custom_call_target="tpu_custom_call" | custom-call | tf_op jit(solution)/shard_map/forward_step/pallas_call | solution.py:189
  294.9 32.1 %forward_step.3 = (f32[64,2048]{1,0:T(8,128)S(1)}, bf16[8,64,2048]{2,1,0:T(8,128)(2,1)S(1)}) custom-call(bf16[8,64,2048]{2,1,0:T(8,128)(2,1)S(1)} %reshape.387.part, f32[64,2048]{1,0:T(8,128)S(1)} %copy-done.5, f32[1,2048]{1,0:T(1,128)S(1)} %get-tuple-element.119.gain), custom_call_target="tpu_custom_call" | custom-call | tf_op jit(solution)/shard_map/forward_step/pallas_call | solution.py:189
  328.3 7.9 convolution_bitcast_fusion
  336.3 43.3 %all-gather.21.cloned.1.call-done = bf16[4,640,512]{2,1,0:T(8,128)(2,1)} async-done(((bf16[1,640,512]{2,1,0:T(8,128)(2,1)}), bf16[4,640,512]{2,1,0:T(8,128)(2,1)}) %all-gather.21.cloned.1.call-update) | async-done | bytes 2621456 | tf_op jit(solution)/shard_map/all_gather | solution.py:342
  379.5 6.6 multiply_bitcast_fusion
  389.6 32.8 %backward_step.2 = (f32[64,2048]{1,0:T(8,128)S(1)}, f32[1,2048]{1,0:T(1,128)S(1)}, bf16[8,64,2048]{2,1,0:T(8,128)(2,1)S(1)}) custom-call(bf16[8,64,2048]{2,1,0:T(8,128)(2,1)S(1)} %bitcast.229, f32[64,2048]{1,0:T(8,128)S(1)} %get-tuple-element.26.residual.values, f32[64,2048]{1,0:T(8,128)S(1)} %copy-done.7, f32[1,2048]{1,0:T(1,128)S(1)} %get-tuple-element.119.gain), custom_call_target="tpu_custom_call" | custom-call | tf_op jit(solution)/shard_map/backward_step/pallas_call | solution.py:189
  439.3 32.5 %backward_step.3 = (f32[64,2048]{1,0:T(8,128)S(1)}, f32[1,2048]{1,0:T(1,128)S(1)}, bf16[8,64,2048]{2,1,0:T(8,128)(2,1)S(1)}) custom-call(bf16[8,64,2048]{2,1,0:T(8,128)(2,1)S(1)} %bitcast.225, f32[64,2048]{1,0:T(8,128)S(1)} %copy-done.6, f32[64,2048]{1,0:T(8,128)S(1)} %copy-done.9, f32[1,2048]{1,0:T(1,128)S(1)} %get-tuple-element.120.gain), custom_call_target="tpu_custom_call" | custom-call | tf_op jit(solution)/shard_map/backward_step/pallas_call | solution.py:189
  501.7 32.4 %input_step.1 = (f32[4,64,2048]{2,1,0:T(8,128)S(1)}, f32[1,2048]{1,0:T(1,128)S(1)}) custom-call(bf16[8,64,2048]{2,1,0:T(8,128)(2,1)S(1)} %bitcast.230, f32[64,2048]{1,0:T(8,128)S(1)} %bitcast_convert_fusion.4.residual.values, f32[64,2048]{1,0:T(8,128)S(1)} %get-tuple-element.30.grad, f32[1,2048]{1,0:T(1,128)S(1)} %get-tuple-element.121.gain), custom_call_target="tpu_custom_call" | custom-call | tf_op jit(solution)/shard_map/input_step/pallas_call | solution.py:189
  545.8 18.4 %scatter_step.1 = bf16[512,256]{1,0:T(8,128)(2,1)S(1)} custom-call(bf16[8,512,256]{2,1,0:T(8,128)(2,1)S(1)} %bitcast.227), custom_call_target="tpu_custom_call" | custom-call | tf_op jit(solution)/shard_map/scatter_step/pallas_call | solution.py:189
  610.6 25.5 %output_step.1 = bf16[4,64,2048]{2,1,0:T(8,128)(2,1)S(1)} custom-call(bf16[8,64,2048]{2,1,0:T(8,128)(2,1)S(1)} %reshape.389.part, f32[64,2048]{1,0:T(8,128)S(1)} %copy-done.3), custom_call_target="tpu_custom_call" | custom-call | tf_op jit(solution)/shard_map/output_step/pallas_call | solution.py:189
  637.1 7.6 psum.8
  652.5 28.2 %reduce-scatter.14.cloned.1.call-done = bf16[1,256,512]{1,2,0:T(8,128)(2,1)} async-done(((bf16[4,256,512]{1,2,0:T(8,128)(2,1)}), bf16[1,256,512]{1,2,0:T(8,128)(2,1)}) %reduce-scatter.14.cloned.1.call-update) | async-done | bytes 262160 | tf_op jit(solution)/shard_map/reduce_scatter | solution.py:351
  683.5 25.2 %reduce-scatter.16.cloned.1.call-done = bf16[512,256]{1,0:T(8,128)(2,1)} async-done(((bf16[2048,256]{1,0:T(8,128)(2,1)}), bf16[512,256]{1,0:T(8,128)(2,1)}) %reduce-scatter.16.cloned.1.call-update) | async-done | bytes 262160 | tf_op jit(solution)/shard_map/reduce_scatter | solution.py:346
  718.5 35.1 %reduce-scatter.18.cloned.1.call-done = bf16[2,512,256]{1,2,0:T(8,128)(2,1)} async-done(((bf16[2,2048,256]{1,2,0:T(8,128)(2,1)}), bf16[2,512,256]{1,2,0:T(8,128)(2,1)}) %reduce-scatter.18.cloned.1.call-update) | async-done | bytes 524304 | tf_op jit(solution)/shard_map/reduce_scatter | solution.py:346
  756.3 51.6 %reduce-scatter.26.cloned.1.call-done = bf16[1,640,512]{1,2,0:T(8,128)(2,1)} async-done(((bf16[4,640,512]{1,2,0:T(8,128)(2,1)}), bf16[1,640,512]{1,2,0:T(8,128)(2,1)}) %reduce-scatter.26.cloned.1.call-update) | async-done | bytes 655376 | tf_op jit(solution)/shard_map/reduce_scatter | solution.py:351
  811.4 92.1 %reduce-scatter.24.cloned.1.call-done = bf16[2,512,640]{1,2,0:T(8,128)(2,1)} async-done(((bf16[2,2048,640]{1,2,0:T(8,128)(2,1)}), bf16[2,512,640]{1,2,0:T(8,128)(2,1)}) %reduce-scatter.24.cloned.1.call-update) | async-done | bytes 1310736 | tf_op jit(solution)/shard_map/reduce_scatter | solution.py:346
  907.2 59.3 %reduce-scatter.12.cloned.1.call-done = bf16[3,512,256]{1,2,0:T(8,128)(2,1)} async-done(((bf16[3,2048,256]{1,2,0:T(8,128)(2,1)}), bf16[3,512,256]{1,2,0:T(8,128)(2,1)}) %reduce-scatter.12.cloned.1.call-update) | async-done | bytes 786448 | tf_op jit(solution)/shard_map/reduce_scatter | solution.py:346
  (361 shorter events, 261.6 us)
Async XLA Ops:
  7.2 215.6 %all-gather.11.cloned.1.call-start = ((), (), s32[]{:S(2)}) async-start(), calls=%async_computation.10 | async-start | bytes 2621440 | tf_op jit(solution)/shard_map/all_gather | solution.py:338
  18.8 207.2 %all-gather.13.cloned.1.call-start = ((), (), s32[]{:S(2)}) async-start(), calls=%async_computation.11 | async-start | bytes 3932160 | tf_op jit(solution)/shard_map/all_gather | solution.py:338
  30.6 206.1 %all-gather.15.cloned.1.call-start = ((), (), s32[]{:S(2)}) async-start(), calls=%async_computation.12 | async-start | bytes 1310720 | tf_op jit(solution)/shard_map/all_gather | solution.py:342
  36.5 243.7 %all-gather.17.cloned.1.call-start = ((), (), s32[]{:S(2)}) async-start(), calls=%async_computation.13 | async-start | bytes 1310720 | tf_op jit(solution)/shard_map/all_gather | solution.py:338
  42.5 243.0 %all-gather.19.cloned.1.call-start = ((), (), s32[]{:S(2)}) async-start(), calls=%async_computation.14 | async-start | bytes 1310720 | tf_op jit(solution)/shard_map/all_gather | solution.py:342
  48.5 279.9 %all-gather.9.cloned.1.call-start = ((), (), s32[]{:S(2)}) async-start(), calls=%async_computation.9 | async-start | bytes 6553600 | tf_op jit(solution)/shard_map/all_gather | solution.py:338
  63.5 316.1 %all-gather.21.cloned.1.call-start = ((), (), s32[]{:S(2)}) async-start(), calls=%async_computation.15 | async-start | bytes 3276800 | tf_op jit(solution)/shard_map/all_gather | solution.py:342
  63.5 153.9 %collective-permute-start.5 = (bf16[256,2048]{1,0:T(8,128)(2,1)}, bf16[256,2048]{1,0:T(8,128)(2,1)}, u32[]{:S(2)}, u32[]{:S(2)}) collective-permute-start(bf16[256,2048]{1,0:T(8,128)(2,1)} %bitcast.6), channel_id=1, source_target_pairs={{0,4},{4,0},{1,5},{5,1},{2,6},{6,2},{3,7},{7,3},{8,12},{12,8},{9,1... | collective-permute-start | bytes 3145736 | tf_op jit(solution)/shard_map/ppermute | solution.py:333
  65.2 101.8 %collective-permute-start.3 = (bf16[208,256]{1,0:T(8,128)(2,1)S(1)}, bf16[208,256]{1,0:T(8,128)(2,1)S(1)}, u32[]{:S(2)}, u32[]{:S(2)}) collective-permute-start(bf16[208,256]{1,0:T(8,128)(2,1)S(1)} %get-tuple-element.118), channel_id=1, source_target_pairs={{0,4},{4,0},{1,5},{5,1},{2,6},{6,2},{3,7},{7,3},{8,12},{12,8},{9,1... | collective-permute-start | bytes 319496 | tf_op jit(solution)/shard_map/ppermute | solution.py:329
  65.7 128.7 %collective-permute-start.2 = (bf16[256,1664]{1,0:T(8,128)(2,1)}, bf16[256,1664]{1,0:T(8,128)(2,1)}, u32[]{:S(2)}, u32[]{:S(2)}) collective-permute-start(bf16[256,1664]{1,0:T(8,128)(2,1)} %bitcast.263), channel_id=1, source_target_pairs={{0,4},{4,0},{1,5},{5,1},{2,6},{6,2},{3,7},{7,3},{8,12},{12,8},{9,1... | collective-permute-start | bytes 2555912 | tf_op jit(solution)/shard_map/ppermute | solution.py:333
  67.4 125.4 %collective-permute-start.9 = (bf16[640,256]{1,0:T(8,128)(2,1)S(1)}, bf16[640,256]{1,0:T(8,128)(2,1)S(1)}, u32[]{:S(2)}, u32[]{:S(2)}) collective-permute-start(bf16[640,256]{1,0:T(8,128)(2,1)S(1)} %get-tuple-element.96), channel_id=1, source_target_pairs={{0,4},{4,0},{1,5},{5,1},{2,6},{6,2},{3,7},{7,3},{8,12},{12,8},{9,1... | collective-permute-start | bytes 983048 | tf_op jit(solution)/shard_map/ppermute | solution.py:329
  67.8 152.7 %collective-permute-start.10 = (bf16[256,2048]{1,0:T(8,128)(2,1)}, bf16[256,2048]{1,0:T(8,128)(2,1)}, u32[]{:S(2)}, u32[]{:S(2)}) collective-permute-start(bf16[256,2048]{1,0:T(8,128)(2,1)} %bitcast.29), channel_id=1, source_target_pairs={{0,4},{4,0},{1,5},{5,1},{2,6},{6,2},{3,7},{7,3},{8,12},{12,8},{9,1... | collective-permute-start | bytes 3145736 | tf_op jit(solution)/shard_map/ppermute | solution.py:333
  193.8 442.3 %reduce-scatter.28.cloned.1.call-start = ((), (), s32[]{:S(2)}) async-start(), calls=%async_computation.24 | async-start | bytes 1179648
  536.7 108.0 %reduce-scatter.22.cloned.1.call-start = ((), (), s32[]{:S(2)}) async-start(), calls=%async_computation.21 | async-start | bytes 1064960 | tf_op jit(solution)/shard_map/reduce_scatter | solution.py:346
  567.4 85.1 %reduce-scatter.20.cloned.1.call-start = ((), (), s32[]{:S(2)}) async-start(), calls=%async_computation.20 | async-start | bytes 1310720 | tf_op jit(solution)/shard_map/reduce_scatter | solution.py:351
  569.3 111.4 %reduce-scatter.14.cloned.1.call-start = ((), (), s32[]{:S(2)}) async-start(), calls=%async_computation.17 | async-start | bytes 1310720 | tf_op jit(solution)/shard_map/reduce_scatter | solution.py:351
  572.9 135.8 %reduce-scatter.16.cloned.1.call-start = ((), (), s32[]{:S(2)}) async-start(), calls=%async_computation.18 | async-start | bytes 1310720 | tf_op jit(solution)/shard_map/reduce_scatter | solution.py:346
  574.8 178.8 %reduce-scatter.18.cloned.1.call-start = ((), (), s32[]{:S(2)}) async-start(), calls=%async_computation.19 | async-start | bytes 2621440 | tf_op jit(solution)/shard_map/reduce_scatter | solution.py:346
  579.1 228.8 %reduce-scatter.26.cloned.1.call-start = ((), (), s32[]{:S(2)}) async-start(), calls=%async_computation.23 | async-start | bytes 3276800 | tf_op jit(solution)/shard_map/reduce_scatter | solution.py:351
  585.1 318.3 %reduce-scatter.24.cloned.1.call-start = ((), (), s32[]{:S(2)}) async-start(), calls=%async_computation.22 | async-start | bytes 6553600 | tf_op jit(solution)/shard_map/reduce_scatter | solution.py:346
  592.7 373.7 %reduce-scatter.12.cloned.1.call-start = ((), (), s32[]{:S(2)}) async-start(), calls=%async_computation.16 | async-start | bytes 3932160 | tf_op jit(solution)/shard_map/reduce_scatter | solution.py:346
  754.7 215.2 %collective-permute-start.14 = (bf16[2,256,256]{1,2,0:T(8,128)(2,1)S(1)}, bf16[2,256,256]{1,2,0:T(8,128)(2,1)S(1)}, u32[]{:S(2)}, u32[]{:S(2)}) collective-permute-start(bf16[2,256,256]{1,2,0:T(8,128)(2,1)S(1)} %get-tuple-element.98), channel_id=1, source_target_pairs={{0,4},{4,0},{1,5},{5,1},{2,6},{6,2},{3,7},{7,3},{8,12},{12,8},{9,1... | collective-permute-start | bytes 786440 | tf_op jit(solution)/shard_map/ppermute | solution.py:329
  809.9 163.5 %collective-permute-start.18 = (bf16[640,256]{1,0:T(8,128)(2,1)}, bf16[640,256]{1,0:T(8,128)(2,1)}, u32[]{:S(2)}, u32[]{:S(2)}) collective-permute-start(bf16[640,256]{1,0:T(8,128)(2,1)} %bitcast.69), channel_id=1, source_target_pairs={{0,4},{4,0},{1,5},{5,1},{2,6},{6,2},{3,7},{7,3},{8,12},{12,8},{9,1... | collective-permute-start | bytes 983048 | tf_op jit(solution)/shard_map/ppermute | solution.py:329
  905.7 77.0 %collective-permute-start.17 = (bf16[2,256,640]{1,2,0:T(8,128)(2,1)}, bf16[2,256,640]{1,2,0:T(8,128)(2,1)}, u32[]{:S(2)}, u32[]{:S(2)}) collective-permute-start(bf16[2,256,640]{1,2,0:T(8,128)(2,1)} %get-tuple-element.83), channel_id=1, source_target_pairs={{0,4},{4,0},{1,5},{5,1},{2,6},{6,2},{3,7},{7,3},{8,12},{12,8},{9,1... | collective-permute-start | bytes 1966088 | tf_op jit(solution)/shard_map/ppermute | solution.py:329
  (77 other events, 767.2 us)
Sparse Core Ops, SparseCore 0:
  18.9 47.4 all-gather.10
  68.5 62.1 all-gather.12
  132.9 26.6 all-gather.14
  161.5 33.8 all-gather.16
  197.4 27.7 all-gather.18
  227.2 97.5 all-gather.8
  326.4 53.1 all-gather.20
  536.8 61.5 reduce-scatter.27
  600.8 23.1 reduce-scatter.21
  626.2 26.2 reduce-scatter.19
  654.9 25.7 reduce-scatter.13
  682.9 25.7 reduce-scatter.15
  711.1 42.5 reduce-scatter.17
  756.4 51.4 reduce-scatter.25
  810.0 93.4 reduce-scatter.23
  905.6 60.7 reduce-scatter.11

commit v2 on v1

--- a/solution.py
+++ b/solution.py
@@ -309,47 +309,74 @@
 SWAP = ((0, 1), (1, 0))
 
 
-def halves(values, axis, x):
-    size = values.shape[axis] // 2
-    keep = lax.dynamic_slice_in_dim(values, x * size, size, axis)
-    give = lax.dynamic_slice_in_dim(values, (1 - x) * size, size, axis)
-    return keep, give
-
-
-def in_order(own, other, axis, x):
-    return jnp.where(
-        x == 0,
-        jnp.concatenate([own, other], axis),
-        jnp.concatenate([other, own], axis),
-    )
-
-
-def exchange(values, cut, join, x):
-    keep, give = halves(values, cut, x)
-    return in_order(keep, lax.ppermute(give, "x", SWAP), join, x)
+def ignore(*refs):
+    del refs
+
+
+def after(value, *earlier):
+    anywhere = pl.BlockSpec(memory_space=pl.ANY)
+    return pl.pallas_call(
+        ignore,
+        name="after",
+        out_shape=jax.ShapeDtypeStruct(value.shape, value.dtype),
+        in_specs=[anywhere] * (1 + len(earlier)),
+        out_specs=anywhere,
+        input_output_aliases={0: 0},
+    )(value, *earlier)
+
+
+def either(own, other, x, join):
+    return jnp.where(x == 0, join([own, other]), join([other, own]))
 
 
 def both_items(values, x):
-    return in_order(values, lax.ppermute(values, "x", SWAP), 0, x)
-
-
-def gather_in(weight, x):
-    swapped = exchange(weight, weight.ndim - 1, weight.ndim - 2, x)
-    return lax.all_gather(swapped, "z", axis=weight.ndim - 2, tiled=True)
-
-
-def gather_out(weight, x):
-    return lax.all_gather(exchange(weight, 0, 1, x), "z", axis=0, tiled=False)
-
-
-def scatter_in(grad, x):
-    share = lax.psum_scatter(rounded(grad), "z", scatter_dimension=grad.ndim - 2, tiled=True)
-    return exchange(share, grad.ndim - 2, grad.ndim - 1, x).astype(jnp.float32)
-
-
-def scatter_out(grad, x):
-    share = lax.psum_scatter(rounded(grad), "z", scatter_dimension=0, tiled=False)
-    return exchange(share, 1, 0, x).astype(jnp.float32)
+    return either(values, lax.ppermute(values, "x", SWAP), x, jnp.concatenate)
+
+
+def cut_in(weight, x):
+    flat = weight.reshape(-1, weight.shape[-1])
+    size = flat.shape[1] // 2
+    return [lax.dynamic_slice_in_dim(flat, k * size, size, 1) for k in (x, 1 - x)]
+
+
+def cut_out(weight, x, columns):
+    size = weight.shape[0] // 2
+    return [
+        lax.dynamic_slice_in_dim(weight, k * size, size, 0).reshape(-1, columns)
+        for k in (x, 1 - x)
+    ]
+
+
+def swap_group(pairs, x, *earlier):
+    keep = jnp.concatenate([pair[0] for pair in pairs])
+    give = jnp.concatenate([pair[1] for pair in pairs])
+    if earlier:
+        give = after(give, *earlier)
+    return either(keep, lax.ppermute(give, "x", SWAP), x, jnp.stack)
+
+
+def gather_group(swapped):
+    return lax.all_gather(swapped, "z", axis=0, tiled=True)
+
+
+def scatter_group(parts):
+    return lax.psum_scatter(parts, "z", scatter_dimension=0, tiled=True)
+
+
+def home_group(share, x):
+    give = lax.dynamic_index_in_dim(share, 1 - x, 0, False)
+    return lax.dynamic_index_in_dim(share, x, 0, False), lax.ppermute(give, "x", SWAP)
+
+
+def home(pair, place, shape, axis, x):
+    own, other = (half[place[0] : place[1]].reshape(shape) for half in pair)
+    joined = either(own, other, x, functools.partial(jnp.concatenate, axis=axis))
+    return joined.astype(jnp.float32)
+
+
+def places(*sizes):
+    ends = [sum(sizes[: k + 1]) for k in range(len(sizes))]
+    return [(end - size, end) for end, size in zip(ends, sizes)]
 
 
 def on_device(
@@ -372,29 +399,59 @@
     m = lax.axis_index("mp")
     slots, width = tokens.shape[1], tokens.shape[2]
     rows = slots // 4
-    gains = lax.all_gather(norm_gains, ("z", "x"), axis=1, tiled=True).astype(jnp.float32)
+    depth, patch_depth = cross_q.shape[0], patch_proj.shape[0]
+    blocks = width // depth
+    heads, units = self_out.shape[0] // 2, ffn_out.shape[0] // 2
+    at_patch, at_qkv, at_gain = places(patch_depth, 3 * depth, 16)
+    at_kv, at_q, at_self, at_cross = places(2 * depth, depth, depth, depth)
+
+    def padded(values):
+        flat = values.reshape(-1, 3 * depth)
+        return jnp.pad(flat, ((0, 0), (0, 16 * heads - 3 * depth))).reshape(-1, 16, heads)
+
+    def unpadded(values):
+        return values.reshape(-1, 16 * heads)[:, : 3 * depth].reshape(-1, 3, depth)
+
+    first = swap_group(
+        [cut_in(patch_proj, x), cut_in(self_qkv, x), [padded(norm_gains)[0]] * 2], x
+    )
+    first_w = gather_group(first)
+    token_all = both_items(after(tokens[0], first), x)
+    second = swap_group(
+        [
+            cut_in(cross_kv, x),
+            cut_in(cross_q, x),
+            cut_out(self_out, x, heads),
+            cut_out(cross_out, x, heads),
+        ],
+        x,
+        token_all,
+    )
+    second_w = gather_group(after(second, first_w))
+    patch_all = both_items(after(patches[0], second), x)
+    third = swap_group([cut_in(ffn_in, x)], x, patch_all)
+    fourth = swap_group([cut_out(ffn_out, x, depth)], x, third)
+    grad_all = both_items(after(cotangent[0], fourth), x)
+
+    patch_w = first_w[:, at_patch[0] : at_patch[1]].reshape(-1, heads)
+    qkv_w = first_w[:, at_qkv[0] : at_qkv[1]].reshape(blocks, 3, depth, heads)
+    cross_kv_w = second_w[:, at_kv[0] : at_kv[1]].reshape(blocks, 2, depth, heads)
+    cross_q_w = second_w[:, at_q[0] : at_q[1]].reshape(width, heads)
+    self_out_w = second_w[:, at_self[0] : at_self[1]].reshape(blocks, heads, depth)
+    cross_out_w = second_w[:, at_cross[0] : at_cross[1]].reshape(blocks, heads, depth)
+
+    gains = unpadded(first_w[:, at_gain[0] : at_gain[1]])
+    gains = gains.transpose(1, 0, 2).reshape(3, width).astype(jnp.float32)
     gain_of = [gains[i : i + 1] for i in range(3)]
     facts = jnp.concatenate([patch_keep, lengths[:, None]], axis=1)
     facts = lax.all_gather(facts, "x", axis=0, tiled=True)
     patch_keep, lengths = facts[:, :-1], facts[:, -1]
 
-    patch_w = gather_in(patch_proj, x)
-    qkv_w = gather_in(self_qkv, x)
-    self_out_w = gather_out(self_out, x)
-    cross_kv_w = gather_in(cross_kv, x)
-    cross_q_w = gather_in(cross_q, x)
-    cross_out_w = gather_out(cross_out, x)
-    ffn_in_w = gather_in(ffn_in, x)
-    ffn_out_w = gather_out(ffn_out, x)
-
     row_index = lax.broadcasted_iota(jnp.int32, (slots, slots), 0)
     col_index = lax.broadcasted_iota(jnp.int32, (slots, slots), 1)
     self_allowed = (col_index <= row_index)[None] & (col_index[None] < lengths[:, None, None])
     cross_allowed = (patch_keep > 0)[:, None, :]
 
-    token_all = both_items(tokens[0], x)
-    patch_all = both_items(patches[0], x)
-    grad_all = both_items(cotangent[0], x)
     own_tokens = lax.dynamic_slice_in_dim(tokens[0], m * rows, rows, 0).astype(jnp.float32)
     own_grad = lax.dynamic_slice_in_dim(cotangent[0], m * rows, rows, 0).astype(jnp.float32)
 
@@ -408,9 +465,18 @@
     def to_blocks(partial_value):
         return rounded(partial_value).reshape(8, rows, width)
 
-    def from_blocks(blocks):
-        return blocks.reshape(8 * rows, width)
-
+    def from_blocks(values):
+        return values.reshape(8 * rows, width)
+
+    def cut(values):
+        return values.reshape(values.shape[0], blocks, depth)
+
+    def stacked(*parts):
+        return jnp.concatenate([rounded(part).reshape(blocks, -1, heads) for part in parts], axis=1)
+
+    projected = rounded(dot("sbd,bcdf->csf", cut(normed_self), qkv_w))
+    self_parts = [split_heads(projected[i]) for i in range(3)]
+    mixed_self, total_self = attend(*self_parts, self_allowed)
     memory_part = rounded(dot("pk,kd->pd", patch_all, patch_w))
     memory_blocks = gather_step(memory_part)
     memory = (
@@ -418,45 +484,43 @@
         .transpose(2, 1, 0, 3)
         .reshape(memory_part.shape[0], -1)
     )
-
-    projected = rounded(dot("sd,cdf->csf", normed_self, qkv_w))
-    self_parts = [split_heads(projected[i]) for i in range(3)]
-    mixed_self, total_self = attend(*self_parts, self_allowed)
-    part = dot("sk,zkd->szd", mixed_self, self_out_w)
+    third_w = gather_group(after(third, second_w, mixed_self, memory_blocks))
+    ffn_in_w = third_w.reshape(blocks, 2, depth, units)
+
+    part = dot("sk,bkd->sbd", mixed_self, self_out_w)
     after_self, normed_cross = forward_step(to_blocks(part), own_tokens, gain_of[1])
     normed_cross = from_blocks(normed_cross)
 
-    key_value = rounded(dot("pd,cdf->cpf", memory, cross_kv_w))
+    key_value = rounded(dot("pbd,bcdf->cpf", cut(memory), cross_kv_w))
     query_heads = split_heads(rounded(dot("sd,df->sf", normed_cross, cross_q_w)))
     cross_keys = split_heads(key_value[0])
     cross_values = split_heads(key_value[1])
     mixed_cross, total_cross = attend(query_heads, cross_keys, cross_values, cross_allowed)
-    part = dot("sk,zkd->szd", mixed_cross, cross_out_w)
+    part = dot("sk,bkd->sbd", mixed_cross, cross_out_w)
     after_cross, normed_ffn = forward_step(to_blocks(part), after_self, gain_of[2])
+    fourth_w = gather_group(after(fourth, third_w, normed_ffn))
+    ffn_out_w = fourth_w.reshape(blocks, units, depth)
     normed_ffn = from_blocks(normed_ffn)
 
-    gate_up = dot("sd,cdf->csf", normed_ffn, ffn_in_w)
+    gate_up = dot("sbd,bcdf->csf", cut(normed_ffn), ffn_in_w)
     hidden = rounded(gated_gelu(gate_up))
-    part = dot("sf,zfd->szd", hidden, ffn_out_w)
-    output = output_step(to_blocks(part), after_cross).reshape(1, slots, width)
-
-    cuts = ffn_out_w.shape[0]
-
-    def cut(grad):
-        return grad.reshape(grad.shape[0], cuts, -1)
-
-    grad_ffn_out = scatter_out(dot("sf,szd->zfd", hidden, cut(grad_all)), x)
-    grad_hidden = dot("szd,zfd->sf", cut(grad_all), ffn_out_w)
+    ffn_out_part = rounded(dot("sf,sbd->bfd", hidden, cut(grad_all)))
+    ffn_out_share = scatter_group(after(ffn_out_part, fourth_w))
+    output_part = to_blocks(dot("sf,bfd->sbd", hidden, ffn_out_w))
+
+    grad_hidden = dot("sbd,bfd->sf", cut(grad_all), ffn_out_w)
     grad_gate_up = rounded(jax.vjp(gated_gelu, gate_up)[1](grad_hidden)[0])
-    grad_ffn_in = scatter_in(dot("sd,csf->cdf", normed_ffn, grad_gate_up), x)
-    part = dot("csf,cdf->sd", grad_gate_up, ffn_in_w)
+    ffn_in_part = rounded(dot("sbd,csf->bcdf", cut(normed_ffn), grad_gate_up))
+    part = dot("csf,bcdf->sbd", grad_gate_up, ffn_in_w)
     grad_after_cross, gain_ffn, grad_all = backward_step(
         to_blocks(part), after_cross, own_grad, gain_of[2]
     )
+    ffn_in_part = ffn_in_part.reshape(blocks, 2 * depth, units)
+    ffn_in_share = scatter_group(after(ffn_in_part, ffn_out_share, grad_all))
     grad_all = from_blocks(grad_all)
 
-    grad_cross_out = scatter_out(dot("sk,szd->zkd", mixed_cross, cut(grad_all)), x)
-    grad_mixed = split_heads(rounded(dot("szd,zkd->sk", cut(grad_all), cross_out_w)))
+    cross_out_part = dot("sk,sbd->bkd", mixed_cross, cut(grad_all))
+    grad_mixed = split_heads(rounded(dot("sbd,bkd->sk", cut(grad_all), cross_out_w)))
     grad_queries, grad_keys, grad_values = attend_back(
         query_heads, cross_keys, cross_values, cross_allowed, total_cross, grad_mixed
     )
@@ -466,27 +530,53 @@
     )
     grad_all = from_blocks(grad_all)
     grad_key_value = jnp.stack([grad_keys, grad_values])
-    grad_cross_q = scatter_in(dot("sd,sf->df", normed_cross, grad_queries), x)
-    grad_cross_kv = scatter_in(dot("pd,cpf->cdf", memory, grad_key_value), x)
-    part = rounded(dot("cpf,cdf->pd", grad_key_value, cross_kv_w))
+    second_part = stacked(
+        dot("pbd,cpf->bcdf", cut(memory), grad_key_value),
+        dot("sbd,sf->bdf", cut(normed_cross), grad_queries),
+        cross_out_part,
+    )
+    self_out_part = dot("sk,sbd->bkd", mixed_self, cut(grad_all))
+    grad_mixed = split_heads(rounded(dot("sbd,bkd->sk", cut(grad_all), self_out_w)))
+    grad_projected = jnp.stack(attend_back(*self_parts, self_allowed, total_self, grad_mixed))
+    second_share = scatter_group(after(second_part, ffn_in_share, grad_projected))
+
+    part = rounded(dot("cpf,bcdf->pbd", grad_key_value, cross_kv_w))
     part = part.reshape(part.shape[0], 4, 2, -1).transpose(2, 1, 0, 3)
     grad_memory = scatter_step(part.reshape(8, *memory_part.shape))
-    grad_patch = scatter_in(dot("pk,pd->kd", patch_all, grad_memory), x)
-
-    grad_self_out = scatter_out(dot("sk,szd->zkd", mixed_self, cut(grad_all)), x)
-    grad_mixed = split_heads(rounded(dot("szd,zkd->sk", cut(grad_all), self_out_w)))
-    grad_projected = jnp.stack(attend_back(*self_parts, self_allowed, total_self, grad_mixed))
-    grad_self_qkv = scatter_in(dot("sd,csf->cdf", normed_self, grad_projected), x)
-    part = dot("csf,cdf->sd", grad_projected, qkv_w)
-    grad_input, gain_self = input_step(to_blocks(part), own_tokens, grad_after_self, gain_of[0])
-    grad_input = grad_input.reshape(1, slots, width)
-    grad_gains = jnp.concatenate([gain_self, gain_cross, gain_ffn], axis=0)
-    grad_gains = lax.psum_scatter(
-        lax.psum(grad_gains, "mp"), ("z", "x"), scatter_dimension=1, tiled=True
-    )
+    part = to_blocks(dot("csf,bcdf->sbd", grad_projected, qkv_w))
+    grad_input, gain_self = input_step(part, own_tokens, grad_after_self, gain_of[0])
+    gains_part = jnp.concatenate([gain_self, gain_cross, gain_ffn], axis=0)
+    gains_part = gains_part.reshape(3, blocks, depth).transpose(1, 0, 2)
+    patch_cut = patch_all.reshape(patch_all.shape[0], blocks, patch_depth)
+    first_part = stacked(
+        dot("pbk,pd->bkd", patch_cut, grad_memory),
+        dot("sbd,csf->bcdf", cut(normed_self), grad_projected),
+        self_out_part,
+        padded(gains_part),
+    )
+    first_part = after(first_part, second_share, grad_input)
+    first_share = scatter_group(first_part)
+    output = output_step(after(output_part, first_part), after_cross)
+
+    pair = home_group(after(ffn_out_share, first_part), x)
+    grad_ffn_out = home(pair, (0, units), (units, depth), 0, x)
+    pair = home_group(after(ffn_in_share, first_part), x)
+    grad_ffn_in = home(pair, (0, 2 * depth), (2, depth, units), 2, x)
+    pair = home_group(after(second_share, first_part), x)
+    at_kv, at_q, at_cross = places(2 * depth, depth, depth)
+    grad_cross_kv = home(pair, at_kv, (2, depth, heads), 2, x)
+    grad_cross_q = home(pair, at_q, (depth, heads), 1, x)
+    grad_cross_out = home(pair, at_cross, (heads, depth), 0, x)
+    pair = home_group(first_share, x)
+    at_patch, at_qkv, at_self, at_gain = places(patch_depth, 3 * depth, depth, 16)
+    grad_patch = home(pair, at_patch, (patch_depth, heads), 1, x)
+    grad_self_qkv = home(pair, at_qkv, (3, depth, heads), 2, x)
+    grad_self_out = home(pair, at_self, (heads, depth), 0, x)
+    grad_gains = sum(half[at_gain[0] : at_gain[1]].astype(jnp.float32) for half in pair)
+    grad_gains = lax.psum(unpadded(grad_gains)[0], "mp")
     return (
-        output,
-        grad_input,
+        output.reshape(1, slots, width),
+        grad_input.reshape(1, slots, width),
         grad_gains,
         grad_self_qkv,
         grad_self_out,

time: 1000 us -> 751 us (0.75)
  waiting for transfers between devices: 384 us -> 214 us
  blocking collectives: 124 us -> 25.1 us
  local copies, waits for them, and re-layouts: 104 us -> 130 us
  matrix products: 92.7 us -> 71.3 us
  other arithmetic: 26.8 us -> 38 us
  starting transfers between devices: 29.2 us -> 18 us
    reduce_scatter x8 -> x4, waiting for transfers between devices: 297 us -> 41.4 us  [scatter_group(): return lax.psum_scatter(parts, 'z', scatter_dimension=0, tiled=True)]
    all_gather x2 -> x0, blocking collectives: 52.3 us -> none  [the longest x1 26.6 us: on_device(): lax.all_gather(norm_gains, ('z', 'x'), axis=1, tiled=True)]
    ppermute x19 -> x11, waiting for transfers between devices: 43 us -> 94.8 us  [the longest x4 41.8 us: swap_group(): return either(keep, lax.ppermute(give, 'x', SWAP), x, jnp.stack)]
    all_gather x1, blocking collectives: 64.2 us -> 18.6 us  [on_device(): facts = lax.all_gather(facts, 'x', axis=0, tiled=True)]
    all_gather x7 -> x4, waiting for transfers between devices: 43.3 us -> 77.5 us  [gather_group(): return lax.all_gather(swapped, 'z', axis=0, tiled=True)]
    dot_general x23, matrix products: 83.1 us -> 60.3 us  [dot(): return jnp.einsum(pattern, left, right, preferred_element_type=jnp.float32)]
    convert_element_type x16 -> x24, local copies, waits for them, and re-layouts: 12.4 us -> 32.2 us  [rounded(): return values.astype(jnp.bfloat16)]
    slice x1 -> x17, local copies, waits for them, and re-layouts: 0.02 us -> 11.2 us  [the longest x10 3.91 us: home(): own, other = (half[place[0]:place[1]].reshape(shape) for half in pair)]
  transfers between devices with their start and end apart: 35 -> 19, of which waited for: 17 -> 13; matrix products, arithmetic and copies ran while one was open for 14% -> 26% of each run, Pallas kernels for 12% -> 31%
where the time goes in v2:
time: 751 us; the launch traced here: 743 us
  Pallas kernels  230 us (31%)
  waiting for transfers between devices  214 us (28%)
  local copies, waits for them, and re-layouts  130 us (17%)
  matrix products  71.3 us (9%)
  other arithmetic  38 us (5%)
  blocking collectives  25.1 us (3%)
  starting transfers between devices  18 us (2%)
  between operations  16.8 us (2%)
    pallas_call x8, Pallas kernels, plane_call(): pl.pallas_call(kernel, name=name, out_shape=outs, in_specs=[whole] * len(...  230 us
    all_gather x4, waiting for transfers between devices, gather_group(): return lax.all_gather(swapped, 'z', axis=0, tiled=True)  77.5 us
    dot_general x23, matrix products, dot(): return jnp.einsum(pattern, left, right, preferred_element_type=jnp.float32)  60.3 us
    ppermute x4, waiting for transfers between devices, swap_group(): return either(keep, lax.ppermute(give, 'x', SWAP), x, jnp.stack)  41.8 us
    ppermute x3, waiting for transfers between devices, both_items(): return either(values, lax.ppermute(values, 'x', SWAP), x, jnp.concatenate)  41.5 us
    reduce_scatter x4, waiting for transfers between devices, scatter_group(): return lax.psum_scatter(parts, 'z', scatter_dimension=0, tiled=True)  41.4 us
    unnamed x208, local copies, waits for them, and re-layouts  36.2 us
    convert_element_type x24, local copies, waits for them, and re-layouts, rounded(): return values.astype(jnp.bfloat16)  32.2 us
  transfers between devices with their start and end apart: 19, of which 13 were waited for; matrix products, arithmetic and copies ran while one was open for 26% of the time, Pallas kernels for 31%

profile of v2, /device:TPU:0, one launch (start us, length us, event | category | flops | bytes accessed | tf_op | source)
XLA Modules:
  0.0 742.5 jit_solution(14734109336902856238)
XLA Ops:
  15.0 11.8 %collective-permute-done = bf16[992,256]{1,0:T(8,128)(2,1)S(1)} collective-permute-done((bf16[992,256]{1,0:T(8,128)(2,1)}, bf16[992,256]{1,0:T(8,128)(2,1)S(1)}, u32[]{:S(2)}, u32[]{:S(2)}) %collective-permute-start) | collective-permute-done | bytes 507936 | tf_op jit(solution)/shard_map/ppermute | solution.py:355
  33.9 18.7 %collective-permute-done.1 = bf16[256,2048]{1,0:T(8,128)(2,1)S(1)} collective-permute-done((bf16[256,2048]{1,0:T(8,128)(2,1)}, bf16[256,2048]{1,0:T(8,128)(2,1)S(1)}, u32[]{:S(2)}, u32[]{:S(2)}) %collective-permute-start.1) | collective-permute-done | bytes 1048608 | tf_op jit(solution)/shard_map/ppermute | solution.py:333
  57.1 12.8 %collective-permute-done.2 = bf16[1280,256]{1,0:T(8,128)(2,1)S(1)} collective-permute-done((bf16[1280,256]{1,0:T(8,128)(2,1)}, bf16[1280,256]{1,0:T(8,128)(2,1)S(1)}, u32[]{:S(2)}, u32[]{:S(2)}) %collective-permute-start.2) | collective-permute-done | bytes 655392 | tf_op jit(solution)/shard_map/ppermute | solution.py:355
  71.1 37.1 %all-gather.6.cloned.1.call-done.refs_1_ = bf16[8,992,256]{2,1,0:T(8,128)(2,1)} async-done(((bf16[2,992,256]{2,1,0:T(8,128)(2,1)}), bf16[8,992,256]{2,1,0:T(8,128)(2,1)}) %all-gather.6.cloned.1.call-update) | async-done | bytes 4063248 | tf_op jit(solution)/shard_map/all_gather | solution.py:359
  110.5 18.6 %all-gather = s32[2,1,257]{2,1,0:T(1,128)S(1)} all-gather(s32[1,1,257]{2,1,0:T(1,128)S(1)} %add_bitcast_fusion), channel_id=1, replica_groups=mesh['z'=4,'x'=2,'mp'=4] {'x'}, dimensions={0}, use_global_device_ids=true | all-gather | bytes 3084 | tf_op jit(solution)/shard_map/all_gather | solution.py:447
  140.9 9.9 %collective-permute-done.4 = bf16[512,640]{1,0:T(8,128)(2,1)} collective-permute-done((bf16[512,640]{1,0:T(8,128)(2,1)}, bf16[512,640]{1,0:T(8,128)(2,1)}, u32[]{:S(2)}, u32[]{:S(2)}) %collective-permute-start.4) | collective-permute-done | bytes 655392 | tf_op jit(solution)/shard_map/ppermute | solution.py:355
  162.0 16.1 %gather_step.1.refs_3_ = bf16[8,512,256]{2,1,0:T(8,128)(2,1)S(1)} custom-call(bf16[512,256]{1,0:T(8,128)(2,1)S(1)} %convolution_convert_fusion.8.own), custom_call_target="tpu_custom_call" | custom-call | tf_op jit(solution)/shard_map/gather_step/pallas_call | solution.py:189
  181.4 25.6 %all-gather.8.cloned.1.call-done.refs_1_ = bf16[8,1280,256]{2,1,0:T(8,128)(2,1)} async-done(((bf16[2,1280,256]{2,1,0:T(8,128)(2,1)}), bf16[8,1280,256]{2,1,0:T(8,128)(2,1)}) %all-gather.8.cloned.1.call-update) | async-done | bytes 5242896 | tf_op jit(solution)/shard_map/all_gather | solution.py:359
  209.4 7.3 collective-permute-done.5
  229.2 32.2 %forward_step.2 = (f32[64,2048]{1,0:T(8,128)S(1)}, bf16[8,64,2048]{2,1,0:T(8,128)(2,1)S(1)}) custom-call(bf16[8,64,2048]{2,1,0:T(8,128)(2,1)S(1)} %reshape.365.part, f32[64,2048]{1,0:T(8,128)S(1)} %bitcast_convert_fusion.5.residual.values, f32[1,2048]{1,0:T(1,128)S(1)} %bitcast.357), custom_call_target="tpu_custom_call" | custom-call | tf_op jit(solution)/shard_map/forward_step/pallas_call | solution.py:189
  280.9 32.8 %forward_step.3 = (f32[64,2048]{1,0:T(8,128)S(1)}, bf16[8,64,2048]{2,1,0:T(8,128)(2,1)S(1)}) custom-call(bf16[8,64,2048]{2,1,0:T(8,128)(2,1)S(1)} %reshape.369.part, f32[64,2048]{1,0:T(8,128)S(1)} %copy-done.12, f32[1,2048]{1,0:T(1,128)S(1)} %bitcast.359), custom_call_target="tpu_custom_call" | custom-call | tf_op jit(solution)/shard_map/forward_step/pallas_call | solution.py:189
  318.5 22.7 %collective-permute-done.6 = bf16[256,2048]{1,0:T(8,128)(2,1)} collective-permute-done((bf16[256,2048]{1,0:T(8,128)(2,1)}, bf16[256,2048]{1,0:T(8,128)(2,1)}, u32[]{:S(2)}, u32[]{:S(2)}) %collective-permute-start.6) | collective-permute-done | bytes 1048608 | tf_op jit(solution)/shard_map/ppermute | solution.py:333
  345.4 7.1 fusion.16
  352.5 14.8 %all-gather.12.cloned.1.call-done.refs_1_ = bf16[8,640,256]{2,1,0:T(8,128)(2,1)} async-done(((bf16[2,640,256]{2,1,0:T(8,128)(2,1)}), bf16[8,640,256]{2,1,0:T(8,128)(2,1)}) %all-gather.12.cloned.1.call-update) | async-done | bytes 2621456 | tf_op jit(solution)/shard_map/all_gather | solution.py:359
  367.3 6.3 multiply_bitcast_fusion
  382.0 6.5 bitcast_convert_fusion.2
  402.0 33.1 %backward_step.2 = (f32[64,2048]{1,0:T(8,128)S(1)}, f32[1,2048]{1,0:T(1,128)S(1)}, bf16[8,64,2048]{2,1,0:T(8,128)(2,1)S(1)}) custom-call(bf16[8,64,2048]{2,1,0:T(8,128)(2,1)S(1)} %reshape.371.part, f32[64,2048]{1,0:T(8,128)S(1)} %get-tuple-element.26.values.residual, f32[64,2048]{1,0:T(8,128)S(1)} %copy-done.14, f32[1,2048]{1,0:T(1,128)S(1)} %bitcast.360), custom_call_target="tpu_custom_call" | custom-call | tf_op jit(solution)/shard_map/backward_step/pallas_call | solution.py:189
  467.0 32.7 %backward_step.3 = (f32[64,2048]{1,0:T(8,128)S(1)}, f32[1,2048]{1,0:T(1,128)S(1)}, bf16[8,64,2048]{2,1,0:T(8,128)(2,1)S(1)}) custom-call(bf16[8,64,2048]{2,1,0:T(8,128)(2,1)S(1)} %bitcast.350, f32[64,2048]{1,0:T(8,128)S(1)} %copy-done.13, f32[64,2048]{1,0:T(8,128)S(1)} %copy-done.18, f32[1,2048]{1,0:T(1,128)S(1)} %bitcast.358), custom_call_target="tpu_custom_call" | custom-call | tf_op jit(solution)/shard_map/backward_step/pallas_call | solution.py:189
  536.7 17.0 %scatter_step.1 = bf16[512,256]{1,0:T(8,128)(2,1)S(1)} custom-call(bf16[8,512,256]{2,1,0:T(8,128)(2,1)S(1)} %bitcast.351), custom_call_target="tpu_custom_call" | custom-call | tf_op jit(solution)/shard_map/scatter_step/pallas_call | solution.py:189
  562.1 32.4 %input_step.1 = (f32[4,64,2048]{2,1,0:T(8,128)S(1)}, f32[1,2048]{1,0:T(1,128)S(1)}) custom-call(bf16[8,64,2048]{2,1,0:T(8,128)(2,1)S(1)} %reshape.378.part, f32[64,2048]{1,0:T(8,128)S(1)} %bitcast_convert_fusion.5.residual.values, f32[64,2048]{1,0:T(8,128)S(1)} %copy-done.16, f32[1,2048]{1,0:T(1,128)S(1)} %bitcast.361), custom_call_target="tpu_custom_call" | custom-call | tf_op jit(solution)/shard_map/input_step/pallas_call | solution.py:189
  625.8 33.6 %output_step.1 = bf16[4,64,2048]{2,1,0:T(8,128)(2,1)S(1)} custom-call(bf16[8,64,2048]{2,1,0:T(8,128)(2,1)S(1)} %copy-done.2, f32[64,2048]{1,0:T(8,128)S(1)} %get-tuple-element.26.values.residual), custom_call_target="tpu_custom_call" | custom-call | tf_op jit(solution)/shard_map/output_step/pallas_call | solution.py:189
  668.1 35.1 %reduce-scatter.11.cloned.1.call-done = bf16[2,1248,256]{2,1,0:T(8,128)(2,1)} async-done(((bf16[8,1248,256]{2,1,0:T(8,128)(2,1)}), bf16[2,1248,256]{2,1,0:T(8,128)(2,1)}) %reduce-scatter.11.cloned.1.call-update) | async-done | bytes 1277968 | tf_op jit(solution)/shard_map/reduce_scatter | solution.py:363
  709.0 11.6 %collective-permute-done.7 = bf16[1248,256]{1,0:T(8,128)(2,1)S(1)} collective-permute-done((bf16[1248,256]{1,0:T(8,128)(2,1)S(1)}, bf16[1248,256]{1,0:T(8,128)(2,1)S(1)}, u32[]{:S(2)}, u32[]{:S(2)}) %collective-permute-start.7) | collective-permute-done | bytes 639008 | tf_op jit(solution)/shard_map/ppermute | solution.py:368
  721.5 6.5 psum.7
  (418 shorter events, 243.3 us)
Async XLA Ops:
  7.2 101.0 %all-gather.6.cloned.1.call-start = ((), (), s32[]{:S(2)}) async-start(), calls=%async_computation.4 | async-start | bytes 5079040 | tf_op jit(solution)/shard_map/all_gather | solution.py:359
  9.7 198.9 %copy-start.27 = (bf16[1,256,2048]{2,1,0:T(8,128)(2,1)}, bf16[1,256,2048]{2,1,0:T(8,128)(2,1)S(1)}, u32[]{:S(2)}) copy-start(bf16[1,256,2048]{2,1,0:T(8,128)(2,1)S(1)} %copy.621) | copy-start | bytes 3145732
  12.1 14.7 %collective-permute-start = (bf16[992,256]{1,0:T(8,128)(2,1)}, bf16[992,256]{1,0:T(8,128)(2,1)S(1)}, u32[]{:S(2)}, u32[]{:S(2)}) collective-permute-start(bf16[992,256]{1,0:T(8,128)(2,1)} %get-tuple-element.74), channel_id=1, source_target_pairs={{0,4},{4,0},{1,5},{5,1},{2,6},{6,2},{3,7},{7,3},{8,12},{12,8},{9,1... | collective-permute-start | bytes 1523720 | tf_op jit(solution)/shard_map/ppermute | solution.py:355
  28.0 24.6 %collective-permute-start.1 = (bf16[256,2048]{1,0:T(8,128)(2,1)}, bf16[256,2048]{1,0:T(8,128)(2,1)S(1)}, u32[]{:S(2)}, u32[]{:S(2)}) collective-permute-start(bf16[256,2048]{1,0:T(8,128)(2,1)} %after.17), channel_id=1, source_target_pairs={{0,4},{4,0},{1,5},{5,1},{2,6},{6,2},{3,7},{7,3},{8,12},{12,8},{9,1... | collective-permute-start | bytes 3145736 | tf_op jit(solution)/shard_map/ppermute | solution.py:333
  54.5 15.3 %collective-permute-start.2 = (bf16[1280,256]{1,0:T(8,128)(2,1)}, bf16[1280,256]{1,0:T(8,128)(2,1)S(1)}, u32[]{:S(2)}, u32[]{:S(2)}) collective-permute-start(bf16[1280,256]{1,0:T(8,128)(2,1)} %after.18), channel_id=1, source_target_pairs={{0,4},{4,0},{1,5},{5,1},{2,6},{6,2},{3,7},{7,3},{8,12},{12,8},{9,1... | collective-permute-start | bytes 1966088 | tf_op jit(solution)/shard_map/ppermute | solution.py:355
  71.1 37.1 %copy-start.25 = (bf16[256,1664]{1,0:T(8,128)(2,1)S(1)}, bf16[256,1664]{1,0:T(8,128)(2,1)}, u32[]{:S(2)}) copy-start(bf16[256,1664]{1,0:T(8,128)(2,1)} %after.19) | copy-start | bytes 2555908
  71.1 39.4 %copy-start.88 = (s32[1,256]{1,0:T(1,128)S(1)}, s32[1,256]{1,0:T(1,128)}, u32[]{:S(2)}) copy-start(s32[1,256]{1,0:T(1,128)} %param.17) | copy-start | bytes 3076
  71.1 135.9 %all-gather.8.cloned.1.call-start = ((), (), s32[]{:S(2)}) async-start(), calls=%async_computation.5 | async-start | bytes 6553600 | tf_op jit(solution)/shard_map/all_gather | solution.py:359
  108.2 23.4 %collective-permute-start.3 = (bf16[256,1664]{1,0:T(8,128)(2,1)S(1)}, bf16[256,1664]{1,0:T(8,128)(2,1)}, u32[]{:S(2)}, u32[]{:S(2)}) collective-permute-start(bf16[256,1664]{1,0:T(8,128)(2,1)S(1)} %copy-done.25), channel_id=1, source_target_pairs={{0,4},{4,0},{1,5},{5,1},{2,6},{6,2},{3,7},{7,3},{8,12},{12,8},{9,1... | collective-permute-start | bytes 2555912 | tf_op jit(solution)/shard_map/ppermute | solution.py:333
  134.8 16.1 %collective-permute-start.4 = (bf16[512,640]{1,0:T(8,128)(2,1)}, bf16[512,640]{1,0:T(8,128)(2,1)}, u32[]{:S(2)}, u32[]{:S(2)}) collective-permute-start(bf16[512,640]{1,0:T(8,128)(2,1)} %after.20), channel_id=1, source_target_pairs={{0,4},{4,0},{1,5},{5,1},{2,6},{6,2},{3,7},{7,3},{8,12},{12,8},{9,1... | collective-permute-start | bytes 1966088 | tf_op jit(solution)/shard_map/ppermute | solution.py:355
  153.4 161.6 %all-gather.10.cloned.1.call-start = ((), (), s32[]{:S(2)}) async-start(), calls=%async_computation.6 | async-start | bytes 6553600 | tf_op jit(solution)/shard_map/all_gather | solution.py:359
  207.0 9.7 %collective-permute-start.5 = (bf16[640,256]{1,0:T(8,128)(2,1)S(1)}, bf16[640,256]{1,0:T(8,128)(2,1)S(1)}, u32[]{:S(2)}, u32[]{:S(2)}) collective-permute-start(bf16[640,256]{1,0:T(8,128)(2,1)S(1)} %copy-done.55), channel_id=1, source_target_pairs={{0,4},{4,0},{1,5},{5,1},{2,6},{6,2},{3,7},{7,3},{8,12},{12,8},{9,1... | collective-permute-start | bytes 983048 | tf_op jit(solution)/shard_map/ppermute | solution.py:355
  219.0 148.4 %all-gather.12.cloned.1.call-start = ((), (), s32[]{:S(2)}) async-start(), calls=%async_computation.7 | async-start | bytes 3276800 | tf_op jit(solution)/shard_map/all_gather | solution.py:359
  315.0 122.2 %reduce-scatter.5.cloned.1.call-start = ((), (), s32[]{:S(2)}) async-start(), calls=%async_computation.8 | async-start | bytes 3276800 | tf_op jit(solution)/shard_map/reduce_scatter | solution.py:363
  315.3 25.8 %collective-permute-start.6 = (bf16[256,2048]{1,0:T(8,128)(2,1)}, bf16[256,2048]{1,0:T(8,128)(2,1)}, u32[]{:S(2)}, u32[]{:S(2)}) collective-permute-start(bf16[256,2048]{1,0:T(8,128)(2,1)} %after.25), channel_id=1, source_target_pairs={{0,4},{4,0},{1,5},{5,1},{2,6},{6,2},{3,7},{7,3},{8,12},{12,8},{9,1... | collective-permute-start | bytes 3145736 | tf_op jit(solution)/shard_map/ppermute | solution.py:333
  377.6 151.4 %reduce-scatter.7.cloned.1.call-start = ((), (), s32[]{:S(2)}) async-start(), calls=%async_computation.9 | async-start | bytes 6553600 | tf_op jit(solution)/shard_map/reduce_scatter | solution.py:363
  437.2 171.4 %reduce-scatter.9.cloned.1.call-start = ((), (), s32[]{:S(2)}) async-start(), calls=%async_computation.10 | async-start | bytes 5242880 | tf_op jit(solution)/shard_map/reduce_scatter | solution.py:363
  529.1 174.2 %reduce-scatter.11.cloned.1.call-start = ((), (), s32[]{:S(2)}) async-start(), calls=%async_computation.11 | async-start | bytes 6389760 | tf_op jit(solution)/shard_map/reduce_scatter | solution.py:363
  562.1 32.6 %copy-start.63 = (bf16[256,2048]{0,1:T(8,128)(2,1)S(1)}, bf16[256,2048]{0,1:T(8,128)(2,1)}, u32[]{:S(2)}) copy-start(bf16[256,2048]{0,1:T(8,128)(2,1)} %copy-done.62) | copy-start | bytes 3145732
  618.9 42.1 %collective-permute-start.10 = (bf16[640,256]{1,0:T(8,128)(2,1)}, bf16[640,256]{1,0:T(8,128)(2,1)}, u32[]{:S(2)}, u32[]{:S(2)}) collective-permute-start(bf16[640,256]{1,0:T(8,128)(2,1)} %get-tuple-element.52), channel_id=1, source_target_pairs={{0,4},{4,0},{1,5},{5,1},{2,6},{6,2},{3,7},{7,3},{8,12},{12,8},{9,1... | collective-permute-start | bytes 983048 | tf_op jit(solution)/shard_map/ppermute | solution.py:368
  622.1 41.1 %collective-permute-start.8 = (bf16[1024,256]{1,0:T(8,128)(2,1)}, bf16[1024,256]{1,0:T(8,128)(2,1)}, u32[]{:S(2)}, u32[]{:S(2)}) collective-permute-start(bf16[1024,256]{1,0:T(8,128)(2,1)} %dynamic-slice_bitcast_fusion.3), channel_id=1, source_target_pairs={{0,4},{4,0},{1,5},{5,1},{2,6},{6,2},{3,7},{7,3},{8,12},{12,8},{9,1... | collective-permute-start | bytes 1572872 | tf_op jit(solution)/shard_map/ppermute | solution.py:368
  625.8 35.1 %copy-start.28 = (bf16[2,1024,256]{2,1,0:T(8,128)(2,1)S(1)}, bf16[2,1024,256]{2,1,0:T(8,128)(2,1)}, u32[]{:S(2)}) copy-start(bf16[2,1024,256]{2,1,0:T(8,128)(2,1)} %after.31) | copy-start | bytes 3145732
  659.3 46.6 %collective-permute-start.9 = (bf16[512,640]{1,0:T(8,128)(2,1)S(1)}, bf16[512,640]{1,0:T(8,128)(2,1)}, u32[]{:S(2)}, u32[]{:S(2)}) collective-permute-start(bf16[512,640]{1,0:T(8,128)(2,1)S(1)} %get-tuple-element.41), channel_id=1, source_target_pairs={{0,4},{4,0},{1,5},{5,1},{2,6},{6,2},{3,7},{7,3},{8,12},{12,8},{9,1... | collective-permute-start | bytes 1966088 | tf_op jit(solution)/shard_map/ppermute | solution.py:368
  704.4 16.2 %collective-permute-start.7 = (bf16[1248,256]{1,0:T(8,128)(2,1)S(1)}, bf16[1248,256]{1,0:T(8,128)(2,1)S(1)}, u32[]{:S(2)}, u32[]{:S(2)}) collective-permute-start(bf16[1248,256]{1,0:T(8,128)(2,1)S(1)} %dynamic-slice_bitcast_fusion.2), channel_id=1, source_target_pairs={{0,4},{4,0},{1,5},{5,1},{2,6},{6,2},{3,7},{7,3},{8,12},{12,8},{9,1... | collective-permute-start | bytes 1916936 | tf_op jit(solution)/shard_map/ppermute | solution.py:368
  (87 other events, 492.8 us)
Sparse Core Ops, SparseCore 0:
  28.1 80.0 all-gather.5
  110.3 96.6 all-gather.7
  209.1 96.4 all-gather.9
  315.2 52.1 all-gather.11
  377.7 50.8 reduce-scatter.4
  437.4 91.6 reduce-scatter.6
  531.3 77.2 reduce-scatter.8
  611.1 92.1 reduce-scatter.10

commit v3 on v2

--- a/solution.py
+++ b/solution.py
@@ -35,13 +35,17 @@
     def block(self, dx, dy, dc):
         return (flip(self.x, dx) * 2 + flip(self.y, dy)) * 2 + flip(self.c, dc)
 
-    def greet(self, relations):
+    def greet(self, relations, line=None):
         barrier = pltpu.get_barrier_semaphore()
         for relation in relations:
             pl.semaphore_signal(
                 barrier, inc=1, device_id=self.device(*relation), device_id_type=pl.DeviceIdType.MESH
             )
-        pl.semaphore_wait(barrier, len(relations))
+        if line is None:
+            pl.semaphore_wait(barrier, len(relations))
+        else:
+            line.greet(barrier)
+            pl.semaphore_wait(barrier, len(relations) + line.partners)
 
     def send(self, src, dst, sems, slot, relation):
         copy = pltpu.make_async_remote_copy(
@@ -54,6 +58,72 @@
         )
         copy.start()
         return copy
+
+
+class Line:
+    def __init__(self, count, at, sems):
+        self.z = lax.axis_index("z")
+        self.count, self.at, self.sems = count, at, sems
+        self.partners = (self.z > 0).astype(jnp.int32) + (self.z < self.count - 1).astype(jnp.int32)
+
+    def greet(self, barrier):
+        for there, step in ((self.z > 0, -1), (self.z < self.count - 1, 1)):
+
+            @pl.when(there)
+            def signal(step=step):
+                pl.semaphore_signal(
+                    barrier,
+                    inc=1,
+                    device_id={"z": self.z + step},
+                    device_id_type=pl.DeviceIdType.MESH,
+                )
+
+    def copy(self, block, step, way):
+        at = self.at(jnp.clip(block, 0, self.count - 1))
+        return pltpu.make_async_remote_copy(
+            src_ref=at,
+            dst_ref=at,
+            send_sem=self.sems.at[0, way, step],
+            recv_sem=self.sems.at[1, way, step],
+            device_id={"z": jnp.clip(self.z + (1 - 2 * way), 0, self.count - 1)},
+            device_id_type=pl.DeviceIdType.MESH,
+        )
+
+    def sent(self, step, way):
+        block = self.z - step * (1 - 2 * way)
+        last = self.count - 1
+        goes = (self.z < last) & (block >= 0) if way == 0 else (self.z > 0) & (block <= last)
+        return block, goes
+
+    def start(self, step):
+        for way in (0, 1):
+            block, goes = self.sent(step, way)
+
+            @pl.when(goes)
+            def begin(block=block, way=way):
+                self.copy(block, step, way).start()
+
+    def arrive(self, step):
+        for way in (0, 1):
+            block = self.z - (step + 1) * (1 - 2 * way)
+
+            @pl.when((block >= 0) & (block < self.count))
+            def wait(block=block, way=way):
+                self.copy(block, step, way).wait_recv()
+
+    def onward(self, step):
+        self.arrive(step)
+        if step + 1 < self.count - 1:
+            self.start(step + 1)
+
+    def finish(self):
+        for step in range(self.count - 1):
+            for way in (0, 1):
+                block, goes = self.sent(step, way)
+
+                @pl.when(goes)
+                def wait(block=block, way=way, step=step):
+                    self.copy(block, step, way).wait_send()
 
 
 ALL_RELATIONS = ((0, 0, 1), (1, 1, 0), (1, 0, 0), (0, 1, 0))
@@ -161,6 +231,31 @@
     gain_part[...] = gain_sum
     out[plane.y * 2 + plane.c] = grad[...] + side
     gather_rows(plane, out, sems, 7)
+
+
+def weights_kernel(count, others, keep, give, *refs):
+    sources, out, received = refs[:others], refs[others], refs[others + 1 : 2 * others + 1]
+    swap_sems, own_sems, other_sems = refs[2 * others + 1 :]
+    plane = Plane()
+    own = Line(count, lambda block: out.at[block, plane.x], own_sems)
+    other = Line(count, lambda block: out.at[block, 1 - plane.x], other_sems)
+    plane.greet(((1, 0, 0),), own)
+    swap = plane.send(give, out.at[own.z, plane.x], swap_sems, 0, (1, 0, 0))
+    out[own.z, plane.x] = keep[...]
+    own.start(0)
+    swaps = [
+        plane.send(sources[i], received[i], swap_sems, 1 + i, (1, 0, 0)) for i in range(others)
+    ]
+    swap.wait_recv()
+    other.start(0)
+    for step in range(count - 1):
+        own.onward(step)
+        other.onward(step)
+    for copy in swaps:
+        copy.wait()
+    swap.wait_send()
+    own.finish()
+    other.finish()
 
 
 def gather_kernel(own, out, sems):
@@ -237,6 +332,28 @@
     )
 
 
+def weights_step(keep, give, sources, planes):
+    anywhere = pl.BlockSpec(memory_space=pl.ANY)
+    whole = pl.BlockSpec(memory_space=pltpu.VMEM)
+    outs = [full((planes, 2) + keep.shape, keep.dtype)]
+    outs += [full(source.shape, source.dtype) for source in sources]
+    return pl.pallas_call(
+        functools.partial(weights_kernel, planes, len(sources)),
+        name="weights_step",
+        out_shape=outs,
+        in_specs=[whole, whole] + [anywhere] * len(sources),
+        out_specs=[whole] + [anywhere] * len(sources),
+        scratch_shapes=[
+            pltpu.SemaphoreType.DMA((2, 1 + len(sources))),
+            pltpu.SemaphoreType.DMA((2, 2, planes - 1)),
+            pltpu.SemaphoreType.DMA((2, 2, planes - 1)),
+        ],
+        compiler_params=pltpu.CompilerParams(
+            collective_id=6, has_side_effects=True, vmem_limit_bytes=VMEM_LIMIT
+        ),
+    )(keep, give, *sources)
+
+
 def gather_step(own):
     rows, columns = own.shape
     return plane_call(
@@ -329,10 +446,6 @@
     return jnp.where(x == 0, join([own, other]), join([other, own]))
 
 
-def both_items(values, x):
-    return either(values, lax.ppermute(values, "x", SWAP), x, jnp.concatenate)
-
-
 def cut_in(weight, x):
     flat = weight.reshape(-1, weight.shape[-1])
     size = flat.shape[1] // 2
@@ -345,14 +458,6 @@
         lax.dynamic_slice_in_dim(weight, k * size, size, 0).reshape(-1, columns)
         for k in (x, 1 - x)
     ]
-
-
-def swap_group(pairs, x, *earlier):
-    keep = jnp.concatenate([pair[0] for pair in pairs])
-    give = jnp.concatenate([pair[1] for pair in pairs])
-    if earlier:
-        give = after(give, *earlier)
-    return either(keep, lax.ppermute(give, "x", SWAP), x, jnp.stack)
 
 
 def gather_group(swapped):
@@ -412,26 +517,32 @@
     def unpadded(values):
         return values.reshape(-1, 16 * heads)[:, : 3 * depth].reshape(-1, 3, depth)
 
-    first = swap_group(
-        [cut_in(patch_proj, x), cut_in(self_qkv, x), [padded(norm_gains)[0]] * 2], x
-    )
-    first_w = gather_group(first)
-    token_all = both_items(after(tokens[0], first), x)
-    second = swap_group(
-        [
-            cut_in(cross_kv, x),
-            cut_in(cross_q, x),
-            cut_out(self_out, x, heads),
-            cut_out(cross_out, x, heads),
-        ],
-        x,
-        token_all,
-    )
-    second_w = gather_group(after(second, first_w))
-    patch_all = both_items(after(patches[0], second), x)
-    third = swap_group([cut_in(ffn_in, x)], x, patch_all)
-    fourth = swap_group([cut_out(ffn_out, x, depth)], x, third)
-    grad_all = both_items(after(cotangent[0], fourth), x)
+    early = [
+        cut_in(patch_proj, x),
+        cut_in(self_qkv, x),
+        [padded(norm_gains)[0]] * 2,
+        cut_in(cross_kv, x),
+        cut_in(cross_q, x),
+        cut_out(self_out, x, heads),
+        cut_out(cross_out, x, heads),
+    ]
+    keep, give = (jnp.concatenate([pair[k] for pair in early]) for k in (0, 1))
+    third, fourth = cut_in(ffn_in, x), cut_out(ffn_out, x, depth)
+    facts = jnp.concatenate([patch_keep, lengths[:, None]], axis=1)
+    facts = jnp.pad(facts, ((0, 7), (0, 127)))
+    sources = (third[1], tokens[0], patches[0], fourth[1], cotangent[0], facts)
+    early_w, third_other, token_other, patch_other, fourth_other, grad_other, facts_other = (
+        weights_step(keep, give, sources, blocks // 2)
+    )
+    third = either(third[0], third_other, x, jnp.stack)
+    fourth = either(fourth[0], fourth_other, x, jnp.stack)
+    token_all = either(tokens[0], token_other, x, jnp.concatenate)
+    patch_all = either(patches[0], patch_other, x, jnp.concatenate)
+    grad_all = either(cotangent[0], grad_other, x, jnp.concatenate)
+    third_w = gather_group(third)
+    early_w = early_w.reshape(blocks, *keep.shape)
+    split = at_gain[1]
+    first_w, second_w = early_w[:, :split], early_w[:, split:]
 
     patch_w = first_w[:, at_patch[0] : at_patch[1]].reshape(-1, heads)
     qkv_w = first_w[:, at_qkv[0] : at_qkv[1]].reshape(blocks, 3, depth, heads)
@@ -443,9 +554,9 @@
     gains = unpadded(first_w[:, at_gain[0] : at_gain[1]])
     gains = gains.transpose(1, 0, 2).reshape(3, width).astype(jnp.float32)
     gain_of = [gains[i : i + 1] for i in range(3)]
-    facts = jnp.concatenate([patch_keep, lengths[:, None]], axis=1)
-    facts = lax.all_gather(facts, "x", axis=0, tiled=True)
-    patch_keep, lengths = facts[:, :-1], facts[:, -1]
+    facts = either(facts[:1], facts_other[:1], x, jnp.concatenate)
+    length_at = patch_keep.shape[1]
+    patch_keep, lengths = facts[:, :length_at], facts[:, length_at]
 
     row_index = lax.broadcasted_iota(jnp.int32, (slots, slots), 0)
     col_index = lax.broadcasted_iota(jnp.int32, (slots, slots), 1)
@@ -484,7 +595,6 @@
         .transpose(2, 1, 0, 3)
         .reshape(memory_part.shape[0], -1)
     )
-    third_w = gather_group(after(third, second_w, mixed_self, memory_blocks))
     ffn_in_w = third_w.reshape(blocks, 2, depth, units)
 
     part = dot("sk,bkd->sbd", mixed_self, self_out_w)
@@ -493,12 +603,12 @@
 
     key_value = rounded(dot("pbd,bcdf->cpf", cut(memory), cross_kv_w))
     query_heads = split_heads(rounded(dot("sd,df->sf", normed_cross, cross_q_w)))
+    fourth_w = gather_group(after(fourth, third_w, normed_cross, key_value))
     cross_keys = split_heads(key_value[0])
     cross_values = split_heads(key_value[1])
     mixed_cross, total_cross = attend(query_heads, cross_keys, cross_values, cross_allowed)
     part = dot("sk,bkd->sbd", mixed_cross, cross_out_w)
     after_cross, normed_ffn = forward_step(to_blocks(part), after_self, gain_of[2])
-    fourth_w = gather_group(after(fourth, third_w, normed_ffn))
     ffn_out_w = fourth_w.reshape(blocks, units, depth)
     normed_ffn = from_blocks(normed_ffn)
 

time: 751 us -> 727 us (0.968)
  Pallas kernels: 230 us -> 390 us
  waiting for transfers between devices: 214 us -> 59.2 us
  blocking collectives: 25.1 us -> 6.34 us
  starting transfers between devices: 18 us -> 6.21 us
  other arithmetic: 38 us -> 28.5 us
  matrix products: 71.3 us -> 79.8 us
    pallas_call x0 -> x1, Pallas kernels: none -> 162 us  [weights_step(): pl.pallas_call(functools.partial(weights_kernel, planes, len(sources)), n...]
    ppermute x7 -> x0, waiting for transfers between devices: 83.2 us -> none  [the longest x4 41.8 us: swap_group(): return either(keep, lax.ppermute(give, 'x', SWAP), x, jnp.stack)]
    all_gather x4 -> x2, waiting for transfers between devices: 77.5 us -> 6.66 us  [gather_group(): return lax.all_gather(swapped, 'z', axis=0, tiled=True)]
    all_gather x1 -> x0, blocking collectives: 18.6 us -> none  [on_device(): facts = lax.all_gather(facts, 'x', axis=0, tiled=True)]
    ppermute x7 -> x0, starting transfers between devices: 11.6 us -> none  [the longest x4 7.37 us: swap_group(): return either(keep, lax.ppermute(give, 'x', SWAP), x, jnp.stack)]
    select_n x5 -> x3, other arithmetic: 10.4 us -> 2.29 us  [either(): return jnp.where(x == 0, join([own, other]), join([other, own]))]
    convert_element_type x24 -> x23, local copies, waits for them, and re-layouts: 32.2 us -> 29.6 us  [rounded(): return values.astype(jnp.bfloat16)]
    unnamed x208 -> x193, local copies, waits for them, and re-layouts: 36.2 us -> 35.4 us
  transfers between devices with their start and end apart: 19 -> 10, of which waited for: 13 -> 5; matrix products, arithmetic and copies ran while one was open for 26% -> 26% of each run, Pallas kernels for 31% -> 32%
where the time goes in v3:
time: 727 us; the launch traced here: 715 us
  Pallas kernels  390 us (54%)
  local copies, waits for them, and re-layouts  129 us (18%)
  matrix products  79.8 us (11%)
  waiting for transfers between devices  59.2 us (8%)
  other arithmetic  28.5 us (4%)
  between operations  16.6 us (2%)
    pallas_call x8, Pallas kernels, plane_call(): pl.pallas_call(kernel, name=name, out_shape=outs, in_specs=[whole] * len(...  228 us
    pallas_call x1, Pallas kernels, weights_step(): pl.pallas_call(functools.partial(weights_kernel, planes, len(sources)), n...  162 us
    dot_general x23, matrix products, dot(): return jnp.einsum(pattern, left, right, preferred_element_type=jnp.float32)  67.3 us
    reduce_scatter x4, waiting for transfers between devices, scatter_group(): return lax.psum_scatter(parts, 'z', scatter_dimension=0, tiled=True)  39.6 us
    unnamed x193, local copies, waits for them, and re-layouts  35.4 us
    convert_element_type x23, local copies, waits for them, and re-layouts, rounded(): return values.astype(jnp.bfloat16)  29.6 us
  transfers between devices with their start and end apart: 10, of which 5 were waited for; matrix products, arithmetic and copies ran while one was open for 26% of the time, Pallas kernels for 32%

profile of v3, /device:TPU:0, one launch (start us, length us, event | category | flops | bytes accessed | tf_op | source)
XLA Modules:
  0.0 715.5 jit_solution(9369869466234386027)
XLA Ops:
  15.2 161.6 %weights_step.1 = (bf16[4,2,2272,256]{3,2,1,0:T(8,128)(2,1)}, bf16[512,640]{1,0:T(8,128)(2,1)S(1)}, bf16[256,2048]{1,0:T(8,128)(2,1)S(1)}, bf16[256,1664]{1,0:T(...) custom-call(bf16[2272,256]{1,0:T(8,128)(2,1)} %copy-done.54, ...), custom_call_target="tpu_custom_call" | custom-call | tf_op jit(solution)/shard_map/weights_step/pallas_call | solution.py:340
  184.5 3.2 slice.190
  187.7 3.9 slice.194
  195.6 16.2 %gather_step.1 = bf16[8,512,256]{2,1,0:T(8,128)(2,1)S(1)} custom-call(bf16[512,256]{1,0:T(8,128)(2,1)S(1)} %fusion.84.own), custom_call_target="tpu_custom_call" | custom-call | tf_op jit(solution)/shard_map/gather_step/pallas_call | solution.py:284
  216.7 3.8 fusion.64
  233.6 32.1 %forward_step.2 = (f32[64,2048]{1,0:T(8,128)S(1)}, bf16[8,64,2048]{2,1,0:T(8,128)(2,1)S(1)}) custom-call(bf16[8,64,2048]{2,1,0:T(8,128)(2,1)S(1)} %reshape.375.part, f32[64,2048]{1,0:T(8,128)S(1)} %get-tuple-element.96.residual.values, f32[1,2048]{1,0:T(1,128)S(1)} %bitcast.353), custom_call_target="tpu_custom_call" | custom-call | tf_op jit(solution)/shard_map/forward_step/pallas_call | solution.py:284
  270.8 6.7 all-gather.3.cloned.1.call-done.refs_1_
  299.5 3.1 reshape.379.part
  303.7 32.9 %forward_step.3 = (f32[64,2048]{1,0:T(8,128)S(1)}, bf16[8,64,2048]{2,1,0:T(8,128)(2,1)S(1)}) custom-call(bf16[8,64,2048]{2,1,0:T(8,128)(2,1)S(1)} %reshape.379.part, f32[64,2048]{1,0:T(8,128)S(1)} %copy-done.11, f32[1,2048]{1,0:T(1,128)S(1)} %bitcast.355), custom_call_target="tpu_custom_call" | custom-call | tf_op jit(solution)/shard_map/forward_step/pallas_call | solution.py:284
  337.3 6.9 fusion.16
  344.2 7.7 %multiply_bitcast_fusion = (f32[1,512,640]{1,2,0:T(8,128)}, f32[1,512,640]{1,2,0:T(8,128)}, bf16[512,640,1]{0,1,2:T(8,128)(2,1)S(1)}) fusion(f32[2,512,640]{1,2,0:T(8,128)} %fusion.16, bf16[8,640,256]{2,1,0:T(8,128)(2,1)} %all-gather.5.cloned.1.call-done.refs_1_, bf16[256,8,256]{0,2,1:T(8,128)(2,1)} %bitcast.403, bf16[256,8,256]{0,2,1:T(8,128)(2,1)} %bitcast.401, ...), kind=kOutput, calls=%fused_computation.89 | convolution fusion | flops 1359478784 | bytes 10616833 | tf_op jit(solution)/shard_map/sbd,bfd->sf/dot_general | solution.py:423
  352.8 3.1 convert_bitcast_fusion.2.refs_0_
  355.9 3.1 copy.360
  359.0 6.4 bitcast_convert_fusion.2
  370.8 5.3 convert_bitcast_fusion
  379.0 33.0 %backward_step.2 = (f32[64,2048]{1,0:T(8,128)S(1)}, f32[1,2048]{1,0:T(1,128)S(1)}, bf16[8,64,2048]{2,1,0:T(8,128)(2,1)S(1)}) custom-call(bf16[8,64,2048]{2,1,0:T(8,128)(2,1)S(1)} %reshape.381.part, f32[64,2048]{1,0:T(8,128)S(1)} %get-tuple-element.40.values.residual, f32[64,2048]{1,0:T(8,128)S(1)} %copy-done.13, f32[1,2048]{1,0:T(1,128)S(1)} %bitcast.356), custom_call_target="tpu_custom_call" | custom-call | tf_op jit(solution)/shard_map/backward_step/pallas_call | solution.py:284
  444.7 32.3 %backward_step.3 = (f32[64,2048]{1,0:T(8,128)S(1)}, f32[1,2048]{1,0:T(1,128)S(1)}, bf16[8,64,2048]{2,1,0:T(8,128)(2,1)S(1)}) custom-call(bf16[8,64,2048]{2,1,0:T(8,128)(2,1)S(1)} %bitcast.340, f32[64,2048]{1,0:T(8,128)S(1)} %copy-done.12, f32[64,2048]{1,0:T(8,128)S(1)} %copy-done.22, f32[1,2048]{1,0:T(1,128)S(1)} %bitcast.354), custom_call_target="tpu_custom_call" | custom-call | tf_op jit(solution)/shard_map/backward_step/pallas_call | solution.py:284
  513.0 17.0 %scatter_step.1 = bf16[512,256]{1,0:T(8,128)(2,1)S(1)} custom-call(bf16[8,512,256]{2,1,0:T(8,128)(2,1)S(1)} %bitcast.342), custom_call_target="tpu_custom_call" | custom-call | tf_op jit(solution)/shard_map/scatter_step/pallas_call | solution.py:284
  538.4 32.5 %input_step.1 = (f32[4,64,2048]{2,1,0:T(8,128)S(1)}, f32[1,2048]{1,0:T(1,128)S(1)}) custom-call(bf16[8,64,2048]{2,1,0:T(8,128)(2,1)S(1)} %reshape.388.part, f32[64,2048]{1,0:T(8,128)S(1)} %get-tuple-element.96.residual.values, f32[64,2048]{1,0:T(8,128)S(1)} %copy-done.20, f32[1,2048]{1,0:T(1,128)S(1)} %bitcast.357), custom_call_target="tpu_custom_call" | custom-call | tf_op jit(solution)/shard_map/input_step/pallas_call | solution.py:284
  576.8 6.0 pad_maximum_fusion.refs_0_
  602.2 32.2 %output_step.1 = bf16[4,64,2048]{2,1,0:T(8,128)(2,1)S(1)} custom-call(bf16[8,64,2048]{2,1,0:T(8,128)(2,1)S(1)} %copy-done, f32[64,2048]{1,0:T(8,128)S(1)} %get-tuple-element.40.values.residual), custom_call_target="tpu_custom_call" | custom-call | tf_op jit(solution)/shard_map/output_step/pallas_call | solution.py:284
  643.3 35.9 %reduce-scatter.11.cloned.1.call-done = bf16[2,1248,256]{2,1,0:T(8,128)(2,1)} async-done(((bf16[8,1248,256]{2,1,0:T(8,128)(2,1)}), bf16[2,1248,256]{2,1,0:T(8,128)(2,1)}) %reduce-scatter.11.cloned.1.call-update) | async-done | bytes 1277968 | tf_op jit(solution)/shard_map/reduce_scatter | solution.py:468
  683.7 12.9 %collective-permute-done = bf16[1248,256]{1,0:T(8,128)(2,1)S(1)} collective-permute-done((bf16[1248,256]{1,0:T(8,128)(2,1)S(1)}, bf16[1248,256]{1,0:T(8,128)(2,1)S(1)}, u32[]{:S(2)}, u32[]{:S(2)}) %collective-permute-start) | collective-permute-done | bytes 639008 | tf_op jit(solution)/shard_map/ppermute | solution.py:473
  696.6 6.3 psum.7
  (367 shorter events, 195.0 us)
Async XLA Ops:
  7.2 270.3 %all-gather.3.cloned.1.call-start = ((), (), s32[]{:S(2)}) async-start(), calls=%async_computation.4 | async-start | bytes 6553600 | tf_op jit(solution)/shard_map/all_gather | solution.py:464
  15.2 163.5 %copy-start.33 = (bf16[1,512,640]{2,1,0:T(8,128)(2,1)S(1)}, bf16[1,512,640]{2,1,0:T(8,128)(2,1)}, u32[]{:S(2)}) copy-start(bf16[1,512,640]{2,1,0:T(8,128)(2,1)} %get-tuple-element.54) | copy-start | bytes 1966084
  180.1 164.1 %all-gather.5.cloned.1.call-start = ((), (), s32[]{:S(2)}) async-start(), calls=%async_computation.5 | async-start | bytes 3276800 | tf_op jit(solution)/shard_map/all_gather | solution.py:464
  231.5 36.3 %copy-start.56 = (bf16[1,640,256]{2,1,0:T(8,128)(2,1)S(1)}, bf16[1,640,256]{2,1,0:T(8,128)(2,1)}, u32[]{:S(2)}) copy-start(bf16[1,640,256]{2,1,0:T(8,128)(2,1)} %get-tuple-element.65) | copy-start | bytes 983044
  231.5 37.2 %copy-start.45 = (bf16[512,4,2,256]{0,3,2,1:T(8,128)(2,1)S(1)}, bf16[512,4,2,256]{0,3,2,1:T(8,128)(2,1)}, u32[]{:S(2)}) copy-start(bf16[512,4,2,256]{0,3,2,1:T(8,128)(2,1)} %copy.278) | copy-start | bytes 6291460
  233.6 35.1 %copy-start.44 = (bf16[8,512,256]{2,1,0:T(8,128)(2,1)S(1)}, bf16[8,512,256]{2,1,0:T(8,128)(2,1)}, u32[]{:S(2)}) copy-start(bf16[8,512,256]{2,1,0:T(8,128)(2,1)} %slice.190) | copy-start | bytes 6291460
  277.5 136.5 %reduce-scatter.5.cloned.1.call-start = ((), (), s32[]{:S(2)}) async-start(), calls=%async_computation.6 | async-start | bytes 3276800 | tf_op jit(solution)/shard_map/reduce_scatter | solution.py:468
  344.2 8.6 %copy-start.64 = (bf16[1,256,2048]{1,2,0:T(8,128)(2,1)S(1)}, bf16[1,256,2048]{1,2,0:T(8,128)(2,1)}, u32[]{:S(2)}) copy-start(bf16[1,256,2048]{1,2,0:T(8,128)(2,1)} %copy.424) | copy-start | bytes 3145732
  344.2 8.6 %copy-start.65 = (bf16[256,2048]{0,1:T(8,128)(2,1)S(1)}, bf16[256,2048]{0,1:T(8,128)(2,1)}, u32[]{:S(2)}) copy-start(bf16[256,2048]{0,1:T(8,128)(2,1)} %copy.425) | copy-start | bytes 3145732
  355.9 149.4 %reduce-scatter.7.cloned.1.call-start = ((), (), s32[]{:S(2)}) async-start(), calls=%async_computation.7 | async-start | bytes 6553600 | tf_op jit(solution)/shard_map/reduce_scatter | solution.py:468
  414.1 170.6 %reduce-scatter.9.cloned.1.call-start = ((), (), s32[]{:S(2)}) async-start(), calls=%async_computation.8 | async-start | bytes 5242880 | tf_op jit(solution)/shard_map/reduce_scatter | solution.py:468
  421.1 6.9 copy-start.24
  505.3 173.9 %reduce-scatter.11.cloned.1.call-start = ((), (), s32[]{:S(2)}) async-start(), calls=%async_computation.9 | async-start | bytes 6389760 | tf_op jit(solution)/shard_map/reduce_scatter | solution.py:468
  512.9 17.2 %copy-start.31 = (bf16[8,768,256]{2,1,0:T(8,128)(2,1)S(1)}, bf16[8,768,256]{2,1,0:T(8,128)(2,1)}, u32[]{:S(2)}) copy-start(bf16[8,768,256]{2,1,0:T(8,128)(2,1)} %slice.194) | copy-start | bytes 9437188
  513.0 17.1 %copy-start.51 = (bf16[3,512,256]{2,1,0:T(8,128)(2,1)S(1)}, bf16[3,512,256]{2,1,0:T(8,128)(2,1)}, u32[]{:S(2)}) copy-start(bf16[3,512,256]{2,1,0:T(8,128)(2,1)} %copy-done.50) | copy-start | bytes 2359300
  538.4 32.6 %copy-start.52 = (bf16[3,512,256]{2,1,0:T(8,128)(2,1)S(1)}, bf16[3,512,256]{2,1,0:T(8,128)(2,1)}, u32[]{:S(2)}) copy-start(bf16[3,512,256]{2,1,0:T(8,128)(2,1)} %copy-done.50) | copy-start | bytes 2359300
  538.4 32.6 %copy-start.61 = (bf16[1,256,2048]{1,2,0:T(8,128)(2,1)S(1)}, bf16[1,256,2048]{1,2,0:T(8,128)(2,1)}, u32[]{:S(2)}) copy-start(bf16[1,256,2048]{1,2,0:T(8,128)(2,1)} %copy.418) | copy-start | bytes 3145732
  538.4 32.6 %copy-start.63 = (bf16[256,2048]{0,1:T(8,128)(2,1)S(1)}, bf16[256,2048]{0,1:T(8,128)(2,1)}, u32[]{:S(2)}) copy-start(bf16[256,2048]{0,1:T(8,128)(2,1)} %copy.419) | copy-start | bytes 3145732
  594.2 41.9 %collective-permute-start.3 = (bf16[640,256]{1,0:T(8,128)(2,1)S(1)}, bf16[640,256]{1,0:T(8,128)(2,1)}, u32[]{:S(2)}, u32[]{:S(2)}) collective-permute-start(bf16[640,256]{1,0:T(8,128)(2,1)S(1)} %get-tuple-element.64), channel_id=1, source_target_pairs={{0,4},{4,0},{1,5},{5,1},{2,6},{6,2},{3,7},{7,3},{8,12},{12,8},{9,1... | collective-permute-start | bytes 983048 | tf_op jit(solution)/shard_map/ppermute | solution.py:473
  597.5 40.8 %collective-permute-start.1 = (bf16[1024,256]{1,0:T(8,128)(2,1)}, bf16[1024,256]{1,0:T(8,128)(2,1)}, u32[]{:S(2)}, u32[]{:S(2)}) collective-permute-start(bf16[1024,256]{1,0:T(8,128)(2,1)} %dynamic-slice_bitcast_fusion.3), channel_id=1, source_target_pairs={{0,4},{4,0},{1,5},{5,1},{2,6},{6,2},{3,7},{7,3},{8,12},{12,8},{9,1... | collective-permute-start | bytes 1572872 | tf_op jit(solution)/shard_map/ppermute | solution.py:473
  602.2 33.8 %copy-start.27 = (bf16[2,1024,256]{2,1,0:T(8,128)(2,1)S(1)}, bf16[2,1024,256]{2,1,0:T(8,128)(2,1)}, u32[]{:S(2)}) copy-start(bf16[2,1024,256]{2,1,0:T(8,128)(2,1)} %after.15) | copy-start | bytes 3145732
  634.4 47.4 %collective-permute-start.2 = (bf16[512,640]{1,0:T(8,128)(2,1)}, bf16[512,640]{1,0:T(8,128)(2,1)S(1)}, u32[]{:S(2)}, u32[]{:S(2)}) collective-permute-start(bf16[512,640]{1,0:T(8,128)(2,1)} %get-tuple-element.53), channel_id=1, source_target_pairs={{0,4},{4,0},{1,5},{5,1},{2,6},{6,2},{3,7},{7,3},{8,12},{12,8},{9,1... | collective-permute-start | bytes 1966088 | tf_op jit(solution)/shard_map/ppermute | solution.py:473
  640.3 41.5 %copy-start.34 = (bf16[1,512,640]{2,1,0:T(8,128)(2,1)S(1)}, bf16[1,512,640]{2,1,0:T(8,128)(2,1)}, u32[]{:S(2)}) copy-start(bf16[1,512,640]{2,1,0:T(8,128)(2,1)} %get-tuple-element.52) | copy-start | bytes 1966084
  680.3 16.2 %collective-permute-start = (bf16[1248,256]{1,0:T(8,128)(2,1)S(1)}, bf16[1248,256]{1,0:T(8,128)(2,1)S(1)}, u32[]{:S(2)}, u32[]{:S(2)}) collective-permute-start(bf16[1248,256]{1,0:T(8,128)(2,1)S(1)} %dynamic-slice_bitcast_fusion.2), channel_id=1, source_target_pairs={{0,4},{4,0},{1,5},{5,1},{2,6},{6,2},{3,7},{7,3},{8,12},{12,8},{9,1... | collective-permute-start | bytes 1916936 | tf_op jit(solution)/shard_map/ppermute | solution.py:473
  (68 other events, 144.6 us)
Sparse Core Ops, SparseCore 0:
  180.2 97.2 all-gather.2
  279.1 53.1 all-gather.4
  356.0 49.4 reduce-scatter.4
  414.2 90.9 reduce-scatter.6
  507.4 77.2 reduce-scatter.8
  587.0 92.1 reduce-scatter.10

commit v4 on v3

--- a/solution.py
+++ b/solution.py
@@ -223,39 +223,66 @@
     gather_rows(plane, out, sems, 7)
 
 
-def input_kernel(part, values, grad, gain, out, gain_part, from_core, to_chip, from_chip, sems):
+def input_kernel(
+    part, values, grad, gain, gains_before, out, gains_sum,
+    from_core, to_chip, from_chip, sems, sums, beside,
+):
     plane = Plane()
     plane.greet(ALL_RELATIONS)
     total = reduce_blocks(plane, part, from_core, to_chip, from_chip, sems)
     side, gain_sum = back_values(values[...], gain[...], total)
-    gain_part[...] = gain_sum
     out[plane.y * 2 + plane.c] = grad[...] + side
+    sums[0] = gains_before[...]
+    sums[0, 0:1] = gain_sum
+    pair = plane.send(sums.at[0], beside.at[0], sems, 10, (0, 0, 1))
+    pair.wait_recv()
+    sums[1] = sums[0] + beside[0]
+    across = plane.send(sums.at[1], beside.at[1], sems, 11, (0, 1, 0))
     gather_rows(plane, out, sems, 7)
-
-
-def weights_kernel(count, others, keep, give, *refs):
-    sources, out, received = refs[:others], refs[others], refs[others + 1 : 2 * others + 1]
-    swap_sems, own_sems, other_sems = refs[2 * others + 1 :]
+    across.wait_recv()
+    gains_sum[...] = sums[1] + beside[1]
+    pair.wait_send()
+    across.wait_send()
+
+
+def weights_kernel(count, groups, others, *refs):
+    keeps, gives, sources = refs[:groups], refs[groups : 2 * groups], refs[2 * groups :][:others]
+    outs, received = refs[2 * groups + others :][:groups], refs[3 * groups + others :][:others]
+    swap_sems, line_sems = refs[3 * groups + 2 * others :]
     plane = Plane()
-    own = Line(count, lambda block: out.at[block, plane.x], own_sems)
-    other = Line(count, lambda block: out.at[block, 1 - plane.x], other_sems)
-    plane.greet(((1, 0, 0),), own)
-    swap = plane.send(give, out.at[own.z, plane.x], swap_sems, 0, (1, 0, 0))
-    out[own.z, plane.x] = keep[...]
-    own.start(0)
+
+    def line(i, side):
+        at = flip(plane.x, side)
+        return Line(count, lambda block: outs[i].at[block, at], line_sems.at[i, side])
+
+    lines = [[line(i, 0), line(i, 1)] for i in range(groups)]
+    here = lines[0][0].z
+    plane.greet(((1, 0, 0),), lines[0][0])
     swaps = [
-        plane.send(sources[i], received[i], swap_sems, 1 + i, (1, 0, 0)) for i in range(others)
+        plane.send(gives[i], outs[i].at[here, plane.x], swap_sems, i, (1, 0, 0))
+        for i in range(groups)
     ]
-    swap.wait_recv()
-    other.start(0)
+    for i in range(groups):
+        outs[i][here, plane.x] = keeps[i][...]
+        lines[i][0].start(0)
+    swaps += [
+        plane.send(sources[i], received[i], swap_sems, groups + i, (1, 0, 0))
+        for i in range(others)
+    ]
+    for i in range(groups):
+        swaps[i].wait_recv()
+        lines[i][1].start(0)
     for step in range(count - 1):
-        own.onward(step)
-        other.onward(step)
+        for side in (0, 1):
+            for i in range(groups):
+                lines[i][side].onward(step)
+    for copy in swaps[groups:]:
+        copy.wait_recv()
     for copy in swaps:
-        copy.wait()
-    swap.wait_send()
-    own.finish()
-    other.finish()
+        copy.wait_send()
+    for i in range(groups):
+        lines[i][0].finish()
+        lines[i][1].finish()
 
 
 def gather_kernel(own, out, sems):
@@ -271,7 +298,7 @@
     out[...] = rounded(reduce_blocks(plane, part, from_core, to_chip, from_chip, sems))
 
 
-def plane_call(kernel, name, number, outs, rows, columns, copies, reduces, operands):
+def plane_call(kernel, name, number, outs, rows, columns, copies, reduces, operands, more=()):
     whole = pl.BlockSpec(memory_space=pltpu.VMEM)
     scratch = []
     if reduces:
@@ -280,7 +307,7 @@
             pltpu.VMEM((3, rows, columns), jnp.bfloat16),
             pltpu.VMEM((3, rows, columns), jnp.bfloat16),
         ]
-    scratch.append(pltpu.SemaphoreType.DMA((2, copies)))
+    scratch += [pltpu.SemaphoreType.DMA((2, copies)), *more]
     return pl.pallas_call(
         kernel,
         name=name,
@@ -324,34 +351,36 @@
     )
 
 
-def input_step(part, values, grad, gain):
+def input_step(part, values, grad, gain, gains_before):
     rows, columns = values.shape
     return plane_call(
-        input_kernel, "input_step", 3, (full((4, rows, columns)), full((1, columns))),
-        rows, columns, 10, True, (part, values, grad, gain),
-    )
-
-
-def weights_step(keep, give, sources, planes):
+        input_kernel, "input_step", 3, (full((4, rows, columns)), full((8, columns))),
+        rows, columns, 12, True, (part, values, grad, gain, gains_before),
+        (pltpu.VMEM((2, 8, columns), jnp.float32), pltpu.VMEM((2, 8, columns), jnp.float32)),
+    )
+
+
+def weights_step(keeps, gives, sources, planes):
     anywhere = pl.BlockSpec(memory_space=pl.ANY)
     whole = pl.BlockSpec(memory_space=pltpu.VMEM)
-    outs = [full((planes, 2) + keep.shape, keep.dtype)]
+    outs = [full((planes, 2) + keep.shape, keep.dtype) for keep in keeps]
     outs += [full(source.shape, source.dtype) for source in sources]
-    return pl.pallas_call(
-        functools.partial(weights_kernel, planes, len(sources)),
+    groups, others = len(keeps), len(sources)
+    results = pl.pallas_call(
+        functools.partial(weights_kernel, planes, groups, others),
         name="weights_step",
         out_shape=outs,
-        in_specs=[whole, whole] + [anywhere] * len(sources),
-        out_specs=[whole] + [anywhere] * len(sources),
+        in_specs=[whole] * (2 * groups) + [anywhere] * others,
+        out_specs=[whole] * groups + [anywhere] * others,
         scratch_shapes=[
-            pltpu.SemaphoreType.DMA((2, 1 + len(sources))),
-            pltpu.SemaphoreType.DMA((2, 2, planes - 1)),
-            pltpu.SemaphoreType.DMA((2, 2, planes - 1)),
+            pltpu.SemaphoreType.DMA((2, groups + others)),
+            pltpu.SemaphoreType.DMA((groups, 2, 2, 2, planes - 1)),
         ],
         compiler_params=pltpu.CompilerParams(
             collective_id=6, has_side_effects=True, vmem_limit_bytes=VMEM_LIMIT
         ),
-    )(keep, give, *sources)
+    )(*keeps, *gives, *sources)
+    return results[:groups], results[groups:]
 
 
 def gather_step(own):
@@ -507,9 +536,6 @@
     depth, patch_depth = cross_q.shape[0], patch_proj.shape[0]
     blocks = width // depth
     heads, units = self_out.shape[0] // 2, ffn_out.shape[0] // 2
-    at_patch, at_qkv, at_gain = places(patch_depth, 3 * depth, 16)
-    at_kv, at_q, at_self, at_cross = places(2 * depth, depth, depth, depth)
-
     def padded(values):
         flat = values.reshape(-1, 3 * depth)
         return jnp.pad(flat, ((0, 0), (0, 16 * heads - 3 * depth))).reshape(-1, 16, heads)
@@ -526,32 +552,28 @@
         cut_out(self_out, x, heads),
         cut_out(cross_out, x, heads),
     ]
-    keep, give = (jnp.concatenate([pair[k] for pair in early]) for k in (0, 1))
     third, fourth = cut_in(ffn_in, x), cut_out(ffn_out, x, depth)
     facts = jnp.concatenate([patch_keep, lengths[:, None]], axis=1)
     facts = jnp.pad(facts, ((0, 7), (0, 127)))
     sources = (third[1], tokens[0], patches[0], fourth[1], cotangent[0], facts)
-    early_w, third_other, token_other, patch_other, fourth_other, grad_other, facts_other = (
-        weights_step(keep, give, sources, blocks // 2)
-    )
+    weights, received = weights_step(
+        [pair[0] for pair in early], [pair[1] for pair in early], sources, blocks // 2
+    )
+    third_other, token_other, patch_other, fourth_other, grad_other, facts_other = received
+    patch_w, qkv_w, gains, cross_kv_w, cross_q_w, self_out_w, cross_out_w = weights
     third = either(third[0], third_other, x, jnp.stack)
     fourth = either(fourth[0], fourth_other, x, jnp.stack)
     token_all = either(tokens[0], token_other, x, jnp.concatenate)
     patch_all = either(patches[0], patch_other, x, jnp.concatenate)
     grad_all = either(cotangent[0], grad_other, x, jnp.concatenate)
     third_w = gather_group(third)
-    early_w = early_w.reshape(blocks, *keep.shape)
-    split = at_gain[1]
-    first_w, second_w = early_w[:, :split], early_w[:, split:]
-
-    patch_w = first_w[:, at_patch[0] : at_patch[1]].reshape(-1, heads)
-    qkv_w = first_w[:, at_qkv[0] : at_qkv[1]].reshape(blocks, 3, depth, heads)
-    cross_kv_w = second_w[:, at_kv[0] : at_kv[1]].reshape(blocks, 2, depth, heads)
-    cross_q_w = second_w[:, at_q[0] : at_q[1]].reshape(width, heads)
-    self_out_w = second_w[:, at_self[0] : at_self[1]].reshape(blocks, heads, depth)
-    cross_out_w = second_w[:, at_cross[0] : at_cross[1]].reshape(blocks, heads, depth)
-
-    gains = unpadded(first_w[:, at_gain[0] : at_gain[1]])
+    patch_w = patch_w.reshape(-1, heads)
+    qkv_w = qkv_w.reshape(blocks, 3, depth, heads)
+    cross_kv_w = cross_kv_w.reshape(blocks, 2, depth, heads)
+    cross_q_w = cross_q_w.reshape(width, heads)
+    self_out_w = self_out_w.reshape(blocks, heads, depth)
+    cross_out_w = cross_out_w.reshape(blocks, heads, depth)
+    gains = unpadded(gains)
     gains = gains.transpose(1, 0, 2).reshape(3, width).astype(jnp.float32)
     gain_of = [gains[i : i + 1] for i in range(3)]
     facts = either(facts[:1], facts_other[:1], x, jnp.concatenate)
@@ -644,8 +666,8 @@
         dot("pbd,cpf->bcdf", cut(memory), grad_key_value),
         dot("sbd,sf->bdf", cut(normed_cross), grad_queries),
         cross_out_part,
-    )
-    self_out_part = dot("sk,sbd->bkd", mixed_self, cut(grad_all))
+        dot("sk,sbd->bkd", mixed_self, cut(grad_all)),
+    )
     grad_mixed = split_heads(rounded(dot("sbd,bkd->sk", cut(grad_all), self_out_w)))
     grad_projected = jnp.stack(attend_back(*self_parts, self_allowed, total_self, grad_mixed))
     second_share = scatter_group(after(second_part, ffn_in_share, grad_projected))
@@ -654,14 +676,16 @@
     part = part.reshape(part.shape[0], 4, 2, -1).transpose(2, 1, 0, 3)
     grad_memory = scatter_step(part.reshape(8, *memory_part.shape))
     part = to_blocks(dot("csf,bcdf->sbd", grad_projected, qkv_w))
-    grad_input, gain_self = input_step(part, own_tokens, grad_after_self, gain_of[0])
-    gains_part = jnp.concatenate([gain_self, gain_cross, gain_ffn], axis=0)
-    gains_part = gains_part.reshape(3, blocks, depth).transpose(1, 0, 2)
+    gains_before = jnp.concatenate([jnp.zeros_like(gain_ffn), gain_cross, gain_ffn])
+    gains_before = jnp.pad(gains_before, ((0, 5), (0, 0)))
+    grad_input, gains_part = input_step(
+        part, own_tokens, grad_after_self, gain_of[0], gains_before
+    )
+    gains_part = gains_part[:3].reshape(3, blocks, depth).transpose(1, 0, 2)
     patch_cut = patch_all.reshape(patch_all.shape[0], blocks, patch_depth)
     first_part = stacked(
         dot("pbk,pd->bkd", patch_cut, grad_memory),
         dot("sbd,csf->bcdf", cut(normed_self), grad_projected),
-        self_out_part,
         padded(gains_part),
     )
     first_part = after(first_part, second_share, grad_input)
@@ -673,17 +697,17 @@
     pair = home_group(after(ffn_in_share, first_part), x)
     grad_ffn_in = home(pair, (0, 2 * depth), (2, depth, units), 2, x)
     pair = home_group(after(second_share, first_part), x)
-    at_kv, at_q, at_cross = places(2 * depth, depth, depth)
+    at_kv, at_q, at_cross, at_self = places(2 * depth, depth, depth, depth)
     grad_cross_kv = home(pair, at_kv, (2, depth, heads), 2, x)
     grad_cross_q = home(pair, at_q, (depth, heads), 1, x)
     grad_cross_out = home(pair, at_cross, (heads, depth), 0, x)
+    grad_self_out = home(pair, at_self, (heads, depth), 0, x)
     pair = home_group(first_share, x)
-    at_patch, at_qkv, at_self, at_gain = places(patch_depth, 3 * depth, depth, 16)
+    at_patch, at_qkv, at_gain = places(patch_depth, 3 * depth, 16)
+    grad_gains = sum(half[at_gain[0] : at_gain[1]].astype(jnp.float32) for half in pair)
+    grad_gains = unpadded(grad_gains)[0]
     grad_patch = home(pair, at_patch, (patch_depth, heads), 1, x)
     grad_self_qkv = home(pair, at_qkv, (3, depth, heads), 2, x)
-    grad_self_out = home(pair, at_self, (heads, depth), 0, x)
-    grad_gains = sum(half[at_gain[0] : at_gain[1]].astype(jnp.float32) for half in pair)
-    grad_gains = lax.psum(unpadded(grad_gains)[0], "mp")
     return (
         output.reshape(1, slots, width),
         grad_input.reshape(1, slots, width),

time: 727 us -> 705 us (0.970)
  local copies, waits for them, and re-layouts: 129 us -> 118 us
    slice x4 -> x1, local copies, waits for them, and re-layouts: 11.5 us -> 0.01 us  [on_device(): gains_part = gains_part[:3].reshape(3, blocks, depth).transpose(1, 0, 2)]
    unnamed x193 -> x194, local copies, waits for them, and re-layouts: 35.4 us -> 31.3 us
  transfers between devices with their start and end apart: 10 -> 10, of which waited for: 5 -> 5; matrix products, arithmetic and copies ran while one was open for 26% -> 25% of each run, Pallas kernels for 32% -> 33%
where the time goes in v4:
time: 705 us; the launch traced here: 700 us
  Pallas kernels  391 us (55%)
  local copies, waits for them, and re-layouts  118 us (17%)
  matrix products  75.3 us (11%)
  waiting for transfers between devices  62 us (9%)
  other arithmetic  29.9 us (4%)
  between operations  16.6 us (2%)
    pallas_call x8, Pallas kernels, plane_call(): pl.pallas_call(kernel, name=name, out_shape=outs, in_specs=[whole] * len(...  232 us
    pallas_call x1, Pallas kernels, weights_step(): pl.pallas_call(functools.partial(weights_kernel, planes, groups, others),...  160 us
    dot_general x23, matrix products, dot(): return jnp.einsum(pattern, left, right, preferred_element_type=jnp.float32)  63.2 us
    reduce_scatter x4, waiting for transfers between devices, scatter_group(): return lax.psum_scatter(parts, 'z', scatter_dimension=0, tiled=True)  34.2 us
    unnamed x194, local copies, waits for them, and re-layouts  31.3 us
    convert_element_type x23, local copies, waits for them, and re-layouts, rounded(): return values.astype(jnp.bfloat16)  30.7 us
    ppermute x4, waiting for transfers between devices, home_group(): lax.ppermute(give, 'x', SWAP)  14.7 us
    reshape x5, local copies, waits for them, and re-layouts, to_blocks(): return rounded(partial_value).reshape(8, rows, width)  14.3 us
  transfers between devices with their start and end apart: 10, of which 5 were waited for; matrix products, arithmetic and copies ran while one was open for 25% of the time, Pallas kernels for 33%

profile of v4, /device:TPU:0, one launch (start us, length us, event | category | flops | bytes accessed | tf_op | source)
XLA Modules:
  0.0 700.5 jit_solution(11977794207865361072)
XLA Ops:
  15.2 159.8 %weights_step.1 = (bf16[4,2,208,256]{3,2,1,0:T(8,128)(2,1)S(1)}, bf16[4,2,768,256]{3,2,1,0:T(8,128)(2,1)}, bf16[4,2,16,256]{3,2,1,0:T(8,128)(2,1)S(1)}, bf16[4,2...) custom-call(bf16[208,256]{1,0:T(8,128)(2,1)S(1)} %get-tuple-element., ...), custom_call_target="tpu_custom_call" | custom-call | tf_op jit(solution)/shard_map/weights_step/pallas_call | solution.py:369
  184.6 4.1 fusion.64
  193.7 16.3 %gather_step.1 = bf16[8,512,256]{2,1,0:T(8,128)(2,1)S(1)} custom-call(bf16[512,256]{1,0:T(8,128)(2,1)S(1)} %fusion.84.own), custom_call_target="tpu_custom_call" | custom-call | tf_op jit(solution)/shard_map/gather_step/pallas_call | solution.py:311
  224.7 32.6 %forward_step.2 = (f32[64,2048]{1,0:T(8,128)S(1)}, bf16[8,64,2048]{2,1,0:T(8,128)(2,1)S(1)}) custom-call(bf16[8,64,2048]{2,1,0:T(8,128)(2,1)S(1)} %reshape.378.part, f32[64,2048]{1,0:T(8,128)S(1)} %get-tuple-element.110.residual.values, f32[1,2048]{1,0:T(1,128)S(1)} %bitcast.357), custom_call_target="tpu_custom_call" | custom-call | tf_op jit(solution)/shard_map/forward_step/pallas_call | solution.py:311
  262.6 13.0 %all-gather.3.cloned.1.call-done.refs_1_ = bf16[8,512,640]{2,1,0:T(8,128)(2,1)} async-done(((bf16[2,512,640]{2,1,0:T(8,128)(2,1)}), bf16[8,512,640]{2,1,0:T(8,128)(2,1)}) %all-gather.3.cloned.1.call-update) | async-done | bytes 5242896 | tf_op jit(solution)/shard_map/all_gather | solution.py:493
  294.1 3.1 reshape.383.part
  298.3 32.8 %forward_step.3 = (f32[64,2048]{1,0:T(8,128)S(1)}, bf16[8,64,2048]{2,1,0:T(8,128)(2,1)S(1)}) custom-call(bf16[8,64,2048]{2,1,0:T(8,128)(2,1)S(1)} %reshape.383.part, f32[64,2048]{1,0:T(8,128)S(1)} %copy-done.9, f32[1,2048]{1,0:T(1,128)S(1)} %bitcast.359), custom_call_target="tpu_custom_call" | custom-call | tf_op jit(solution)/shard_map/forward_step/pallas_call | solution.py:311
  331.8 6.9 fusion.16
  338.8 7.7 %multiply_bitcast_fusion = (f32[1,512,640]{1,2,0:T(8,128)}, f32[1,512,640]{1,2,0:T(8,128)}, bf16[512,640,1]{0,1,2:T(8,128)(2,1)S(1)}) fusion(f32[2,512,640]{1,2,0:T(8,128)} %fusion.16, bf16[8,640,256]{2,1,0:T(8,128)(2,1)} %all-gather.5.cloned.1.call-done.refs_1_, bf16[256,8,256]{0,2,1:T(8,128)(2,1)} %bitcast.402, bf16[256,8,256]{0,2,1:T(8,128)(2,1)} %bitcast.400, ...), kind=kOutput, calls=%fused_computation.89 | convolution fusion | flops 1359478784 | bytes 10616833 | tf_op jit(solution)/shard_map/sbd,bfd->sf/dot_general | solution.py:452
  347.3 3.1 convert_bitcast_fusion.2.refs_0_
  353.5 6.5 bitcast_convert_fusion.2
  365.4 5.3 convert_bitcast_fusion
  373.5 32.9 %backward_step.2 = (f32[64,2048]{1,0:T(8,128)S(1)}, f32[1,2048]{1,0:T(1,128)S(1)}, bf16[8,64,2048]{2,1,0:T(8,128)(2,1)S(1)}) custom-call(bf16[8,64,2048]{2,1,0:T(8,128)(2,1)S(1)} %reshape.385.part, f32[64,2048]{1,0:T(8,128)S(1)} %get-tuple-element.52.values.residual, f32[64,2048]{1,0:T(8,128)S(1)} %copy-done.11, f32[1,2048]{1,0:T(1,128)S(1)} %bitcast.360), custom_call_target="tpu_custom_call" | custom-call | tf_op jit(solution)/shard_map/backward_step/pallas_call | solution.py:311
  439.1 33.1 %backward_step.3 = (f32[64,2048]{1,0:T(8,128)S(1)}, f32[1,2048]{1,0:T(1,128)S(1)}, bf16[8,64,2048]{2,1,0:T(8,128)(2,1)S(1)}) custom-call(bf16[8,64,2048]{2,1,0:T(8,128)(2,1)S(1)} %bitcast.345, f32[64,2048]{1,0:T(8,128)S(1)} %copy-done.10, f32[64,2048]{1,0:T(8,128)S(1)} %copy-done.17, f32[1,2048]{1,0:T(1,128)S(1)} %bitcast.358), custom_call_target="tpu_custom_call" | custom-call | tf_op jit(solution)/shard_map/backward_step/pallas_call | solution.py:311
  495.4 7.2 %pad_maximum_fusion.refs_0_ = bf16[8,1280,256]{2,1,0:T(8,128)(2,1)} fusion(bf16[8,256,256]{2,1,0:T(8,128)(2,1)S(1)} %fusion.47, bf16[8,256,256]{2,1,0:T(8,128)(2,1)S(1)} %fusion.50, bf16[8,256,256]{2,1,0:T(8,128)(2,1)S(1)} %fusion.41, bf16[8,512,256]{2,1,0:T(8,128)(2,1)S(1)} %bitcast.368), kind=kLoop, calls=%fused_computation | loop fusion | flops 20971520 | bytes 10485760 | tf_op jit(solution)/shard_map/concatenate | solution.py:608
  509.3 17.0 %scatter_step.1 = bf16[512,256]{1,0:T(8,128)(2,1)S(1)} custom-call(bf16[8,512,256]{2,1,0:T(8,128)(2,1)S(1)} %bitcast.347), custom_call_target="tpu_custom_call" | custom-call | tf_op jit(solution)/shard_map/scatter_step/pallas_call | solution.py:311
  534.7 34.5 %input_step.1 = (f32[4,64,2048]{2,1,0:T(8,128)S(1)}, f32[8,2048]{1,0:T(8,128)S(1)}) custom-call(bf16[8,64,2048]{2,1,0:T(8,128)(2,1)S(1)} %reshape.392.part, f32[64,2048]{1,0:T(8,128)S(1)} %get-tuple-element.110.residual.values, f32[64,2048]{1,0:T(8,128)S(1)} %copy-done.15, f32[1,2048]{1,0:T(1,128)S(1)} %bitcast.362, f32[8,2048]{1,0:T(8,128)S(1)} %pad.27.gains_before), custom_call_target="tpu_custom_call" | custom-call | tf_op jit(solution)/shard_map/input_step/pallas_call | solution.py:311
  575.7 20.7 %reduce-scatter.9.cloned.1.call-done.refs_1_.refs_0_ = bf16[2,1280,256]{2,1,0:T(8,128)(2,1)} async-done(((bf16[8,1280,256]{2,1,0:T(8,128)(2,1)}), bf16[2,1280,256]{2,1,0:T(8,128)(2,1)}) %reduce-scatter.9.cloned.1.call-update) | async-done | bytes 1310736 | tf_op jit(solution)/shard_map/reduce_scatter | solution.py:497
  597.5 3.6 convolution_convert_fusion.1
  611.2 32.3 %output_step.1 = bf16[4,64,2048]{2,1,0:T(8,128)(2,1)S(1)} custom-call(bf16[8,64,2048]{2,1,0:T(8,128)(2,1)S(1)} %copy-done, f32[64,2048]{1,0:T(8,128)S(1)} %get-tuple-element.52.values.residual), custom_call_target="tpu_custom_call" | custom-call | tf_op jit(solution)/shard_map/output_step/pallas_call | solution.py:311
  648.0 6.2 collective-permute-done.3
  660.3 13.5 %reduce-scatter.11.cloned.1.call-done = bf16[2,992,256]{2,1,0:T(8,128)(2,1)} async-done(((bf16[8,992,256]{2,1,0:T(8,128)(2,1)}), bf16[2,992,256]{2,1,0:T(8,128)(2,1)}) %reduce-scatter.11.cloned.1.call-update) | async-done | bytes 1015824 | tf_op jit(solution)/shard_map/reduce_scatter | solution.py:497
  676.4 3.1 fusion.60
  679.6 8.6 %collective-permute-done = bf16[992,256]{1,0:T(8,128)(2,1)S(1)} collective-permute-done((bf16[992,256]{1,0:T(8,128)(2,1)S(1)}, bf16[992,256]{1,0:T(8,128)(2,1)S(1)}, u32[]{:S(2)}, u32[]{:S(2)}) %collective-permute-start) | collective-permute-done | bytes 507936 | tf_op jit(solution)/shard_map/ppermute | solution.py:502
  (365 shorter events, 180.2 us)
Async XLA Ops:
  7.2 268.4 %all-gather.3.cloned.1.call-start = ((), (), s32[]{:S(2)}) async-start(), calls=%async_computation.4 | async-start | bytes 6553600 | tf_op jit(solution)/shard_map/all_gather | solution.py:493
  175.9 15.5 %copy-start.12 = (bf16[256,1664]{1,0:T(8,128)(2,1)}, bf16[256,1664]{1,0:T(8,128)(2,1)S(1)}, u32[]{:S(2)}) copy-start(bf16[256,1664]{1,0:T(8,128)(2,1)S(1)} %get-tuple-element.38) | copy-start | bytes 2555908
  177.2 161.5 %all-gather.5.cloned.1.call-start = ((), (), s32[]{:S(2)}) async-start(), calls=%async_computation.5 | async-start | bytes 3276800 | tf_op jit(solution)/shard_map/all_gather | solution.py:493
  190.5 24.0 %copy-start.30 = (bf16[2,256,4,64]{1,0,3,2:T(2,128)(2,1)}, bf16[2,256,4,64]{1,0,3,2:T(2,128)(2,1)S(1)}, u32[]{:S(2)}) copy-start(bf16[2,256,4,64]{1,0,3,2:T(2,128)(2,1)S(1)} %reshape_squeeze.16) | copy-start | bytes 786436
  191.4 21.2 %copy-start.60 = (bf16[2,256,4,64]{1,0,3,2:T(2,128)(2,1)}, bf16[2,256,4,64]{1,0,3,2:T(2,128)(2,1)S(1)}, u32[]{:S(2)}) copy-start(bf16[2,256,4,64]{1,0,3,2:T(2,128)(2,1)S(1)} %reshape_squeeze.17) | copy-start | bytes 786436
  222.6 37.9 %copy-start.83 = (bf16[4,2,512,256]{3,2,1,0:T(8,128)(2,1)S(1)}, bf16[4,2,512,256]{3,2,1,0:T(8,128)(2,1)}, u32[]{:S(2)}) copy-start(bf16[4,2,512,256]{3,2,1,0:T(8,128)(2,1)} %get-tuple-element.37) | copy-start | bytes 6291460
  224.7 35.8 %copy-start.38 = (bf16[512,4,2,256]{0,3,2,1:T(8,128)(2,1)S(1)}, bf16[512,4,2,256]{0,3,2,1:T(8,128)(2,1)}, u32[]{:S(2)}) copy-start(bf16[512,4,2,256]{0,3,2,1:T(8,128)(2,1)} %copy.278) | copy-start | bytes 6291460
  275.6 133.0 %reduce-scatter.5.cloned.1.call-start = ((), (), s32[]{:S(2)}) async-start(), calls=%async_computation.6 | async-start | bytes 3276800 | tf_op jit(solution)/shard_map/reduce_scatter | solution.py:497
  338.7 8.6 %copy-start.58 = (bf16[1,256,2048]{1,2,0:T(8,128)(2,1)S(1)}, bf16[1,256,2048]{1,2,0:T(8,128)(2,1)}, u32[]{:S(2)}) copy-start(bf16[1,256,2048]{1,2,0:T(8,128)(2,1)} %copy.424) | copy-start | bytes 3145732
  338.7 8.6 %copy-start.59 = (bf16[256,2048]{0,1:T(8,128)(2,1)S(1)}, bf16[256,2048]{0,1:T(8,128)(2,1)}, u32[]{:S(2)}) copy-start(bf16[256,2048]{0,1:T(8,128)(2,1)} %copy.425) | copy-start | bytes 3145732
  350.4 152.1 %reduce-scatter.7.cloned.1.call-start = ((), (), s32[]{:S(2)}) async-start(), calls=%async_computation.7 | async-start | bytes 6553600 | tf_op jit(solution)/shard_map/reduce_scatter | solution.py:497
  408.6 187.7 %reduce-scatter.9.cloned.1.call-start = ((), (), s32[]{:S(2)}) async-start(), calls=%async_computation.8 | async-start | bytes 6553600 | tf_op jit(solution)/shard_map/reduce_scatter | solution.py:497
  502.6 171.2 %reduce-scatter.11.cloned.1.call-start = ((), (), s32[]{:S(2)}) async-start(), calls=%async_computation.9 | async-start | bytes 5079040 | tf_op jit(solution)/shard_map/reduce_scatter | solution.py:497
  509.1 17.3 %copy-start.82 = (bf16[4,2,768,256]{3,2,1,0:T(8,128)(2,1)S(1)}, bf16[4,2,768,256]{3,2,1,0:T(8,128)(2,1)}, u32[]{:S(2)}) copy-start(bf16[4,2,768,256]{3,2,1,0:T(8,128)(2,1)} %get-tuple-element.41) | copy-start | bytes 9437188
  509.3 17.1 %copy-start.44 = (bf16[3,512,256]{2,1,0:T(8,128)(2,1)S(1)}, bf16[3,512,256]{2,1,0:T(8,128)(2,1)}, u32[]{:S(2)}) copy-start(bf16[3,512,256]{2,1,0:T(8,128)(2,1)} %copy-done.43) | copy-start | bytes 2359300
  530.8 38.5 %copy-start.79 = (f32[8,256]{1,0:T(8,128)S(1)}, f32[8,256]{1,0:T(8,128)}, u32[]{:S(2)}) copy-start(f32[8,256]{1,0:T(8,128)} %copy-done.78) | copy-start | bytes 24580
  533.6 35.7 %copy-start.81 = (f32[512]{0:T(512)S(1)}, f32[512]{0:T(512)}, u32[]{:S(2)}) copy-start(f32[512]{0:T(512)} %copy-done.80) | copy-start | bytes 6148
  534.7 34.6 %copy-start.45 = (bf16[3,512,256]{2,1,0:T(8,128)(2,1)S(1)}, bf16[3,512,256]{2,1,0:T(8,128)(2,1)}, u32[]{:S(2)}) copy-start(bf16[3,512,256]{2,1,0:T(8,128)(2,1)} %copy-done.43) | copy-start | bytes 2359300
  534.7 34.6 %copy-start.49 = (bf16[1,256,2048]{1,2,0:T(8,128)(2,1)S(1)}, bf16[1,256,2048]{1,2,0:T(8,128)(2,1)}, u32[]{:S(2)}) copy-start(bf16[1,256,2048]{1,2,0:T(8,128)(2,1)} %copy.418) | copy-start | bytes 3145732
  534.7 34.6 %copy-start.51 = (bf16[256,2048]{0,1:T(8,128)(2,1)S(1)}, bf16[256,2048]{0,1:T(8,128)(2,1)}, u32[]{:S(2)}) copy-start(bf16[256,2048]{0,1:T(8,128)(2,1)} %copy.419) | copy-start | bytes 3145732
  606.9 49.5 %collective-permute-start.1 = (bf16[1280,256]{1,0:T(8,128)(2,1)}, bf16[1280,256]{1,0:T(8,128)(2,1)S(1)}, u32[]{:S(2)}, u32[]{:S(2)}) collective-permute-start(bf16[1280,256]{1,0:T(8,128)(2,1)} %dynamic-slice_bitcast_fusion.1), channel_id=1, source_target_pairs={{0,4},{4,0},{1,5},{5,1},{2,6},{6,2},{3,7},{7,3},{8,12},{12,8},{9,1... | collective-permute-start | bytes 1966088 | tf_op jit(solution)/shard_map/ppermute | solution.py:502
  643.5 10.7 %collective-permute-start.3 = (bf16[640,256]{1,0:T(8,128)(2,1)S(1)}, bf16[640,256]{1,0:T(8,128)(2,1)}, u32[]{:S(2)}, u32[]{:S(2)}) collective-permute-start(bf16[640,256]{1,0:T(8,128)(2,1)S(1)} %get-tuple-element.77), channel_id=1, source_target_pairs={{0,4},{4,0},{1,5},{5,1},{2,6},{6,2},{3,7},{7,3},{8,12},{12,8},{9,1... | collective-permute-start | bytes 983048 | tf_op jit(solution)/shard_map/ppermute | solution.py:502
  647.3 29.1 %collective-permute-start.2 = (bf16[512,640]{1,0:T(8,128)(2,1)}, bf16[512,640]{1,0:T(8,128)(2,1)}, u32[]{:S(2)}, u32[]{:S(2)}) collective-permute-start(bf16[512,640]{1,0:T(8,128)(2,1)} %get-tuple-element.65), channel_id=1, source_target_pairs={{0,4},{4,0},{1,5},{5,1},{2,6},{6,2},{3,7},{7,3},{8,12},{12,8},{9,1... | collective-permute-start | bytes 1966088 | tf_op jit(solution)/shard_map/ppermute | solution.py:502
  674.9 13.2 %collective-permute-start = (bf16[992,256]{1,0:T(8,128)(2,1)S(1)}, bf16[992,256]{1,0:T(8,128)(2,1)S(1)}, u32[]{:S(2)}, u32[]{:S(2)}) collective-permute-start(bf16[992,256]{1,0:T(8,128)(2,1)S(1)} %dynamic-slice_bitcast_fusion.3), channel_id=1, source_target_pairs={{0,4},{4,0},{1,5},{5,1},{2,6},{6,2},{3,7},{7,3},{8,12},{12,8},{9,1... | collective-permute-start | bytes 1523720 | tf_op jit(solution)/shard_map/ppermute | solution.py:502
  (72 other events, 168.0 us)
Sparse Core Ops, SparseCore 0:
  177.3 98.1 all-gather.2
  277.7 53.1 all-gather.4
  350.5 49.5 reduce-scatter.4
  408.8 91.1 reduce-scatter.6
  502.7 93.6 reduce-scatter.8
  598.5 75.2 reduce-scatter.10

commit v5 on v4

--- a/solution.py
+++ b/solution.py
@@ -130,15 +130,27 @@
 ROW_RELATIONS = ((0, 0, 1), (0, 1, 0))
 
 
-def reduce_blocks(plane, part, from_core, to_chip, from_chip, sems):
+def row_blocks(plane, part, rows):
+    def at(*relation):
+        start = pl.multiple_of(plane.block(*relation) * rows, rows)
+        return part.at[:, pl.ds(start, rows)]
+
+    return at
+
+
+def as_rows(values):
+    return jnp.concatenate([values[k] for k in range(values.shape[0])], axis=-1)
+
+
+def reduce_blocks(plane, at, from_core, to_chip, from_chip, sems):
     pair = [
-        plane.send(part.at[plane.block(dx, dy, 1)], from_core.at[i], sems, i, (0, 0, 1))
+        plane.send(at(dx, dy, 1), from_core.at[i], sems, i, (0, 0, 1))
         for i, (dx, dy) in enumerate(RELATIVE)
     ]
     across = []
     for i, (dx, dy) in enumerate(RELATIVE):
         pair[i].wait_recv()
-        both = part[plane.block(dx, dy, 0)].astype(jnp.float32) + from_core[i].astype(jnp.float32)
+        both = at(dx, dy, 0)[...].astype(jnp.float32) + from_core[i].astype(jnp.float32)
         if i < 3:
             to_chip[i] = rounded(both)
             across.append(plane.send(to_chip.at[i], from_chip.at[i], sems, 4 + i, (dx, dy, 0)))
@@ -148,6 +160,11 @@
     for copy in pair + across:
         copy.wait_send()
     return both
+
+
+def reduce_rows(plane, part, from_core, to_chip, from_chip, sems):
+    at = row_blocks(plane, part, from_core.shape[2])
+    return as_rows(reduce_blocks(plane, at, from_core, to_chip, from_chip, sems))
 
 
 def gather_blocks(plane, out, sems, first):
@@ -184,7 +201,7 @@
 def forward_kernel(part, residual, gain, after, normed, from_core, to_chip, from_chip, sems):
     plane = Plane()
     plane.greet(ALL_RELATIONS)
-    values = residual[...] + reduce_blocks(plane, part, from_core, to_chip, from_chip, sems)
+    values = residual[...] + reduce_rows(plane, part, from_core, to_chip, from_chip, sems)
     after[...] = values
     scale = lax.rsqrt(jnp.mean(values * values, axis=-1, keepdims=True) + EPS)
     normed[plane.block(0, 0, 0)] = rounded(values * scale * gain[...])
@@ -206,7 +223,7 @@
 ):
     plane = Plane()
     plane.greet(ALL_RELATIONS)
-    total = reduce_blocks(plane, part, from_core, to_chip, from_chip, sems)
+    total = reduce_rows(plane, part, from_core, to_chip, from_chip, sems)
     side, gain_sum = back_values(values[...], gain[...], total)
     gain_part[...] = gain_sum
     result = grad[...] + side
@@ -215,12 +232,41 @@
     gather_blocks(plane, grad_all, sems, 7)
 
 
-def output_kernel(part, residual, out, from_core, to_chip, from_chip, sems):
+def output_kernel(
+    part, residual, pieces, out, pieces_sum,
+    from_core, to_chip, from_chip, sems, arrived, piece_sems,
+):
     plane = Plane()
-    plane.greet(ALL_RELATIONS)
-    values = residual[...] + reduce_blocks(plane, part, from_core, to_chip, from_chip, sems)
+    z, planes = lax.axis_index("z"), pieces.shape[0]
+    others = [lax.rem(z + step, planes) for step in range(1, planes)]
+    barrier = pltpu.get_barrier_semaphore()
+    for target in [{"z": other} for other in others] + [plane.device(*r) for r in ALL_RELATIONS]:
+        pl.semaphore_signal(
+            barrier, inc=1, device_id=target, device_id_type=pl.DeviceIdType.MESH
+        )
+    pl.semaphore_wait(barrier, len(others) + len(ALL_RELATIONS))
+    copies = []
+    for step, other in enumerate(others):
+        copy = pltpu.make_async_remote_copy(
+            src_ref=pieces.at[other],
+            dst_ref=arrived.at[step],
+            send_sem=piece_sems.at[0, step],
+            recv_sem=piece_sems.at[1, step],
+            device_id={"z": other},
+            device_id_type=pl.DeviceIdType.MESH,
+        )
+        copy.start()
+        copies.append(copy)
+    values = residual[...] + reduce_rows(plane, part, from_core, to_chip, from_chip, sems)
     out[plane.y * 2 + plane.c] = rounded(values)
     gather_rows(plane, out, sems, 7)
+    total = pieces[z].astype(jnp.float32)
+    for step, copy in enumerate(copies):
+        copy.wait_recv()
+        total = total + arrived[step].astype(jnp.float32)
+    pieces_sum[...] = total
+    for copy in copies:
+        copy.wait_send()
 
 
 def input_kernel(
@@ -229,7 +275,7 @@
 ):
     plane = Plane()
     plane.greet(ALL_RELATIONS)
-    total = reduce_blocks(plane, part, from_core, to_chip, from_chip, sems)
+    total = reduce_rows(plane, part, from_core, to_chip, from_chip, sems)
     side, gain_sum = back_values(values[...], gain[...], total)
     out[plane.y * 2 + plane.c] = grad[...] + side
     sums[0] = gains_before[...]
@@ -295,18 +341,16 @@
 def scatter_kernel(part, out, from_core, to_chip, from_chip, sems):
     plane = Plane()
     plane.greet(ALL_RELATIONS)
-    out[...] = rounded(reduce_blocks(plane, part, from_core, to_chip, from_chip, sems))
-
-
-def plane_call(kernel, name, number, outs, rows, columns, copies, reduces, operands, more=()):
+    out[...] = rounded(
+        reduce_blocks(
+            plane, lambda *r: part.at[plane.block(*r)], from_core, to_chip, from_chip, sems
+        )
+    )
+
+
+def plane_call(kernel, name, number, outs, block, copies, operands, more=()):
     whole = pl.BlockSpec(memory_space=pltpu.VMEM)
-    scratch = []
-    if reduces:
-        scratch = [
-            pltpu.VMEM((4, rows, columns), jnp.bfloat16),
-            pltpu.VMEM((3, rows, columns), jnp.bfloat16),
-            pltpu.VMEM((3, rows, columns), jnp.bfloat16),
-        ]
+    scratch = [pltpu.VMEM((k,) + block, jnp.bfloat16) for k in (4, 3, 3)] if block else []
     scratch += [pltpu.SemaphoreType.DMA((2, copies)), *more]
     return pl.pallas_call(
         kernel,
@@ -321,6 +365,10 @@
     )(*operands)
 
 
+def block_of(part, rows):
+    return (part.shape[0], rows, part.shape[2])
+
+
 def full(shape, dtype=jnp.float32):
     return jax.ShapeDtypeStruct(shape, dtype)
 
@@ -330,7 +378,7 @@
     return plane_call(
         forward_kernel, "forward_step", 0,
         (full((rows, columns)), full((8, rows, columns), jnp.bfloat16)),
-        rows, columns, 14, True, (part, residual, gain),
+        block_of(part, rows), 14, (part, residual, gain),
     )
 
 
@@ -339,15 +387,18 @@
     return plane_call(
         backward_kernel, "backward_step", 1,
         (full((rows, columns)), full((1, columns)), full((8, rows, columns), jnp.bfloat16)),
-        rows, columns, 14, True, (part, values, grad, gain),
-    )
-
-
-def output_step(part, residual):
+        block_of(part, rows), 14, (part, values, grad, gain),
+    )
+
+
+def output_step(part, residual, pieces):
     rows, columns = residual.shape
+    others, shape = pieces.shape[0] - 1, pieces.shape[1:]
     return plane_call(
-        output_kernel, "output_step", 2, full((4, rows, columns), jnp.bfloat16),
-        rows, columns, 10, True, (part, residual),
+        output_kernel, "output_step", 2,
+        (full((4, rows, columns), jnp.bfloat16), full(shape)),
+        block_of(part, rows), 10, (part, residual, pieces),
+        (pltpu.VMEM((others,) + shape, pieces.dtype), pltpu.SemaphoreType.DMA((2, others))),
     )
 
 
@@ -355,7 +406,7 @@
     rows, columns = values.shape
     return plane_call(
         input_kernel, "input_step", 3, (full((4, rows, columns)), full((8, columns))),
-        rows, columns, 12, True, (part, values, grad, gain, gains_before),
+        block_of(part, rows), 12, (part, values, grad, gain, gains_before),
         (pltpu.VMEM((2, 8, columns), jnp.float32), pltpu.VMEM((2, 8, columns), jnp.float32)),
     )
 
@@ -387,7 +438,7 @@
     rows, columns = own.shape
     return plane_call(
         gather_kernel, "gather_step", 4, full((8, rows, columns), own.dtype),
-        rows, columns, 7, False, (own,),
+        None, 7, (own,),
     )
 
 
@@ -395,7 +446,7 @@
     _, rows, columns = part.shape
     return plane_call(
         scatter_kernel, "scatter_step", 5, full((rows, columns), part.dtype),
-        rows, columns, 7, True, (part,),
+        (rows, columns), 7, (part,),
     )
 
 
@@ -498,14 +549,15 @@
 
 
 def home_group(share, x):
-    give = lax.dynamic_index_in_dim(share, 1 - x, 0, False)
+    give = rounded(lax.dynamic_index_in_dim(share, 1 - x, 0, False))
     return lax.dynamic_index_in_dim(share, x, 0, False), lax.ppermute(give, "x", SWAP)
 
 
 def home(pair, place, shape, axis, x):
-    own, other = (half[place[0] : place[1]].reshape(shape) for half in pair)
-    joined = either(own, other, x, functools.partial(jnp.concatenate, axis=axis))
-    return joined.astype(jnp.float32)
+    own, other = (
+        half[place[0] : place[1]].reshape(shape).astype(jnp.float32) for half in pair
+    )
+    return either(own, other, x, functools.partial(jnp.concatenate, axis=axis))
 
 
 def places(*sizes):
@@ -596,7 +648,10 @@
     )
 
     def to_blocks(partial_value):
-        return rounded(partial_value).reshape(8, rows, width)
+        partial_value = rounded(partial_value)
+        if depth % 128 == 0:
+            return partial_value
+        return jnp.moveaxis(partial_value, 0, 1).reshape(1, 8 * rows, width)
 
     def from_blocks(values):
         return values.reshape(8 * rows, width)
@@ -619,31 +674,31 @@
     )
     ffn_in_w = third_w.reshape(blocks, 2, depth, units)
 
-    part = dot("sk,bkd->sbd", mixed_self, self_out_w)
+    part = dot("sk,bkd->bsd", mixed_self, self_out_w)
     after_self, normed_cross = forward_step(to_blocks(part), own_tokens, gain_of[1])
     normed_cross = from_blocks(normed_cross)
 
     key_value = rounded(dot("pbd,bcdf->cpf", cut(memory), cross_kv_w))
     query_heads = split_heads(rounded(dot("sd,df->sf", normed_cross, cross_q_w)))
-    fourth_w = gather_group(after(fourth, third_w, normed_cross, key_value))
     cross_keys = split_heads(key_value[0])
     cross_values = split_heads(key_value[1])
     mixed_cross, total_cross = attend(query_heads, cross_keys, cross_values, cross_allowed)
-    part = dot("sk,bkd->sbd", mixed_cross, cross_out_w)
+    fourth_w = gather_group(after(fourth, third_w, mixed_cross))
+    part = dot("sk,bkd->bsd", mixed_cross, cross_out_w)
     after_cross, normed_ffn = forward_step(to_blocks(part), after_self, gain_of[2])
-    ffn_out_w = fourth_w.reshape(blocks, units, depth)
     normed_ffn = from_blocks(normed_ffn)
 
     gate_up = dot("sbd,bcdf->csf", cut(normed_ffn), ffn_in_w)
     hidden = rounded(gated_gelu(gate_up))
+    ffn_out_w = after(fourth_w, hidden).reshape(blocks, units, depth)
     ffn_out_part = rounded(dot("sf,sbd->bfd", hidden, cut(grad_all)))
-    ffn_out_share = scatter_group(after(ffn_out_part, fourth_w))
-    output_part = to_blocks(dot("sf,bfd->sbd", hidden, ffn_out_w))
+    ffn_out_share = scatter_group(after(ffn_out_part, ffn_out_w))
+    output_part = to_blocks(dot("sf,bfd->bsd", hidden, ffn_out_w))
 
     grad_hidden = dot("sbd,bfd->sf", cut(grad_all), ffn_out_w)
     grad_gate_up = rounded(jax.vjp(gated_gelu, gate_up)[1](grad_hidden)[0])
     ffn_in_part = rounded(dot("sbd,csf->bcdf", cut(normed_ffn), grad_gate_up))
-    part = dot("csf,bcdf->sbd", grad_gate_up, ffn_in_w)
+    part = dot("csf,bcdf->bsd", grad_gate_up, ffn_in_w)
     grad_after_cross, gain_ffn, grad_all = backward_step(
         to_blocks(part), after_cross, own_grad, gain_of[2]
     )
@@ -656,26 +711,26 @@
     grad_queries, grad_keys, grad_values = attend_back(
         query_heads, cross_keys, cross_values, cross_allowed, total_cross, grad_mixed
     )
-    part = dot("sf,df->sd", grad_queries, cross_q_w)
+    part = dot("sf,bdf->bsd", grad_queries, cross_q_w.reshape(blocks, depth, heads))
     grad_after_self, gain_cross, grad_all = backward_step(
         to_blocks(part), after_self, grad_after_cross, gain_of[1]
     )
     grad_all = from_blocks(grad_all)
     grad_key_value = jnp.stack([grad_keys, grad_values])
+    grad_mixed = split_heads(rounded(dot("sbd,bkd->sk", cut(grad_all), self_out_w)))
+    grad_projected = jnp.stack(attend_back(*self_parts, self_allowed, total_self, grad_mixed))
     second_part = stacked(
         dot("pbd,cpf->bcdf", cut(memory), grad_key_value),
         dot("sbd,sf->bdf", cut(normed_cross), grad_queries),
         cross_out_part,
         dot("sk,sbd->bkd", mixed_self, cut(grad_all)),
     )
-    grad_mixed = split_heads(rounded(dot("sbd,bkd->sk", cut(grad_all), self_out_w)))
-    grad_projected = jnp.stack(attend_back(*self_parts, self_allowed, total_self, grad_mixed))
     second_share = scatter_group(after(second_part, ffn_in_share, grad_projected))
 
     part = rounded(dot("cpf,bcdf->pbd", grad_key_value, cross_kv_w))
     part = part.reshape(part.shape[0], 4, 2, -1).transpose(2, 1, 0, 3)
     grad_memory = scatter_step(part.reshape(8, *memory_part.shape))
-    part = to_blocks(dot("csf,bcdf->sbd", grad_projected, qkv_w))
+    part = to_blocks(dot("csf,bcdf->bsd", grad_projected, qkv_w))
     gains_before = jnp.concatenate([jnp.zeros_like(gain_ffn), gain_cross, gain_ffn])
     gains_before = jnp.pad(gains_before, ((0, 5), (0, 0)))
     grad_input, gains_part = input_step(
@@ -683,19 +738,22 @@
     )
     gains_part = gains_part[:3].reshape(3, blocks, depth).transpose(1, 0, 2)
     patch_cut = patch_all.reshape(patch_all.shape[0], blocks, patch_depth)
-    first_part = stacked(
-        dot("pbk,pd->bkd", patch_cut, grad_memory),
-        dot("sbd,csf->bcdf", cut(normed_self), grad_projected),
-        padded(gains_part),
-    )
-    first_part = after(first_part, second_share, grad_input)
+    pieces = stacked(dot("pbk,pd->bkd", patch_cut, grad_memory), padded(gains_part))
+    pieces = jnp.pad(pieces, ((0, 0), (0, -pieces.shape[1] % 16), (0, 0)))
+    pieces = pieces.reshape(blocks // 2, 2, -1, heads)
+    output, patch_share = output_step(output_part, after_cross, pieces)
+    pair = home_group(after(ffn_out_share, grad_input), x)
+    grad_ffn_out = home(pair, (0, units), (units, depth), 0, x)
+    pair = home_group(after(ffn_in_share, grad_input), x)
+    grad_ffn_in = home(pair, (0, 2 * depth), (2, depth, units), 2, x)
+    pair = home_group(patch_share, x)
+    at_patch, at_gain = places(patch_depth, 16)
+    grad_patch = home(pair, at_patch, (patch_depth, heads), 1, x)
+    grad_gains = sum(half[at_gain[0] : at_gain[1]].astype(jnp.float32) for half in pair)
+    grad_gains = unpadded(grad_gains)[0]
+    first_part = stacked(dot("sbd,csf->bcdf", cut(normed_self), grad_projected))
+    first_part = after(first_part, second_share, output)
     first_share = scatter_group(first_part)
-    output = output_step(after(output_part, first_part), after_cross)
-
-    pair = home_group(after(ffn_out_share, first_part), x)
-    grad_ffn_out = home(pair, (0, units), (units, depth), 0, x)
-    pair = home_group(after(ffn_in_share, first_part), x)
-    grad_ffn_in = home(pair, (0, 2 * depth), (2, depth, units), 2, x)
     pair = home_group(after(second_share, first_part), x)
     at_kv, at_q, at_cross, at_self = places(2 * depth, depth, depth, depth)
     grad_cross_kv = home(pair, at_kv, (2, depth, heads), 2, x)
@@ -703,11 +761,7 @@
     grad_cross_out = home(pair, at_cross, (heads, depth), 0, x)
     grad_self_out = home(pair, at_self, (heads, depth), 0, x)
     pair = home_group(first_share, x)
-    at_patch, at_qkv, at_gain = places(patch_depth, 3 * depth, 16)
-    grad_gains = sum(half[at_gain[0] : at_gain[1]].astype(jnp.float32) for half in pair)
-    grad_gains = unpadded(grad_gains)[0]
-    grad_patch = home(pair, at_patch, (patch_depth, heads), 1, x)
-    grad_self_qkv = home(pair, at_qkv, (3, depth, heads), 2, x)
+    grad_self_qkv = home(pair, (0, 3 * depth), (3, depth, heads), 2, x)
     return (
         output.reshape(1, slots, width),
         grad_input.reshape(1, slots, width),

time: 705 us -> 685 us (0.972)
  local copies, waits for them, and re-layouts: 118 us -> 87.8 us
  waiting for transfers between devices: 62 us -> 78.2 us
  matrix products: 75.3 us -> 67 us
    ppermute x4 -> x5, waiting for transfers between devices: 14.7 us -> 33.6 us  [home_group(): lax.ppermute(give, 'x', SWAP)]
    reshape x5 -> x0, local copies, waits for them, and re-layouts: 14.3 us -> none  [to_blocks(): return rounded(partial_value).reshape(8, rows, width)]
    dot_general x23, matrix products: 63.2 us -> 52.9 us  [dot(): return jnp.einsum(pattern, left, right, preferred_element_type=jnp.float32)]
    select_n x3 -> x11, other arithmetic: 2.24 us -> 12.2 us  [either(): return jnp.where(x == 0, join([own, other]), join([other, own]))]
    convert_element_type x23 -> x20, local copies, waits for them, and re-layouts: 30.7 us -> 21.8 us  [rounded(): return values.astype(jnp.bfloat16)]
    convert_element_type x8 -> x12, other arithmetic: 11.4 us -> 3.84 us  [the longest x11 2.79 us: home(): half[place[0]:place[1]].reshape(shape).astype(jnp.float32)]
    unnamed x194 -> x168, local copies, waits for them, and re-layouts: 31.3 us -> 28 us
  transfers between devices with their start and end apart: 10 -> 11, of which waited for: 5 -> 10; matrix products, arithmetic and copies ran while one was open for 25% -> 23% of each run, Pallas kernels for 33% -> 34%
where the time goes in v5:
time: 685 us; the launch traced here: 681 us
  Pallas kernels  393 us (57%)
  local copies, waits for them, and re-layouts  87.8 us (13%)
  waiting for transfers between devices  78.2 us (11%)
  matrix products  67 us (10%)
  other arithmetic  29.7 us (4%)
  between operations  16.6 us (2%)
  starting transfers between devices  8.03 us (1%)
    pallas_call x8, Pallas kernels, plane_call(): pl.pallas_call(kernel, name=name, out_shape=outs, in_specs=[whole] * len(...  233 us
    pallas_call x1, Pallas kernels, weights_step(): pl.pallas_call(functools.partial(weights_kernel, planes, groups, others),...  160 us
    dot_general x23, matrix products, dot(): return jnp.einsum(pattern, left, right, preferred_element_type=jnp.float32)  52.9 us
    reduce_scatter x4, waiting for transfers between devices, scatter_group(): return lax.psum_scatter(parts, 'z', scatter_dimension=0, tiled=True)  33.9 us
    ppermute x5, waiting for transfers between devices, home_group(): lax.ppermute(give, 'x', SWAP)  33.6 us
    unnamed x168, local copies, waits for them, and re-layouts  28 us
    convert_element_type x20, local copies, waits for them, and re-layouts, rounded(): return values.astype(jnp.bfloat16)  21.8 us
  transfers between devices with their start and end apart: 11, of which 10 were waited for; matrix products, arithmetic and copies ran while one was open for 23% of the time, Pallas kernels for 34%

profile of v5, /device:TPU:0, one launch (start us, length us, event | category | flops | bytes accessed | tf_op | source)
XLA Modules:
  0.0 680.7 jit_solution(9725668983685509263)
XLA Ops:
  15.9 160.1 %weights_step.1 = (bf16[4,2,208,256]{3,2,1,0:T(8,128)(2,1)S(1)}, bf16[4,2,768,256]{3,2,1,0:T(8,128)(2,1)}, bf16[4,2,16,256]{3,2,1,0:T(8,128)(2,1)S(1)}, bf16[4,2...) custom-call(bf16[208,256]{1,0:T(8,128)(2,1)S(1)} %get-tuple-element., ...), custom_call_target="tpu_custom_call" | custom-call | tf_op jit(solution)/shard_map/weights_step/pallas_call | solution.py:420
  185.0 4.2 fusion.65
  193.6 16.2 %gather_step.1 = bf16[8,512,256]{2,1,0:T(8,128)(2,1)S(1)} custom-call(bf16[512,256]{1,0:T(8,128)(2,1)S(1)} %fusion.85.own), custom_call_target="tpu_custom_call" | custom-call | tf_op jit(solution)/shard_map/gather_step/pallas_call | solution.py:355
  212.1 3.5 fusion.68
  220.9 32.7 %forward_step.2 = (f32[64,2048]{1,0:T(8,128)S(1)}, bf16[8,64,2048]{2,1,0:T(8,128)(2,1)S(1)}) custom-call(bf16[8,512,256]{2,1,0:T(8,128)(2,1)S(1)} %convert_bitcast_fusion.7.part, f32[64,2048]{1,0:T(8,128)S(1)} %bitcast_convert_fusion.6.residual.values, f32[1,2048]{1,0:T(1,128)S(1)} %bitcast.385), custom_call_target="tpu_custom_call" | custom-call | tf_op jit(solution)/shard_map/forward_step/pallas_call | solution.py:355
  267.7 8.8 %all-gather.3.cloned.1.call-done.refs_1_ = bf16[8,512,640]{2,1,0:T(8,128)(2,1)} async-done(((bf16[2,512,640]{2,1,0:T(8,128)(2,1)}), bf16[8,512,640]{2,1,0:T(8,128)(2,1)}) %all-gather.3.cloned.1.call-update) | async-done | bytes 5242896 | tf_op jit(solution)/shard_map/all_gather | solution.py:544
  284.0 32.9 %forward_step.3 = (f32[64,2048]{1,0:T(8,128)S(1)}, bf16[8,64,2048]{2,1,0:T(8,128)(2,1)S(1)}) custom-call(bf16[8,512,256]{2,1,0:T(8,128)(2,1)S(1)} %convert_bitcast_fusion.6.part, f32[64,2048]{1,0:T(8,128)S(1)} %copy-done.7, f32[1,2048]{1,0:T(1,128)S(1)} %bitcast.387), custom_call_target="tpu_custom_call" | custom-call | tf_op jit(solution)/shard_map/forward_step/pallas_call | solution.py:355
  317.5 6.5 fusion.16
  331.4 4.4 copy.350
  336.8 6.8 multiply_bitcast_fusion
  349.6 3.1 fusion.33.part
  352.7 33.0 %backward_step.2 = (f32[64,2048]{1,0:T(8,128)S(1)}, f32[1,2048]{1,0:T(1,128)S(1)}, bf16[8,64,2048]{2,1,0:T(8,128)(2,1)S(1)}) custom-call(bf16[8,512,256]{2,1,0:T(8,128)(2,1)S(1)} %fusion.33.part, f32[64,2048]{1,0:T(8,128)S(1)} %get-tuple-element.53.values.residual, f32[64,2048]{1,0:T(8,128)S(1)} %bitcast_convert_fusion.5.grad, f32[1,2048]{1,0:T(1,128)S(1)} %bitcast.388), custom_call_target="tpu_custom_call" | custom-call | tf_op jit(solution)/shard_map/backward_step/pallas_call | solution.py:355
  416.2 32.7 %backward_step.3 = (f32[64,2048]{1,0:T(8,128)S(1)}, f32[1,2048]{1,0:T(1,128)S(1)}, bf16[8,64,2048]{2,1,0:T(8,128)(2,1)S(1)}) custom-call(bf16[8,512,256]{2,1,0:T(8,128)(2,1)S(1)} %convert_bitcast_fusion.4.part, f32[64,2048]{1,0:T(8,128)S(1)} %copy-done.8, f32[64,2048]{1,0:T(8,128)S(1)} %copy-done.12, f32[1,2048]{1,0:T(1,128)S(1)} %bitcast.386), custom_call_target="tpu_custom_call" | custom-call | tf_op jit(solution)/shard_map/backward_step/pallas_call | solution.py:355
  470.6 7.2 %pad_maximum_fusion.refs_0_ = bf16[8,1280,256]{2,1,0:T(8,128)(2,1)} fusion(bf16[8,256,256]{2,1,0:T(8,128)(2,1)S(1)} %fusion.49, bf16[8,256,256]{2,1,0:T(8,128)(2,1)S(1)} %fusion.52, bf16[8,256,256]{2,1,0:T(8,128)(2,1)S(1)} %fusion.43, bf16[8,512,256]{2,1,0:T(8,128)(2,1)S(1)} %bitcast.396), kind=kLoop, calls=%fused_computation | loop fusion | flops 20971520 | bytes 10485760 | tf_op jit(solution)/shard_map/concatenate | solution.py:663
  486.4 17.0 %scatter_step.1 = bf16[512,256]{1,0:T(8,128)(2,1)S(1)} custom-call(bf16[8,512,256]{2,1,0:T(8,128)(2,1)S(1)} %bitcast.376), custom_call_target="tpu_custom_call" | custom-call | tf_op jit(solution)/shard_map/scatter_step/pallas_call | solution.py:355
  505.4 35.0 %input_step.1 = (f32[4,64,2048]{2,1,0:T(8,128)S(1)}, f32[8,2048]{1,0:T(8,128)S(1)}) custom-call(bf16[8,512,256]{2,1,0:T(8,128)(2,1)S(1)} %fusion.34.part, f32[64,2048]{1,0:T(8,128)S(1)} %bitcast_convert_fusion.6.residual.values, f32[64,2048]{1,0:T(8,128)S(1)} %get-tuple-element.58.grad, f32[1,2048]{1,0:T(1,128)S(1)} %bitcast.390, f32[8,2048]{1,0:T(8,128)S(1)} %pad.27.gains_before), custom_call_target="tpu_custom_call" | custom-call | tf_op jit(solution)/shard_map/input_step/pallas_call | solution.py:355
  548.5 33.7 %output_step.1 = (bf16[4,64,2048]{2,1,0:T(8,128)(2,1)S(1)}, f32[2,224,256]{2,1,0:T(8,128)S(1)}) custom-call(bf16[8,512,256]{2,1,0:T(8,128)(2,1)S(1)} %convert_bitcast_fusion.5.part, f32[64,2048]{1,0:T(8,128)S(1)} %get-tuple-element.53.values.residual, bf16[4,2,224,256]{3,2,1,0:T(8,128)(2,1)S(1)} %bitcast.378), custom_call_target="tpu_custom_call" | custom-call | tf_op jit(solution)/shard_map/output_step/pallas_call | solution.py:355
  583.2 8.2 %reduce-scatter.9.cloned.1.call-done.refs_1_.refs_0_ = bf16[2,1280,256]{2,1,0:T(8,128)(2,1)} async-done(((bf16[8,1280,256]{2,1,0:T(8,128)(2,1)}), bf16[2,1280,256]{2,1,0:T(8,128)(2,1)}) %reduce-scatter.9.cloned.1.call-update) | async-done | bytes 1310736 | tf_op jit(solution)/shard_map/reduce_scatter | solution.py:548
  593.0 3.5 collective-permute-done
  602.6 5.7 collective-permute-done.4
  612.4 10.1 %collective-permute-done.3 = bf16[512,640]{1,0:T(8,128)(2,1)} collective-permute-done((bf16[512,640]{1,0:T(8,128)(2,1)S(1)}, bf16[512,640]{1,0:T(8,128)(2,1)}, u32[]{:S(2)}, u32[]{:S(2)}) %collective-permute-start.3) | collective-permute-done | bytes 655392 | tf_op jit(solution)/shard_map/ppermute | solution.py:553
  625.6 8.8 %collective-permute-done.2 = bf16[1280,256]{1,0:T(8,128)(2,1)S(1)} collective-permute-done((bf16[1280,256]{1,0:T(8,128)(2,1)S(1)}, bf16[1280,256]{1,0:T(8,128)(2,1)S(1)}, u32[]{:S(2)}, u32[]{:S(2)}) %collective-permute-start.2) | collective-permute-done | bytes 655392 | tf_op jit(solution)/shard_map/ppermute | solution.py:553
  634.5 23.3 %reduce-scatter.11.cloned.1.call-done = bf16[2,768,256]{2,1,0:T(8,128)(2,1)} async-done(((bf16[8,768,256]{2,1,0:T(8,128)(2,1)}), bf16[2,768,256]{2,1,0:T(8,128)(2,1)}) %reduce-scatter.11.cloned.1.call-update) | async-done | bytes 786448 | tf_op jit(solution)/shard_map/reduce_scatter | solution.py:548
  664.3 5.4 collective-permute-done.1
  (339 shorter events, 161.4 us)
Async XLA Ops:
  7.2 269.4 %all-gather.3.cloned.1.call-start = ((), (), s32[]{:S(2)}) async-start(), calls=%async_computation.4 | async-start | bytes 6553600 | tf_op jit(solution)/shard_map/all_gather | solution.py:544
  176.9 16.0 %copy-start.9 = (bf16[256,1664]{1,0:T(8,128)(2,1)}, bf16[256,1664]{1,0:T(8,128)(2,1)S(1)}, u32[]{:S(2)}) copy-start(bf16[256,1664]{1,0:T(8,128)(2,1)S(1)} %get-tuple-element.41) | copy-start | bytes 2555908
  178.2 153.1 %all-gather.5.cloned.1.call-start = ((), (), s32[]{:S(2)}) async-start(), calls=%async_computation.5 | async-start | bytes 3276800 | tf_op jit(solution)/shard_map/all_gather | solution.py:544
  191.1 26.7 %copy-start.30 = (bf16[2,256,4,64]{1,0,3,2:T(2,128)(2,1)}, bf16[2,256,4,64]{1,0,3,2:T(2,128)(2,1)S(1)}, u32[]{:S(2)}) copy-start(bf16[2,256,4,64]{1,0,3,2:T(2,128)(2,1)S(1)} %reshape_squeeze.16) | copy-start | bytes 786436
  192.9 24.0 %copy-start.57 = (bf16[2,256,4,64]{1,0,3,2:T(2,128)(2,1)}, bf16[2,256,4,64]{1,0,3,2:T(2,128)(2,1)S(1)}, u32[]{:S(2)}) copy-start(bf16[2,256,4,64]{1,0,3,2:T(2,128)(2,1)S(1)} %reshape_squeeze.17) | copy-start | bytes 786436
  215.7 46.1 %copy-start.32 = (bf16[2,256,4,64]{1,0,3,2:T(2,128)(2,1)}, bf16[2,256,4,64]{1,0,3,2:T(2,128)(2,1)S(1)}, u32[]{:S(2)}) copy-start(bf16[2,256,4,64]{1,0,3,2:T(2,128)(2,1)S(1)} %reshape_squeeze.15) | copy-start | bytes 786436
  220.9 33.5 %copy-start.52 = (bf16[4,2,256,256]{3,2,1,0:T(8,128)(2,1)S(1)}, bf16[4,2,256,256]{3,2,1,0:T(8,128)(2,1)}, u32[]{:S(2)}) copy-start(bf16[4,2,256,256]{3,2,1,0:T(8,128)(2,1)} %get-tuple-element.49) | copy-start | bytes 3145732
  276.6 111.2 %reduce-scatter.5.cloned.1.call-start = ((), (), s32[]{:S(2)}) async-start(), calls=%async_computation.6 | async-start | bytes 3276800 | tf_op jit(solution)/shard_map/reduce_scatter | solution.py:548
  317.5 6.5 copy-start.24
  331.4 148.8 %reduce-scatter.7.cloned.1.call-start = ((), (), s32[]{:S(2)}) async-start(), calls=%async_computation.7 | async-start | bytes 6553600 | tf_op jit(solution)/shard_map/reduce_scatter | solution.py:548
  336.8 6.8 %copy-start.41 = (bf16[512,8,256]{0,2,1:T(8,128)(2,1)S(1)}, bf16[512,8,256]{0,2,1:T(8,128)(2,1)}, u32[]{:S(2)}) copy-start(bf16[512,8,256]{0,2,1:T(8,128)(2,1)} %copy.350) | copy-start | bytes 6291460
  336.8 12.8 %slice-start = ((s8[5242880]{0:T(1024)(128)(4,1)}), s8[4194304]{0:T(1024)(128)(4,1)S(1)}, s32[]{:S(2)}) async-start(s8[5242880]{0:T(1024)(128)(4,1)} %bitcast.403), calls=%async_computation.10 | async-start | bytes 8388608
  387.8 203.5 %reduce-scatter.9.cloned.1.call-start = ((), (), s32[]{:S(2)}) async-start(), calls=%async_computation.8 | async-start | bytes 6553600 | tf_op jit(solution)/shard_map/reduce_scatter | solution.py:548
  405.2 7.0 %copy-start.44 = (bf16[1,512,256]{2,1,0:T(8,128)(2,1)S(1)}, bf16[1,512,256]{2,1,0:T(8,128)(2,1)}, u32[]{:S(2)}) copy-start(bf16[1,512,256]{2,1,0:T(8,128)(2,1)} %reshape.427) | copy-start | bytes 786436
  480.2 177.6 %reduce-scatter.11.cloned.1.call-start = ((), (), s32[]{:S(2)}) async-start(), calls=%async_computation.9 | async-start | bytes 3932160 | tf_op jit(solution)/shard_map/reduce_scatter | solution.py:548
  486.3 17.3 %copy-start.70 = (bf16[4,2,768,256]{3,2,1,0:T(8,128)(2,1)S(1)}, bf16[4,2,768,256]{3,2,1,0:T(8,128)(2,1)}, u32[]{:S(2)}) copy-start(bf16[4,2,768,256]{3,2,1,0:T(8,128)(2,1)} %get-tuple-element.45) | copy-start | bytes 9437188
  486.4 17.1 %copy-start.43 = (bf16[3,512,256]{2,1,0:T(8,128)(2,1)S(1)}, bf16[3,512,256]{2,1,0:T(8,128)(2,1)}, u32[]{:S(2)}) copy-start(bf16[3,512,256]{2,1,0:T(8,128)(2,1)} %copy-done.42) | copy-start | bytes 2359300
  505.4 35.1 %copy-start.47 = (bf16[1,256,2048]{1,2,0:T(8,128)(2,1)S(1)}, bf16[1,256,2048]{1,2,0:T(8,128)(2,1)}, u32[]{:S(2)}) copy-start(bf16[1,256,2048]{1,2,0:T(8,128)(2,1)} %copy.403) | copy-start | bytes 3145732
  505.4 35.1 %copy-start.49 = (bf16[256,2048]{0,1:T(8,128)(2,1)S(1)}, bf16[256,2048]{0,1:T(8,128)(2,1)}, u32[]{:S(2)}) copy-start(bf16[256,2048]{0,1:T(8,128)(2,1)} %copy.404) | copy-start | bytes 3145732
  591.4 5.0 collective-permute-start
  597.6 10.7 %collective-permute-start.4 = (bf16[640,256]{1,0:T(8,128)(2,1)S(1)}, bf16[640,256]{1,0:T(8,128)(2,1)S(1)}, u32[]{:S(2)}, u32[]{:S(2)}) collective-permute-start(bf16[640,256]{1,0:T(8,128)(2,1)S(1)} %get-tuple-element.82), channel_id=1, source_target_pairs={{0,4},{4,0},{1,5},{5,1},{2,6},{6,2},{3,7},{7,3},{8,12},{12,8},{9,1... | collective-permute-start | bytes 983048 | tf_op jit(solution)/shard_map/ppermute | solution.py:553
  600.6 21.9 %collective-permute-start.3 = (bf16[512,640]{1,0:T(8,128)(2,1)S(1)}, bf16[512,640]{1,0:T(8,128)(2,1)}, u32[]{:S(2)}, u32[]{:S(2)}) collective-permute-start(bf16[512,640]{1,0:T(8,128)(2,1)S(1)} %get-tuple-element.68), channel_id=1, source_target_pairs={{0,4},{4,0},{1,5},{5,1},{2,6},{6,2},{3,7},{7,3},{8,12},{12,8},{9,1... | collective-permute-start | bytes 1966088 | tf_op jit(solution)/shard_map/ppermute | solution.py:553
  609.5 24.9 %collective-permute-start.2 = (bf16[1280,256]{1,0:T(8,128)(2,1)S(1)}, bf16[1280,256]{1,0:T(8,128)(2,1)S(1)}, u32[]{:S(2)}, u32[]{:S(2)}) collective-permute-start(bf16[1280,256]{1,0:T(8,128)(2,1)S(1)} %dynamic-slice_bitcast_fusion.1), channel_id=1, source_target_pairs={{0,4},{4,0},{1,5},{5,1},{2,6},{6,2},{3,7},{7,3},{8,12},{12,8},{9,1... | collective-permute-start | bytes 1966088 | tf_op jit(solution)/shard_map/ppermute | solution.py:553
  659.0 10.8 %collective-permute-start.1 = (bf16[768,256]{1,0:T(8,128)(2,1)S(1)}, bf16[768,256]{1,0:T(8,128)(2,1)S(1)}, u32[]{:S(2)}, u32[]{:S(2)}) collective-permute-start(bf16[768,256]{1,0:T(8,128)(2,1)S(1)} %get-tuple-element.75), channel_id=1, source_target_pairs={{0,4},{4,0},{1,5},{5,1},{2,6},{6,2},{3,7},{7,3},{8,12},{12,8},{9,1... | collective-permute-start | bytes 1179656 | tf_op jit(solution)/shard_map/ppermute | solution.py:553
  (60 other events, 130.0 us)
Sparse Core Ops, SparseCore 0:
  178.3 98.1 all-gather.2
  278.1 53.1 all-gather.4
  333.6 50.8 reduce-scatter.4
  388.0 92.1 reduce-scatter.6
  482.3 109.0 reduce-scatter.8
  593.5 64.2 reduce-scatter.10

commit v6 on v5

--- a/solution.py
+++ b/solution.py
@@ -291,7 +291,21 @@
     across.wait_send()
 
 
-def weights_kernel(count, groups, others, *refs):
+def half_of(ref, axis, side):
+    if axis is None:
+        return ref
+    size = ref.shape[axis] // 2
+    places = [slice(None)] * len(ref.shape)
+    places[axis] = pl.ds(pl.multiple_of(side * size, size), size)
+    return ref.at[tuple(places)]
+
+
+def half_shape(shape, axis):
+    return tuple(n // 2 if k == axis else n for k, n in enumerate(shape))
+
+
+def weights_kernel(count, groups, axes, *refs):
+    others = len(axes)
     keeps, gives, sources = refs[:groups], refs[groups : 2 * groups], refs[2 * groups :][:others]
     outs, received = refs[2 * groups + others :][:groups], refs[3 * groups + others :][:others]
     swap_sems, line_sems = refs[3 * groups + 2 * others :]
@@ -312,7 +326,9 @@
         outs[i][here, plane.x] = keeps[i][...]
         lines[i][0].start(0)
     swaps += [
-        plane.send(sources[i], received[i], swap_sems, groups + i, (1, 0, 0))
+        plane.send(
+            half_of(sources[i], axes[i], 1 - plane.x), received[i], swap_sems, groups + i, (1, 0, 0)
+        )
         for i in range(others)
     ]
     for i in range(groups):
@@ -411,14 +427,17 @@
     )
 
 
-def weights_step(keeps, gives, sources, planes):
+def weights_step(keeps, gives, sources, axes, planes):
     anywhere = pl.BlockSpec(memory_space=pl.ANY)
     whole = pl.BlockSpec(memory_space=pltpu.VMEM)
     outs = [full((planes, 2) + keep.shape, keep.dtype) for keep in keeps]
-    outs += [full(source.shape, source.dtype) for source in sources]
+    outs += [
+        full(half_shape(source.shape, axis), source.dtype)
+        for source, axis in zip(sources, axes)
+    ]
     groups, others = len(keeps), len(sources)
     results = pl.pallas_call(
-        functools.partial(weights_kernel, planes, groups, others),
+        functools.partial(weights_kernel, planes, groups, axes),
         name="weights_step",
         out_shape=outs,
         in_specs=[whole] * (2 * groups) + [anywhere] * others,
@@ -604,17 +623,17 @@
         cut_out(self_out, x, heads),
         cut_out(cross_out, x, heads),
     ]
-    third, fourth = cut_in(ffn_in, x), cut_out(ffn_out, x, depth)
     facts = jnp.concatenate([patch_keep, lengths[:, None]], axis=1)
     facts = jnp.pad(facts, ((0, 7), (0, 127)))
-    sources = (third[1], tokens[0], patches[0], fourth[1], cotangent[0], facts)
+    sources = (ffn_in, tokens[0], patches[0], ffn_out, cotangent[0], facts)
     weights, received = weights_step(
-        [pair[0] for pair in early], [pair[1] for pair in early], sources, blocks // 2
+        [pair[0] for pair in early], [pair[1] for pair in early],
+        sources, (2, None, None, 0, None, None), blocks // 2,
     )
     third_other, token_other, patch_other, fourth_other, grad_other, facts_other = received
     patch_w, qkv_w, gains, cross_kv_w, cross_q_w, self_out_w, cross_out_w = weights
-    third = either(third[0], third_other, x, jnp.stack)
-    fourth = either(fourth[0], fourth_other, x, jnp.stack)
+    third = either(cut_in(ffn_in, x)[0], third_other.reshape(-1, units), x, jnp.stack)
+    fourth = either(cut_out(ffn_out, x, depth)[0], fourth_other, x, jnp.stack)
     token_all = either(tokens[0], token_other, x, jnp.concatenate)
     patch_all = either(patches[0], patch_other, x, jnp.concatenate)
     grad_all = either(cotangent[0], grad_other, x, jnp.concatenate)
@@ -724,6 +743,7 @@
         dot("sbd,sf->bdf", cut(normed_cross), grad_queries),
         cross_out_part,
         dot("sk,sbd->bkd", mixed_self, cut(grad_all)),
+        dot("sbd,csf->bcdf", cut(normed_self), grad_projected[:2]),
     )
     second_share = scatter_group(after(second_part, ffn_in_share, grad_projected))
 
@@ -751,17 +771,20 @@
     grad_patch = home(pair, at_patch, (patch_depth, heads), 1, x)
     grad_gains = sum(half[at_gain[0] : at_gain[1]].astype(jnp.float32) for half in pair)
     grad_gains = unpadded(grad_gains)[0]
-    first_part = stacked(dot("sbd,csf->bcdf", cut(normed_self), grad_projected))
-    first_part = after(first_part, second_share, output)
+    first_part = stacked(dot("sbd,sf->bdf", cut(normed_self), grad_projected[2]))
+    first_part = after(first_part, second_share, output, grad_ffn_out, grad_ffn_in, grad_patch)
     first_share = scatter_group(first_part)
     pair = home_group(after(second_share, first_part), x)
-    at_kv, at_q, at_cross, at_self = places(2 * depth, depth, depth, depth)
+    at_kv, at_q, at_cross, at_self, at_pair = places(
+        2 * depth, depth, depth, depth, 2 * depth
+    )
     grad_cross_kv = home(pair, at_kv, (2, depth, heads), 2, x)
     grad_cross_q = home(pair, at_q, (depth, heads), 1, x)
     grad_cross_out = home(pair, at_cross, (heads, depth), 0, x)
     grad_self_out = home(pair, at_self, (heads, depth), 0, x)
+    grad_pair = home(pair, at_pair, (2, depth, heads), 2, x)
     pair = home_group(first_share, x)
-    grad_self_qkv = home(pair, (0, 3 * depth), (3, depth, heads), 2, x)
+    grad_self_qkv = jnp.concatenate([grad_pair, home(pair, (0, depth), (1, depth, heads), 2, x)])
     return (
         output.reshape(1, slots, width),
         grad_input.reshape(1, slots, width),

time: 685 us -> 683 us (level)
  other arithmetic: 29.7 us -> 19.7 us
    reduce_scatter x4, waiting for transfers between devices: 33.9 us -> 21.3 us  [scatter_group(): return lax.psum_scatter(parts, 'z', scatter_dimension=0, tiled=True)]
    unnamed x168 -> x231, local copies, waits for them, and re-layouts: 28 us -> 39.6 us
    ppermute x5, waiting for transfers between devices: 33.6 us -> 42.5 us  [home_group(): lax.ppermute(give, 'x', SWAP)]
    concatenate x2 -> x1, other arithmetic: 7.22 us -> 0.06 us  [stacked(): jnp.concatenate([rounded(part).reshape(blocks, -1, heads) for part in par...]
    convert_element_type x20 -> x22, local copies, waits for them, and re-layouts: 21.8 us -> 15.6 us  [rounded(): return values.astype(jnp.bfloat16)]
    dot_general x23 -> x24, matrix products: 52.9 us -> 57.6 us  [dot(): return jnp.einsum(pattern, left, right, preferred_element_type=jnp.float32)]
  transfers between devices with their start and end apart: 11 -> 11, of which waited for: 10 -> 7; matrix products, arithmetic and copies ran while one was open for 23% -> 22% of each run, Pallas kernels for 34% -> 35%
where the time goes in v6:
time: 683 us; the launch traced here: 679 us
  Pallas kernels  394 us (58%)
  local copies, waits for them, and re-layouts  93.6 us (14%)
  waiting for transfers between devices  75.1 us (11%)
  matrix products  71.7 us (10%)
  other arithmetic  19.7 us (3%)
  between operations  16.8 us (2%)
  starting transfers between devices  7.49 us (1%)
    pallas_call x8, Pallas kernels, plane_call(): pl.pallas_call(kernel, name=name, out_shape=outs, in_specs=[whole] * len(...  235 us
    pallas_call x1, Pallas kernels, weights_step(): pl.pallas_call(functools.partial(weights_kernel, planes, groups, axes), n...  160 us
    dot_general x24, matrix products, dot(): return jnp.einsum(pattern, left, right, preferred_element_type=jnp.float32)  57.6 us
    ppermute x5, waiting for transfers between devices, home_group(): lax.ppermute(give, 'x', SWAP)  42.5 us
    unnamed x231, local copies, waits for them, and re-layouts  39.6 us
    reduce_scatter x4, waiting for transfers between devices, scatter_group(): return lax.psum_scatter(parts, 'z', scatter_dimension=0, tiled=True)  21.3 us
    convert_element_type x22, local copies, waits for them, and re-layouts, rounded(): return values.astype(jnp.bfloat16)  15.6 us
  transfers between devices with their start and end apart: 11, of which 7 were waited for; matrix products, arithmetic and copies ran while one was open for 22% of the time, Pallas kernels for 35%

profile of v6, /device:TPU:0, one launch (start us, length us, event | category | flops | bytes accessed | tf_op | source)
XLA Modules:
  0.0 678.7 jit_solution(3206988348755454490)
XLA Ops:
  17.2 159.7 %weights_step.1 = (bf16[4,2,208,256]{3,2,1,0:T(8,128)(2,1)S(1)}, bf16[4,2,768,256]{3,2,1,0:T(8,128)(2,1)}, bf16[4,2,16,256]{3,2,1,0:T(8,128)(2,1)S(1)}, bf16[4,2...) custom-call(bf16[208,256]{1,0:T(8,128)(2,1)S(1)} %copy-done.16, ...), custom_call_target="tpu_custom_call" | custom-call | tf_op jit(solution)/shard_map/weights_step/pallas_call | solution.py:439
  185.2 16.2 %gather_step.1 = bf16[8,512,256]{2,1,0:T(8,128)(2,1)S(1)} custom-call(bf16[512,256]{1,0:T(8,128)(2,1)S(1)} %fusion.97.own), custom_call_target="tpu_custom_call" | custom-call | tf_op jit(solution)/shard_map/gather_step/pallas_call | solution.py:371
  203.8 3.6 fusion.80
  211.8 3.8 fusion.77
  220.8 32.7 %forward_step.2 = (f32[64,2048]{1,0:T(8,128)S(1)}, bf16[8,64,2048]{2,1,0:T(8,128)(2,1)S(1)}) custom-call(bf16[8,512,256]{2,1,0:T(8,128)(2,1)S(1)} %convert_bitcast_fusion.7.part, f32[64,2048]{1,0:T(8,128)S(1)} %bitcast_convert_fusion.6.residual.values, f32[1,2048]{1,0:T(1,128)S(1)} %bitcast.398), custom_call_target="tpu_custom_call" | custom-call | tf_op jit(solution)/shard_map/forward_step/pallas_call | solution.py:371
  267.6 11.2 %all-gather.3.cloned.1.call-done.refs_1_ = bf16[8,512,640]{2,1,0:T(8,128)(2,1)} async-done(((bf16[2,512,640]{2,1,0:T(8,128)(2,1)}), bf16[8,512,640]{2,1,0:T(8,128)(2,1)}) %all-gather.3.cloned.1.call-update) | async-done | bytes 5242896 | tf_op jit(solution)/shard_map/all_gather | solution.py:563
  283.9 32.9 %forward_step.3 = (f32[64,2048]{1,0:T(8,128)S(1)}, bf16[8,64,2048]{2,1,0:T(8,128)(2,1)S(1)}) custom-call(bf16[8,512,256]{2,1,0:T(8,128)(2,1)S(1)} %convert_bitcast_fusion.6.part, f32[64,2048]{1,0:T(8,128)S(1)} %copy-done.7, f32[1,2048]{1,0:T(1,128)S(1)} %bitcast.400), custom_call_target="tpu_custom_call" | custom-call | tf_op jit(solution)/shard_map/forward_step/pallas_call | solution.py:371
  321.1 6.3 fusion.19
  330.7 2.9 convert_bitcast_fusion.1.refs_0_
  333.8 4.4 copy.360
  339.1 6.8 %multiply_bitcast_fusion = (f32[1,512,640]{2,1,0:T(8,128)S(1)}, f32[1,512,640]{2,1,0:T(8,128)S(1)}) fusion(f32[2,512,640]{2,1,0:T(8,128)} %copy-done.35, bf16[8,640,256]{2,1,0:T(8,128)(2,1)} %after.10.refs_1_, bf16[256,8,256]{0,2,1:T(8,128)(2,1)} %bitcast.449, bf16[256,8,256]{0,2,1:T(8,128)(2,1)} %bitcast.447, pred[]{:T(512)S(6)} %eq.2), kind=kOutput, calls=%fused_computation.95 | convolution fusion | flops 1358823424 | bytes 9961473 | tf_op jit(solution)/shard_map/sbd,bfd->sf/dot_general | solution.py:522
  345.9 3.1 convert_bitcast_fusion
  351.9 3.1 fusion.36.part
  355.1 33.0 %backward_step.2 = (f32[64,2048]{1,0:T(8,128)S(1)}, f32[1,2048]{1,0:T(1,128)S(1)}, bf16[8,64,2048]{2,1,0:T(8,128)(2,1)S(1)}) custom-call(bf16[8,512,256]{2,1,0:T(8,128)(2,1)S(1)} %fusion.36.part, f32[64,2048]{1,0:T(8,128)S(1)} %get-tuple-element.53.values.residual, f32[64,2048]{1,0:T(8,128)S(1)} %bitcast_convert_fusion.5.grad, f32[1,2048]{1,0:T(1,128)S(1)} %bitcast.401), custom_call_target="tpu_custom_call" | custom-call | tf_op jit(solution)/shard_map/backward_step/pallas_call | solution.py:371
  411.7 32.7 %backward_step.3 = (f32[64,2048]{1,0:T(8,128)S(1)}, f32[1,2048]{1,0:T(1,128)S(1)}, bf16[8,64,2048]{2,1,0:T(8,128)(2,1)S(1)}) custom-call(bf16[8,512,256]{2,1,0:T(8,128)(2,1)S(1)} %convert_bitcast_fusion.4.part, f32[64,2048]{1,0:T(8,128)S(1)} %copy-done.8, f32[64,2048]{1,0:T(8,128)S(1)} %copy-done.14, f32[1,2048]{1,0:T(1,128)S(1)} %bitcast.399), custom_call_target="tpu_custom_call" | custom-call | tf_op jit(solution)/shard_map/backward_step/pallas_call | solution.py:371
  458.8 3.6 convert_bitcast_fusion.2
  476.5 6.0 reduce-scatter.7.cloned.1.call-done.refs_1_.refs_0_
  490.9 17.0 %scatter_step.1 = bf16[512,256]{1,0:T(8,128)(2,1)S(1)} custom-call(bf16[8,512,256]{2,1,0:T(8,128)(2,1)S(1)} %bitcast.389), custom_call_target="tpu_custom_call" | custom-call | tf_op jit(solution)/shard_map/scatter_step/pallas_call | solution.py:371
  509.9 35.0 %input_step.1 = (f32[4,64,2048]{2,1,0:T(8,128)S(1)}, f32[8,2048]{1,0:T(8,128)S(1)}) custom-call(bf16[8,512,256]{2,1,0:T(8,128)(2,1)S(1)} %fusion.37.part, f32[64,2048]{1,0:T(8,128)S(1)} %bitcast_convert_fusion.6.residual.values, f32[64,2048]{1,0:T(8,128)S(1)} %get-tuple-element.58.grad, f32[1,2048]{1,0:T(1,128)S(1)} %bitcast.403, f32[8,2048]{1,0:T(8,128)S(1)} %pad.27.gains_before), custom_call_target="tpu_custom_call" | custom-call | tf_op jit(solution)/shard_map/input_step/pallas_call | solution.py:371
  549.5 34.8 %output_step.1 = (bf16[4,64,2048]{2,1,0:T(8,128)(2,1)S(1)}, f32[2,224,256]{2,1,0:T(8,128)S(1)}) custom-call(bf16[8,512,256]{2,1,0:T(8,128)(2,1)S(1)} %convert_bitcast_fusion.5.part, f32[64,2048]{1,0:T(8,128)S(1)} %get-tuple-element.53.values.residual, bf16[4,2,224,256]{3,2,1,0:T(8,128)(2,1)S(1)} %bitcast.391), custom_call_target="tpu_custom_call" | custom-call | tf_op jit(solution)/shard_map/output_step/pallas_call | solution.py:371
  593.5 20.4 %collective-permute-done.1 = bf16[640,256]{1,0:T(8,128)(2,1)S(1)} collective-permute-done((bf16[640,256]{1,0:T(8,128)(2,1)S(1)}, bf16[640,256]{1,0:T(8,128)(2,1)S(1)}, u32[]{:S(2)}, u32[]{:S(2)}) %collective-permute-start.1) | collective-permute-done | bytes 327712 | tf_op jit(solution)/shard_map/ppermute | solution.py:572
  617.1 10.5 %reduce-scatter.9.cloned.1.call-done.refs_1_.refs_0_ = bf16[2,1792,256]{2,1,0:T(8,128)(2,1)} async-done(((bf16[8,1792,256]{2,1,0:T(8,128)(2,1)}), bf16[2,1792,256]{2,1,0:T(8,128)(2,1)}) %reduce-scatter.9.cloned.1.call-update) | async-done | bytes 1835024 | tf_op jit(solution)/shard_map/reduce_scatter | solution.py:567
  632.3 20.1 %collective-permute-done.3 = bf16[1792,256]{1,0:T(8,128)(2,1)} collective-permute-done((bf16[1792,256]{1,0:T(8,128)(2,1)}, bf16[1792,256]{1,0:T(8,128)(2,1)}, u32[]{:S(2)}, u32[]{:S(2)}) %collective-permute-start.3) | collective-permute-done | bytes 917536 | tf_op jit(solution)/shard_map/ppermute | solution.py:572
  656.9 4.8 reduce-scatter.11.cloned.1.call-done
  (408 shorter events, 157.0 us)
Async XLA Ops:
  7.2 271.6 %all-gather.3.cloned.1.call-start = ((), (), s32[]{:S(2)}) async-start(), calls=%async_computation.4 | async-start | bytes 6553600 | tf_op jit(solution)/shard_map/all_gather | solution.py:563
  180.5 153.2 %all-gather.5.cloned.1.call-start = ((), (), s32[]{:S(2)}) async-start(), calls=%async_computation.5 | async-start | bytes 3276800 | tf_op jit(solution)/shard_map/all_gather | solution.py:563
  220.8 33.5 %copy-start.63 = (bf16[4,2,256,256]{3,2,1,0:T(8,128)(2,1)S(1)}, bf16[4,2,256,256]{3,2,1,0:T(8,128)(2,1)}, u32[]{:S(2)}) copy-start(bf16[4,2,256,256]{3,2,1,0:T(8,128)(2,1)} %get-tuple-element.49) | copy-start | bytes 3145732
  278.9 111.3 %reduce-scatter.5.cloned.1.call-start = ((), (), s32[]{:S(2)}) async-start(), calls=%async_computation.6 | async-start | bytes 3276800 | tf_op jit(solution)/shard_map/reduce_scatter | solution.py:567
  333.7 148.8 %reduce-scatter.7.cloned.1.call-start = ((), (), s32[]{:S(2)}) async-start(), calls=%async_computation.7 | async-start | bytes 6553600 | tf_op jit(solution)/shard_map/reduce_scatter | solution.py:567
  339.1 6.8 %copy-start.50 = (bf16[512,8,256]{0,2,1:T(8,128)(2,1)S(1)}, bf16[512,8,256]{0,2,1:T(8,128)(2,1)}, u32[]{:S(2)}) copy-start(bf16[512,8,256]{0,2,1:T(8,128)(2,1)} %copy.360) | copy-start | bytes 6291460
  339.1 12.8 %slice-start = ((s8[5242880]{0:T(1024)(128)(4,1)}), s8[4194304]{0:T(1024)(128)(4,1)S(1)}, s32[]{:S(2)}) async-start(s8[5242880]{0:T(1024)(128)(4,1)} %bitcast.416), calls=%async_computation.10 | async-start | bytes 8388608
  345.9 6.0 slice-start.1
  390.2 237.4 %reduce-scatter.9.cloned.1.call-start = ((), (), s32[]{:S(2)}) async-start(), calls=%async_computation.8 | async-start | bytes 9175040 | tf_op jit(solution)/shard_map/reduce_scatter | solution.py:567
  482.5 179.1 %reduce-scatter.11.cloned.1.call-start = ((), (), s32[]{:S(2)}) async-start(), calls=%async_computation.9 | async-start | bytes 1310720 | tf_op jit(solution)/shard_map/reduce_scatter | solution.py:567
  490.7 17.3 %copy-start.101 = (bf16[4,2,768,256]{3,2,1,0:T(8,128)(2,1)S(1)}, bf16[4,2,768,256]{3,2,1,0:T(8,128)(2,1)}, u32[]{:S(2)}) copy-start(bf16[4,2,768,256]{3,2,1,0:T(8,128)(2,1)} %get-tuple-element.45) | copy-start | bytes 9437188
  490.9 17.2 %copy-start.52 = (bf16[3,512,256]{2,1,0:T(8,128)(2,1)S(1)}, bf16[3,512,256]{2,1,0:T(8,128)(2,1)}, u32[]{:S(2)}) copy-start(bf16[3,512,256]{2,1,0:T(8,128)(2,1)} %copy-done.51) | copy-start | bytes 2359300
  509.9 35.1 %copy-start.76 = (bf16[256,1664]{0,1:T(8,128)(2,1)S(1)}, bf16[256,1664]{0,1:T(8,128)(2,1)}, u32[]{:S(2)}) copy-start(bf16[256,1664]{0,1:T(8,128)(2,1)} %copy.310) | copy-start | bytes 2555908
  509.9 35.1 %copy-start.77 = (bf16[1,256,1664]{1,2,0:T(8,128)(2,1)S(1)}, bf16[1,256,1664]{1,2,0:T(8,128)(2,1)}, u32[]{:S(2)}) copy-start(bf16[1,256,1664]{1,2,0:T(8,128)(2,1)} %copy.309) | copy-start | bytes 2555908
  549.4 37.3 %copy-start.68 = (bf16[2,256,4,64]{1,0,3,2:T(2,128)(2,1)S(1)}, bf16[2,256,4,64]{1,0,3,2:T(2,128)(2,1)}, u32[]{:S(2)}) copy-start(bf16[2,256,4,64]{1,0,3,2:T(2,128)(2,1)} %copy.347) | copy-start | bytes 786436
  549.4 37.5 %copy-start.58 = (bf16[1,256,2048]{1,2,0:T(8,128)(2,1)S(1)}, bf16[1,256,2048]{1,2,0:T(8,128)(2,1)}, u32[]{:S(2)}) copy-start(bf16[1,256,2048]{1,2,0:T(8,128)(2,1)} %copy.415) | copy-start | bytes 3145732
  549.5 37.5 %copy-start.60 = (bf16[256,2048]{0,1:T(8,128)(2,1)S(1)}, bf16[256,2048]{0,1:T(8,128)(2,1)}, u32[]{:S(2)}) copy-start(bf16[256,2048]{0,1:T(8,128)(2,1)} %copy.416) | copy-start | bytes 3145732
  549.5 37.5 %copy-start.95 = (f32[8,256]{1,0:T(8,128)S(1)}, f32[8,256]{1,0:T(8,128)}, u32[]{:S(2)}) copy-start(f32[8,256]{1,0:T(8,128)} %copy-done.93) | copy-start | bytes 24580
  549.5 37.5 %copy-start.99 = (f32[512]{0:T(512)S(1)}, f32[512]{0:T(512)}, u32[]{:S(2)}) copy-start(f32[512]{0:T(512)} %copy-done.97) | copy-start | bytes 6148
  585.3 7.4 %collective-permute-start = (bf16[224,256]{1,0:T(8,128)(2,1)S(1)}, bf16[224,256]{1,0:T(8,128)(2,1)S(1)}, u32[]{:S(2)}, u32[]{:S(2)}) collective-permute-start(bf16[224,256]{1,0:T(8,128)(2,1)S(1)} %fusion.137), channel_id=1, source_target_pairs={{0,4},{4,0},{1,5},{5,1},{2,6},{6,2},{3,7},{7,3},{8,12},{12,8},{9,1... | collective-permute-start | bytes 344072 | tf_op jit(solution)/shard_map/ppermute | solution.py:572
  590.5 24.8 %collective-permute-start.2 = (bf16[512,640]{1,0:T(8,128)(2,1)S(1)}, bf16[512,640]{1,0:T(8,128)(2,1)S(1)}, u32[]{:S(2)}, u32[]{:S(2)}) collective-permute-start(bf16[512,640]{1,0:T(8,128)(2,1)S(1)} %get-tuple-element.73), channel_id=1, source_target_pairs={{0,4},{4,0},{1,5},{5,1},{2,6},{6,2},{3,7},{7,3},{8,12},{12,8},{9,1... | collective-permute-start | bytes 1966088 | tf_op jit(solution)/shard_map/ppermute | solution.py:572
  591.3 22.6 %collective-permute-start.1 = (bf16[640,256]{1,0:T(8,128)(2,1)S(1)}, bf16[640,256]{1,0:T(8,128)(2,1)S(1)}, u32[]{:S(2)}, u32[]{:S(2)}) collective-permute-start(bf16[640,256]{1,0:T(8,128)(2,1)S(1)} %get-tuple-element.85), channel_id=1, source_target_pairs={{0,4},{4,0},{1,5},{5,1},{2,6},{6,2},{3,7},{7,3},{8,12},{12,8},{9,1... | collective-permute-start | bytes 983048 | tf_op jit(solution)/shard_map/ppermute | solution.py:572
  630.0 22.4 %collective-permute-start.3 = (bf16[1792,256]{1,0:T(8,128)(2,1)}, bf16[1792,256]{1,0:T(8,128)(2,1)}, u32[]{:S(2)}, u32[]{:S(2)}) collective-permute-start(bf16[1792,256]{1,0:T(8,128)(2,1)} %dynamic-slice_bitcast_fusion), channel_id=1, source_target_pairs={{0,4},{4,0},{1,5},{5,1},{2,6},{6,2},{3,7},{7,3},{8,12},{12,8},{9,1... | collective-permute-start | bytes 2752520 | tf_op jit(solution)/shard_map/ppermute | solution.py:572
  662.6 5.1 collective-permute-start.4
  (91 other events, 188.9 us)
Sparse Core Ops, SparseCore 0:
  180.6 98.1 all-gather.2
  280.4 53.1 all-gather.4
  335.9 50.8 reduce-scatter.4
  390.4 92.0 reduce-scatter.6
  484.6 143.0 reduce-scatter.8
  630.4 31.1 reduce-scatter.10
